TPU v7x, 256 devices: a whole 4x4x8 slice. The times are simulated.
256 devices in a mesh: grp: 16 (over z_hi, y), dev: 16 (over x, z_lo, core).
Axes of the slice: x: 4, y: 4, z: 8 (z_hi: 4, z_lo: 2; z = z_hi * 2 + z_lo), core: 2. Of those that a mesh axis runs over, the one named last changes fastest.
Arguments:
- features: bfloat16 [8192, 32, 768], P(('grp', 'dev'))
- teacher: bfloat16 [8192, 1024], P(('grp', 'dev'))
- gain: float32 [768], replicated, may hold values from 0.25 to 1.75
- w_head: bfloat16 [768, 1024], replicated
- positives: int32 [8192], P(('grp', 'dev')), may hold values from 0 to 8191, as said below
Outputs:
- loss: float32 [], replicated
- grad_features: bfloat16 [8192, 32, 768], P(('grp', 'dev'))
- grad_head: float32 [768, 1024], P('grp', 'dev')
- grad_gain: float32 [768], replicated
Inputs may be any that keep to these rules, and one draw needn't show every extreme that they name: `positives`: every teacher row is the positive of exactly one variant.
All inputs are finite; a program needn't handle non-finite values.
Results may differ from a plain program's by a relative error of at most 0.0061.
Values may be sent and summed in bfloat16 or wider, within the bound.
No kernel may reach another device: no remote copies, remote signals or barrier semaphores. Data moves between devices by JAX's collectives and lax.ppermute only.
A program may use at most 64 MiB of HBM per device.

v0:
```python
import jax
import jax.numpy as jnp
from jax import lax
from jax.sharding import PartitionSpec as P

logit_scale = 64.0
norm_eps = 1e-06


def passed_along(array, axis, by):
    devices = lax.axis_size(axis)
    return lax.ppermute(array, axis, [(i, (i + by) % devices) for i in range(devices)])


def rms_scale(pooled, gain):
    radius = jnp.sqrt(jnp.mean(pooled * pooled, axis=-1, keepdims=True) + norm_eps)
    return pooled / radius * gain


def unit_rows(raw):
    length = jnp.sqrt(jnp.sum(raw * raw, axis=-1, keepdims=True) + norm_eps)
    return (raw / length, length)


def body(features, teacher, gain, w_head, positives):
    local_rows = teacher.shape[0]
    width = teacher.shape[1]
    groups = lax.axis_size("grp")
    members = lax.axis_size("dev")
    group_rows = local_rows * members
    total = group_rows * groups
    pooled = jnp.mean(features, axis=1, dtype=jnp.float32)
    normed = rms_scale(pooled, gain).astype(jnp.bfloat16)
    raw = jnp.dot(normed, w_head, preferred_element_type=jnp.float32)
    unit, length = unit_rows(raw)
    student = unit.astype(jnp.bfloat16)
    teacher_unit = unit_rows(teacher.astype(jnp.float32))[0].astype(jnp.bfloat16)
    group_index = lax.axis_index("grp")
    first_block = lax.all_gather(teacher_unit, "dev", axis=0, tiled=True)

    def place(step, block, scores, store):
        anchor = (group_index - step) % groups
        start = anchor * group_rows
        piece = logit_scale * jnp.dot(student, block.T, preferred_element_type=jnp.float32)
        zero = jnp.zeros((), jnp.int32)
        scores = lax.dynamic_update_slice(scores, piece, (zero, start))
        store = lax.dynamic_update_slice(store, block, (start, zero))
        return (scores, store)

    scores, store = place(
        jnp.zeros((), jnp.int32),
        first_block,
        jnp.zeros((local_rows, total), jnp.float32),
        jnp.zeros((total, width), jnp.bfloat16),
    )

    def advance(step, carry):
        block, scores, store = carry
        block = passed_along(block, "grp", 1)
        scores, store = place(step.astype(jnp.int32), block, scores, store)
        return (block, scores, store)

    _, scores, store = lax.fori_loop(1, groups, advance, (first_block, scores, store))
    expo = jnp.exp(scores)
    column_ids = jnp.arange(total, dtype=jnp.int32)
    mask = (column_ids[None, :] == positives[:, None]).astype(jnp.float32)
    row_totals = jnp.sum(expo, axis=1)
    col_totals = lax.psum(jnp.sum(expo, axis=0), ("grp", "dev"))
    loss_part = jnp.sum(jnp.log(row_totals)) - 2.0 * jnp.sum(scores * mask)
    extra = jnp.sum(jnp.log(col_totals))
    weights = (expo / row_totals[:, None] + expo / col_totals[None, :] - 2.0 * mask).astype(
        jnp.bfloat16
    )
    grad_unit = logit_scale * jnp.dot(weights, store, preferred_element_type=jnp.float32)
    along = jnp.sum(unit * grad_unit, axis=-1, keepdims=True)
    grad_raw = ((grad_unit - unit * along) / length).astype(jnp.bfloat16)
    grad_normed = jnp.dot(grad_raw, w_head.T, preferred_element_type=jnp.float32)
    radius = jnp.sqrt(jnp.mean(pooled * pooled, axis=-1, keepdims=True) + norm_eps)
    gain_local = jnp.sum(grad_normed * pooled / radius, axis=0)
    summed, grad_gain = lax.psum((loss_part, gain_local), ("grp", "dev"))
    loss = (summed + extra) / (2.0 * total)
    head_term = jnp.dot(normed.T, grad_raw, preferred_element_type=jnp.float32)
    head_share = lax.psum_scatter(head_term, "grp", scatter_dimension=0, tiled=True)
    grad_head = lax.psum_scatter(head_share, "dev", scatter_dimension=1, tiled=True)
    _, pullback = jax.vjp(lambda value: rms_scale(value, gain), pooled)
    grad_pooled = pullback(grad_normed)[0]
    window = features.shape[1]
    grad_features = jnp.broadcast_to((grad_pooled / window)[:, None, :], features.shape).astype(
        jnp.bfloat16
    )
    return (loss, grad_features, grad_head, grad_gain)


def solution(mesh):
    in_specs = (P(("grp", "dev"), None, None), P(("grp", "dev"), None), P(), P(), P(("grp", "dev")))
    out_specs = (P(), P(("grp", "dev"), None, None), P("grp", "dev"), P())
    return jax.shard_map(body, mesh=mesh, in_specs=in_specs, out_specs=out_specs, check_vma=False)
```

profile of v0, /device:TPU:1, one launch (start us, length us, event | category | flops | bytes accessed | tf_op | source)
XLA Modules:
  0.0 1083.0 jit_solution(3485637778743189738)
XLA Ops:
  7.2 1.1 fusion.7
  8.3 1.6 fusion.8
  10.0 1.8 convert_reduce_fusion
  11.9 1.2 multiply_reduce_fusion.1
  13.2 36.4 %all-gather.2.cloned.1.call-done = bf16[512,1024]{1,0:T(8,128)(2,1)} async-done(((bf16[32,1024]{1,0:T(8,128)(2,1)}), bf16[512,1024]{1,0:T(8,128)(2,1)}) %all-gather.2.cloned.1.call-update) | async-done | bytes 1048592 | tf_op jit(solution)/shard_map/all_gather | solution.py:39
  49.7 2.1 broadcast_in_dim.9
  52.5 5.2 copy-done.1
  58.6 747.0 %while.19 = (s32[]{:T(128)}, bf16[512,1024]{1,0:T(8,128)(2,1)}, f32[32,8192]{1,0:T(8,128)}, bf16[8192,1024]{1,0:T(8,128)(2,1)}, bf16[32,1024]{1,0:T(8,128)(2,1)S...) while((s32[]{:T(128)}, bf16[512,1024]{1,0:T(8,128)(2,1)}, ...), condition=%wide.region_5.6_spmd, body=%wide.region_4.5_spmd.sunk | while | flops 33570832 | bytes 9568588 | solution.py:63
  58.6 1.2 collective-permute-start
  59.9 40.7 %collective-permute-done = bf16[512,1024]{1,0:T(8,128)(2,1)S(1)} collective-permute-done((bf16[512,1024]{1,0:T(8,128)(2,1)}, bf16[512,1024]{1,0:T(8,128)(2,1)S(1)}, u32[]{:S(2)}, u32[]{:S(2)}) %collective-permute-start) | collective-permute-done | bytes 1048608 | tf_op jit(solution)/shard_map/while/body/eval_jaxpr/ppermute | solution.py:12
  101.6 1.1 constant_dynamic-update-slice_fusion.3
  102.7 1.1 fusion.31
  103.7 34.7 %collective-permute-done = bf16[512,1024]{1,0:T(8,128)(2,1)S(1)} collective-permute-done((bf16[512,1024]{1,0:T(8,128)(2,1)}, bf16[512,1024]{1,0:T(8,128)(2,1)S(1)}, u32[]{:S(2)}, u32[]{:S(2)}) %collective-permute-start) | collective-permute-done | bytes 1048608 | tf_op jit(solution)/shard_map/while/body/eval_jaxpr/ppermute | solution.py:12
  139.4 1.0 constant_dynamic-update-slice_fusion.3
  140.5 1.1 fusion.31
  141.5 62.4 %collective-permute-done = bf16[512,1024]{1,0:T(8,128)(2,1)S(1)} collective-permute-done((bf16[512,1024]{1,0:T(8,128)(2,1)}, bf16[512,1024]{1,0:T(8,128)(2,1)S(1)}, u32[]{:S(2)}, u32[]{:S(2)}) %collective-permute-start) | collective-permute-done | bytes 1048608 | tf_op jit(solution)/shard_map/while/body/eval_jaxpr/ppermute | solution.py:12
  205.0 1.0 constant_dynamic-update-slice_fusion.3
  206.0 1.1 fusion.31
  207.1 70.9 %collective-permute-done = bf16[512,1024]{1,0:T(8,128)(2,1)S(1)} collective-permute-done((bf16[512,1024]{1,0:T(8,128)(2,1)}, bf16[512,1024]{1,0:T(8,128)(2,1)S(1)}, u32[]{:S(2)}, u32[]{:S(2)}) %collective-permute-start) | collective-permute-done | bytes 1048608 | tf_op jit(solution)/shard_map/while/body/eval_jaxpr/ppermute | solution.py:12
  279.0 1.1 constant_dynamic-update-slice_fusion.3
  280.1 1.1 fusion.31
  281.2 62.0 %collective-permute-done = bf16[512,1024]{1,0:T(8,128)(2,1)S(1)} collective-permute-done((bf16[512,1024]{1,0:T(8,128)(2,1)}, bf16[512,1024]{1,0:T(8,128)(2,1)S(1)}, u32[]{:S(2)}, u32[]{:S(2)}) %collective-permute-start) | collective-permute-done | bytes 1048608 | tf_op jit(solution)/shard_map/while/body/eval_jaxpr/ppermute | solution.py:12
  344.2 1.0 constant_dynamic-update-slice_fusion.3
  345.2 1.1 fusion.31
  346.3 67.8 %collective-permute-done = bf16[512,1024]{1,0:T(8,128)(2,1)S(1)} collective-permute-done((bf16[512,1024]{1,0:T(8,128)(2,1)}, bf16[512,1024]{1,0:T(8,128)(2,1)S(1)}, u32[]{:S(2)}, u32[]{:S(2)}) %collective-permute-start) | collective-permute-done | bytes 1048608 | tf_op jit(solution)/shard_map/while/body/eval_jaxpr/ppermute | solution.py:12
  415.1 1.0 constant_dynamic-update-slice_fusion.3
  416.1 1.1 fusion.31
  417.2 46.9 %collective-permute-done = bf16[512,1024]{1,0:T(8,128)(2,1)S(1)} collective-permute-done((bf16[512,1024]{1,0:T(8,128)(2,1)}, bf16[512,1024]{1,0:T(8,128)(2,1)S(1)}, u32[]{:S(2)}, u32[]{:S(2)}) %collective-permute-start) | collective-permute-done | bytes 1048608 | tf_op jit(solution)/shard_map/while/body/eval_jaxpr/ppermute | solution.py:12
  465.1 1.0 constant_dynamic-update-slice_fusion.3
  466.2 1.1 fusion.31
  467.2 47.7 %collective-permute-done = bf16[512,1024]{1,0:T(8,128)(2,1)S(1)} collective-permute-done((bf16[512,1024]{1,0:T(8,128)(2,1)}, bf16[512,1024]{1,0:T(8,128)(2,1)S(1)}, u32[]{:S(2)}, u32[]{:S(2)}) %collective-permute-start) | collective-permute-done | bytes 1048608 | tf_op jit(solution)/shard_map/while/body/eval_jaxpr/ppermute | solution.py:12
  515.9 1.1 constant_dynamic-update-slice_fusion.3
  517.1 1.1 fusion.31
  518.1 51.8 %collective-permute-done = bf16[512,1024]{1,0:T(8,128)(2,1)S(1)} collective-permute-done((bf16[512,1024]{1,0:T(8,128)(2,1)}, bf16[512,1024]{1,0:T(8,128)(2,1)S(1)}, u32[]{:S(2)}, u32[]{:S(2)}) %collective-permute-start) | collective-permute-done | bytes 1048608 | tf_op jit(solution)/shard_map/while/body/eval_jaxpr/ppermute | solution.py:12
  570.9 1.0 constant_dynamic-update-slice_fusion.3
  572.0 1.1 fusion.31
  573.0 48.1 %collective-permute-done = bf16[512,1024]{1,0:T(8,128)(2,1)S(1)} collective-permute-done((bf16[512,1024]{1,0:T(8,128)(2,1)}, bf16[512,1024]{1,0:T(8,128)(2,1)S(1)}, u32[]{:S(2)}, u32[]{:S(2)}) %collective-permute-start) | collective-permute-done | bytes 1048608 | tf_op jit(solution)/shard_map/while/body/eval_jaxpr/ppermute | solution.py:12
  622.2 1.1 constant_dynamic-update-slice_fusion.3
  623.2 1.1 fusion.31
  624.3 46.5 %collective-permute-done = bf16[512,1024]{1,0:T(8,128)(2,1)S(1)} collective-permute-done((bf16[512,1024]{1,0:T(8,128)(2,1)}, bf16[512,1024]{1,0:T(8,128)(2,1)S(1)}, u32[]{:S(2)}, u32[]{:S(2)}) %collective-permute-start) | collective-permute-done | bytes 1048608 | tf_op jit(solution)/shard_map/while/body/eval_jaxpr/ppermute | solution.py:12
  671.8 1.1 constant_dynamic-update-slice_fusion.3
  672.9 1.1 fusion.31
  674.0 40.5 %collective-permute-done = bf16[512,1024]{1,0:T(8,128)(2,1)S(1)} collective-permute-done((bf16[512,1024]{1,0:T(8,128)(2,1)}, bf16[512,1024]{1,0:T(8,128)(2,1)S(1)}, u32[]{:S(2)}, u32[]{:S(2)}) %collective-permute-start) | collective-permute-done | bytes 1048608 | tf_op jit(solution)/shard_map/while/body/eval_jaxpr/ppermute | solution.py:12
  715.4 1.0 constant_dynamic-update-slice_fusion.3
  716.5 1.1 fusion.31
  717.5 27.2 %collective-permute-done = bf16[512,1024]{1,0:T(8,128)(2,1)S(1)} collective-permute-done((bf16[512,1024]{1,0:T(8,128)(2,1)}, bf16[512,1024]{1,0:T(8,128)(2,1)S(1)}, u32[]{:S(2)}, u32[]{:S(2)}) %collective-permute-start) | collective-permute-done | bytes 1048608 | tf_op jit(solution)/shard_map/while/body/eval_jaxpr/ppermute | solution.py:12
  745.8 1.0 constant_dynamic-update-slice_fusion.3
  746.8 1.1 fusion.31
  747.9 26.2 %collective-permute-done = bf16[512,1024]{1,0:T(8,128)(2,1)S(1)} collective-permute-done((bf16[512,1024]{1,0:T(8,128)(2,1)}, bf16[512,1024]{1,0:T(8,128)(2,1)S(1)}, u32[]{:S(2)}, u32[]{:S(2)}) %collective-permute-start) | collective-permute-done | bytes 1048608 | tf_op jit(solution)/shard_map/while/body/eval_jaxpr/ppermute | solution.py:12
  775.1 1.1 constant_dynamic-update-slice_fusion.3
  776.1 1.1 fusion.31
  777.2 25.3 %collective-permute-done = bf16[512,1024]{1,0:T(8,128)(2,1)S(1)} collective-permute-done((bf16[512,1024]{1,0:T(8,128)(2,1)}, bf16[512,1024]{1,0:T(8,128)(2,1)S(1)}, u32[]{:S(2)}, u32[]{:S(2)}) %collective-permute-start) | collective-permute-done | bytes 1048608 | tf_op jit(solution)/shard_map/while/body/eval_jaxpr/ppermute | solution.py:12
  803.5 1.1 constant_dynamic-update-slice_fusion.3
  804.6 1.1 fusion.31
  805.7 2.2 exponential_reduce_fusion
  807.9 101.6 %psum.22 = f32[8192]{0:T(1024)S(1)} all-reduce(f32[8192]{0:T(1024)S(1)} %get-tuple-element.162), channel_id=1, replica_groups=mesh['grp'=16,'dev'=16] {'grp','dev'}, use_global_device_ids=true, to_apply=%region_11.12 | all-reduce | flops 8192 | bytes 65536 | tf_op jit(solution)/shard_map/psum | solution.py:68
  909.4 9.3 multiply_reduce_fusion
  918.7 2.3 fusion.15
  923.8 77.2 %all-reduce = (f32[]{:T(128)}, f32[768]{0:T(1024)}) all-reduce(f32[]{:T(128)S(6)} %sub.19, f32[768]{0:T(1024)S(1)} %get-tuple-element.165), channel_id=1, replica_groups=mesh['grp'=16,'dev'=16] {'grp','dev'}, use_global_device_ids=true, to_apply=%region_9.10 | all-reduce | flops 769 | bytes 6152 | tf_op jit(solution)/shard_map/psum | solution.py:80
  1002.9 8.4 reduce-scatter.5.cloned.1.call-done
  1011.3 1.9 copy.9
  1013.4 59.3 %reduce-scatter.7.cloned.1.call-done = f32[64,48]{1,0:T(8,128)} async-done(((f32[1024,48]{1,0:T(8,128)}), f32[64,48]{1,0:T(8,128)}) %reduce-scatter.7.cloned.1.call-update) | async-done | bytes 12304
  1072.6 1.4 copy.10
  1074.1 1.3 broadcast_in_dim.11
  (59 shorter events, 19.0 us)
Async XLA Ops:
  7.2 4.7 copy-start
  7.2 42.5 %all-gather.2.cloned.1.call-start = ((), (), s32[]{:S(2)}) async-start(), calls=%async_computation.2 | async-start | bytes 1114112 | tf_op jit(solution)/shard_map/all_gather | solution.py:39
  9.9 1001.4 %reduce-scatter.5.cloned.1.call-start = ((), (), s32[]{:S(2)}) async-start(), calls=%async_computation.3 | async-start | bytes 3342336 | tf_op jit(solution)/shard_map/reduce_scatter | solution.py:83
  49.7 2.1 copy-start.2
  51.8 753.8 %copy-start.5 = (s32[32]{0:T(128)S(1)}, s32[32]{0:T(128)}, u32[]{:S(2)}) copy-start(s32[32]{0:T(128)} %param.11) | copy-start | bytes 388
  52.0 5.7 copy-start.1
  57.7 1.0 copy-start.3
  58.6 42.0 %collective-permute-start = (bf16[512,1024]{1,0:T(8,128)(2,1)}, bf16[512,1024]{1,0:T(8,128)(2,1)S(1)}, u32[]{:S(2)}, u32[]{:S(2)}) collective-permute-start(bf16[512,1024]{1,0:T(8,128)(2,1)} %get-tuple-element.238), channel_id=1, source_target_pairs={{0,16},{16,32},{32,48},{48,64},{64,80},{80,96},{96,112},{112,128},... | collective-permute-start | bytes 3145736 | tf_op jit(solution)/shard_map/while/body/eval_jaxpr/ppermute | solution.py:12
  103.7 34.7 %collective-permute-start = (bf16[512,1024]{1,0:T(8,128)(2,1)}, bf16[512,1024]{1,0:T(8,128)(2,1)S(1)}, u32[]{:S(2)}, u32[]{:S(2)}) collective-permute-start(bf16[512,1024]{1,0:T(8,128)(2,1)} %get-tuple-element.238), channel_id=1, source_target_pairs={{0,16},{16,32},{32,48},{48,64},{64,80},{80,96},{96,112},{112,128},... | collective-permute-start | bytes 3145736 | tf_op jit(solution)/shard_map/while/body/eval_jaxpr/ppermute | solution.py:12
  141.5 62.5 %collective-permute-start = (bf16[512,1024]{1,0:T(8,128)(2,1)}, bf16[512,1024]{1,0:T(8,128)(2,1)S(1)}, u32[]{:S(2)}, u32[]{:S(2)}) collective-permute-start(bf16[512,1024]{1,0:T(8,128)(2,1)} %get-tuple-element.238), channel_id=1, source_target_pairs={{0,16},{16,32},{32,48},{48,64},{64,80},{80,96},{96,112},{112,128},... | collective-permute-start | bytes 3145736 | tf_op jit(solution)/shard_map/while/body/eval_jaxpr/ppermute | solution.py:12
  207.1 70.9 %collective-permute-start = (bf16[512,1024]{1,0:T(8,128)(2,1)}, bf16[512,1024]{1,0:T(8,128)(2,1)S(1)}, u32[]{:S(2)}, u32[]{:S(2)}) collective-permute-start(bf16[512,1024]{1,0:T(8,128)(2,1)} %get-tuple-element.238), channel_id=1, source_target_pairs={{0,16},{16,32},{32,48},{48,64},{64,80},{80,96},{96,112},{112,128},... | collective-permute-start | bytes 3145736 | tf_op jit(solution)/shard_map/while/body/eval_jaxpr/ppermute | solution.py:12
  281.1 62.0 %collective-permute-start = (bf16[512,1024]{1,0:T(8,128)(2,1)}, bf16[512,1024]{1,0:T(8,128)(2,1)S(1)}, u32[]{:S(2)}, u32[]{:S(2)}) collective-permute-start(bf16[512,1024]{1,0:T(8,128)(2,1)} %get-tuple-element.238), channel_id=1, source_target_pairs={{0,16},{16,32},{32,48},{48,64},{64,80},{80,96},{96,112},{112,128},... | collective-permute-start | bytes 3145736 | tf_op jit(solution)/shard_map/while/body/eval_jaxpr/ppermute | solution.py:12
  346.3 67.8 %collective-permute-start = (bf16[512,1024]{1,0:T(8,128)(2,1)}, bf16[512,1024]{1,0:T(8,128)(2,1)S(1)}, u32[]{:S(2)}, u32[]{:S(2)}) collective-permute-start(bf16[512,1024]{1,0:T(8,128)(2,1)} %get-tuple-element.238), channel_id=1, source_target_pairs={{0,16},{16,32},{32,48},{48,64},{64,80},{80,96},{96,112},{112,128},... | collective-permute-start | bytes 3145736 | tf_op jit(solution)/shard_map/while/body/eval_jaxpr/ppermute | solution.py:12
  417.2 46.9 %collective-permute-start = (bf16[512,1024]{1,0:T(8,128)(2,1)}, bf16[512,1024]{1,0:T(8,128)(2,1)S(1)}, u32[]{:S(2)}, u32[]{:S(2)}) collective-permute-start(bf16[512,1024]{1,0:T(8,128)(2,1)} %get-tuple-element.238), channel_id=1, source_target_pairs={{0,16},{16,32},{32,48},{48,64},{64,80},{80,96},{96,112},{112,128},... | collective-permute-start | bytes 3145736 | tf_op jit(solution)/shard_map/while/body/eval_jaxpr/ppermute | solution.py:12
  467.2 47.7 %collective-permute-start = (bf16[512,1024]{1,0:T(8,128)(2,1)}, bf16[512,1024]{1,0:T(8,128)(2,1)S(1)}, u32[]{:S(2)}, u32[]{:S(2)}) collective-permute-start(bf16[512,1024]{1,0:T(8,128)(2,1)} %get-tuple-element.238), channel_id=1, source_target_pairs={{0,16},{16,32},{32,48},{48,64},{64,80},{80,96},{96,112},{112,128},... | collective-permute-start | bytes 3145736 | tf_op jit(solution)/shard_map/while/body/eval_jaxpr/ppermute | solution.py:12
  518.1 51.8 %collective-permute-start = (bf16[512,1024]{1,0:T(8,128)(2,1)}, bf16[512,1024]{1,0:T(8,128)(2,1)S(1)}, u32[]{:S(2)}, u32[]{:S(2)}) collective-permute-start(bf16[512,1024]{1,0:T(8,128)(2,1)} %get-tuple-element.238), channel_id=1, source_target_pairs={{0,16},{16,32},{32,48},{48,64},{64,80},{80,96},{96,112},{112,128},... | collective-permute-start | bytes 3145736 | tf_op jit(solution)/shard_map/while/body/eval_jaxpr/ppermute | solution.py:12
  573.0 48.1 %collective-permute-start = (bf16[512,1024]{1,0:T(8,128)(2,1)}, bf16[512,1024]{1,0:T(8,128)(2,1)S(1)}, u32[]{:S(2)}, u32[]{:S(2)}) collective-permute-start(bf16[512,1024]{1,0:T(8,128)(2,1)} %get-tuple-element.238), channel_id=1, source_target_pairs={{0,16},{16,32},{32,48},{48,64},{64,80},{80,96},{96,112},{112,128},... | collective-permute-start | bytes 3145736 | tf_op jit(solution)/shard_map/while/body/eval_jaxpr/ppermute | solution.py:12
  624.3 46.5 %collective-permute-start = (bf16[512,1024]{1,0:T(8,128)(2,1)}, bf16[512,1024]{1,0:T(8,128)(2,1)S(1)}, u32[]{:S(2)}, u32[]{:S(2)}) collective-permute-start(bf16[512,1024]{1,0:T(8,128)(2,1)} %get-tuple-element.238), channel_id=1, source_target_pairs={{0,16},{16,32},{32,48},{48,64},{64,80},{80,96},{96,112},{112,128},... | collective-permute-start | bytes 3145736 | tf_op jit(solution)/shard_map/while/body/eval_jaxpr/ppermute | solution.py:12
  674.0 40.5 %collective-permute-start = (bf16[512,1024]{1,0:T(8,128)(2,1)}, bf16[512,1024]{1,0:T(8,128)(2,1)S(1)}, u32[]{:S(2)}, u32[]{:S(2)}) collective-permute-start(bf16[512,1024]{1,0:T(8,128)(2,1)} %get-tuple-element.238), channel_id=1, source_target_pairs={{0,16},{16,32},{32,48},{48,64},{64,80},{80,96},{96,112},{112,128},... | collective-permute-start | bytes 3145736 | tf_op jit(solution)/shard_map/while/body/eval_jaxpr/ppermute | solution.py:12
  717.5 27.2 %collective-permute-start = (bf16[512,1024]{1,0:T(8,128)(2,1)}, bf16[512,1024]{1,0:T(8,128)(2,1)S(1)}, u32[]{:S(2)}, u32[]{:S(2)}) collective-permute-start(bf16[512,1024]{1,0:T(8,128)(2,1)} %get-tuple-element.238), channel_id=1, source_target_pairs={{0,16},{16,32},{32,48},{48,64},{64,80},{80,96},{96,112},{112,128},... | collective-permute-start | bytes 3145736 | tf_op jit(solution)/shard_map/while/body/eval_jaxpr/ppermute | solution.py:12
  747.9 26.2 %collective-permute-start = (bf16[512,1024]{1,0:T(8,128)(2,1)}, bf16[512,1024]{1,0:T(8,128)(2,1)S(1)}, u32[]{:S(2)}, u32[]{:S(2)}) collective-permute-start(bf16[512,1024]{1,0:T(8,128)(2,1)} %get-tuple-element.238), channel_id=1, source_target_pairs={{0,16},{16,32},{32,48},{48,64},{64,80},{80,96},{96,112},{112,128},... | collective-permute-start | bytes 3145736 | tf_op jit(solution)/shard_map/while/body/eval_jaxpr/ppermute | solution.py:12
  777.2 25.3 %collective-permute-start = (bf16[512,1024]{1,0:T(8,128)(2,1)}, bf16[512,1024]{1,0:T(8,128)(2,1)S(1)}, u32[]{:S(2)}, u32[]{:S(2)}) collective-permute-start(bf16[512,1024]{1,0:T(8,128)(2,1)} %get-tuple-element.238), channel_id=1, source_target_pairs={{0,16},{16,32},{32,48},{48,64},{64,80},{80,96},{96,112},{112,128},... | collective-permute-start | bytes 3145736 | tf_op jit(solution)/shard_map/while/body/eval_jaxpr/ppermute | solution.py:12
  805.6 113.1 %copy-start.4 = (f32[768]{0:T(1024)S(1)}, f32[768]{0:T(1024)}, u32[]{:S(2)}) copy-start(f32[768]{0:T(1024)} %param.9) | copy-start | bytes 9220
  921.1 151.5 %reduce-scatter.7.cloned.1.call-start = ((), (), s32[]{:S(2)}) async-start(), calls=%async_computation.4 | async-start | bytes 557056
Sparse Core Ops, SparseCore 0:
  10.4 39.1 all-gather.1
  921.2 90.0 reduce-scatter.4
  1014.4 58.2 reduce-scatter.6
where the time goes:
time: 1090 us; the launch traced here: 1080 us
  waiting for transfers between devices  803 us (74%)
  blocking collectives  179 us (16%)
  local copies, waits for them, and re-layouts  44 us (4%)
  matrix products  29.8 us (3%)
  between operations  17.6 us (2%)
    ppermute x15, waiting for transfers between devices, passed_along(): lax.ppermute(array, axis, [(i, (i + by) % devices) for i in range(devices)])  699 us
    psum x1, blocking collectives, body(): col_totals = lax.psum(jnp.sum(expo, axis=0), ('grp', 'dev'))  102 us
    psum x1, blocking collectives, body(): summed, grad_gain = lax.psum((loss_part, gain_local), ('grp', 'dev'))  77.2 us
    unnamed x4, waiting for transfers between devices  59.3 us
    all_gather x1, waiting for transfers between devices, body(): first_block = lax.all_gather(teacher_unit, 'dev', axis=0, tiled=True)  36.4 us
  transfers between devices with their start and end apart: 18, of which 18 were waited for; matrix products, arithmetic and copies ran while one was open for 0% of the time, Pallas kernels for 0%

commit v1 on v0

v1 whole, which is shorter than its diff:
```python
import jax
import jax.numpy as jnp
from jax import lax
from jax.sharding import Mesh, PartitionSpec as P

logit_scale = 64.0
norm_eps = 1e-06

AXES = ("zh", "y", "x", "zl", "c")
ROW = ("y", "x")
COL = ("zh", "zl", "c")


def unit_rows(raw):
    length = jnp.sqrt(jnp.sum(raw * raw, axis=-1, keepdims=True) + norm_eps)
    return (raw / length, length)


def swap(blocks, axes):
    return lax.all_to_all(blocks, axes, 0, 0, tiled=True)


def spread(block, axes):
    peers = lax.axis_size(axes)
    return swap(jnp.broadcast_to(block[None], (peers,) + block.shape), axes)


def halves(value):
    high = value.astype(jnp.bfloat16)
    return high, (value - high.astype(jnp.float32)).astype(jnp.bfloat16)


def body(features, teacher, gain, w_head, positives):
    f32, b16 = jnp.float32, jnp.bfloat16
    rows, width = teacher.shape
    depth, window = features.shape[2], features.shape[1]
    nzh, ny, nx, nzl, nc = (lax.axis_size(a) for a in AXES)
    nrow, ncol = ny * nx, nzh * nzl * nc
    devices = nrow * ncol
    total = rows * devices
    part_rows, part_cols = depth // (nzh * ny), width // (nx * nzl * nc)

    teacher_unit = unit_rows(teacher.astype(f32))[0].astype(b16)
    columns = spread(teacher_unit, COL).reshape(ncol * rows, width)

    pooled = jnp.mean(features, axis=1, dtype=f32)
    radius = jnp.sqrt(jnp.mean(pooled * pooled, axis=-1, keepdims=True) + norm_eps)
    scaled = pooled / radius
    normed = (scaled * gain).astype(b16)
    raw = jnp.dot(normed, w_head, preferred_element_type=f32)
    unit, length = unit_rows(raw)
    student = unit.astype(b16)

    share = normed.reshape(rows, nzh, ny, part_rows).transpose(2, 0, 1, 3)
    share = share.reshape(ny, 1, rows, nzh * part_rows)
    share = jnp.broadcast_to(share, (ny, nx) + share.shape[2:]).reshape(nrow, rows, -1)
    pad = 64
    marks = jnp.stack([positives // 128, positives % 128], axis=1).astype(b16)
    marks = jnp.pad(marks, ((0, 0), (0, pad - 2)))
    same = lambda a: jnp.broadcast_to(a[None], (nrow,) + a.shape)
    sent = jnp.concatenate([same(student), share, same(marks)], axis=2)
    got = swap(sent, ROW).reshape(nrow * rows, -1)
    students = got[:, :width]
    normed_rows = got[:, width : width + nzh * part_rows]
    marks = got[:, width + nzh * part_rows :][:, :2].astype(jnp.int32)
    wanted = marks[:, 0] * 128 + marks[:, 1]

    place = jnp.arange(ncol * rows, dtype=jnp.int32)
    peer, inner = place // rows, place % rows
    pzh, pzl, pc = peer // (nzl * nc), (peer // nc) % nzl, peer % nc
    flat = (((pzh * ny + lax.axis_index("y")) * nx + lax.axis_index("x")) * nzl + pzl) * nc + pc
    column_ids = flat * rows + inner

    scores = logit_scale * jnp.dot(students, columns.T, preferred_element_type=f32)
    expo = jnp.exp(scores)
    mask = (column_ids[None, :] == wanted[:, None]).astype(f32)
    row_part = jnp.sum(expo, axis=1)
    col_part = jnp.sum(expo, axis=0)
    pos_part = jnp.sum(scores * mask)
    row_sums = jnp.sum(spread(row_part, ROW), axis=0)
    col_sums = jnp.sum(spread(col_part, COL), axis=0)
    loss_part = (
        jnp.sum(jnp.log(row_sums)) / nrow + jnp.sum(jnp.log(col_sums)) / ncol - 2.0 * pos_part
    )

    weights = (expo / row_sums[:, None] + expo / col_sums[None, :] - 2.0 * mask).astype(b16)
    terms = jnp.dot(weights, columns, preferred_element_type=f32).astype(b16)
    terms = swap(terms.reshape(nrow, rows, width), ROW)
    grad_unit = logit_scale * jnp.sum(terms.astype(f32), axis=0)
    along = jnp.sum(unit * grad_unit, axis=-1, keepdims=True)
    grad_raw = ((grad_unit - unit * along) / length).astype(b16)
    grad_normed = jnp.dot(grad_raw, w_head.T, preferred_element_type=f32)
    gain_part = jnp.sum(grad_normed * scaled, axis=0)

    wide = width // nx
    pieces = grad_raw.reshape(rows, nx, wide).transpose(1, 0, 2)
    pieces = jnp.broadcast_to(pieces[None], (ny,) + pieces.shape).reshape(nrow, rows, wide)
    extra = jnp.concatenate([gain_part, loss_part[None], jnp.zeros((255,), f32)])
    extra = jnp.concatenate(halves(extra)).reshape(-1, wide)
    got = swap(jnp.concatenate([pieces, same(extra)], axis=1), ROW)
    grad_raw_rows = got[:, :rows].reshape(nrow * rows, wide)
    extra = jnp.sum(got[:, rows:].astype(f32), axis=0).reshape(2, -1).sum(axis=0)

    head = jnp.dot(normed_rows.T, grad_raw_rows, preferred_element_type=f32)
    head = head.reshape(nzh, part_rows, nzl * nc, part_cols).transpose(0, 2, 1, 3)
    head = head.reshape(ncol, part_rows, part_cols).astype(b16)
    high, low = halves(extra.reshape(-1, part_cols))
    side = jnp.concatenate([high, low], axis=0)
    side = jnp.pad(side, ((0, part_rows - side.shape[0]), (0, 0)))
    side = jnp.broadcast_to(side[None], (ncol,) + side.shape)
    got = swap(jnp.concatenate([head, side], axis=2), COL).astype(f32)
    got = jnp.sum(got, axis=0)
    grad_head = got[:, :part_cols]
    side = got[:32, part_cols:].reshape(2, -1).sum(axis=0)
    grad_gain = side[:depth]
    loss = side[depth] / (2.0 * total)

    spread_gain = grad_normed * gain
    inner = jnp.mean(spread_gain * scaled, axis=-1, keepdims=True)
    grad_pooled = (spread_gain - scaled * inner) / radius
    grad_features = jnp.broadcast_to((grad_pooled / window)[:, None, :], features.shape)
    return (loss, grad_features.astype(b16), grad_head, grad_gain)


def solution(mesh):
    fine = Mesh(mesh.devices.reshape(4, 4, 4, 2, 2), AXES)
    whole = P(AXES)
    in_specs = (P(AXES, None, None), P(AXES, None), P(), P(), whole)
    out_specs = (P(), P(AXES, None, None), P(("zh", "y"), ("x", "zl", "c")), P())
    return jax.shard_map(body, mesh=fine, in_specs=in_specs, out_specs=out_specs, check_vma=False)
```

time: 1090 us -> 161 us (0.15)
  waiting for transfers between devices: 803 us -> 83.8 us
  blocking collectives: 179 us -> 9.2 us
  starting transfers between devices: 1.39 us -> 37.4 us
  local copies, waits for them, and re-layouts: 44 us -> 8.51 us
  matrix products: 29.8 us -> 8.27 us
  between operations: 17.6 us -> 4.68 us
    ppermute x15 -> x0, waiting for transfers between devices: 699 us -> none  [passed_along(): lax.ppermute(array, axis, [(i, (i + by) % devices) for i in range(devices)])]
    psum x2 -> x0, blocking collectives: 179 us -> none  [the longest x1 102 us: body(): col_totals = lax.psum(jnp.sum(expo, axis=0), ('grp', 'dev'))]
    all_to_all x0 -> x6, waiting for transfers between devices: none -> 83.8 us  [swap(): return lax.all_to_all(blocks, axes, 0, 0, tiled=True)]
    unnamed x4 -> x0, waiting for transfers between devices: 59.3 us -> none
    all_to_all x0 -> x6, starting transfers between devices: none -> 37.4 us  [swap(): return lax.all_to_all(blocks, axes, 0, 0, tiled=True)]
    all_gather x1 -> x0, waiting for transfers between devices: 36.4 us -> none  [body(): first_block = lax.all_gather(teacher_unit, 'dev', axis=0, tiled=True)]
    dot_general x20 -> x5, matrix products: 29.8 us -> 8.27 us  [the longest x1 3.63 us: body(): jnp.dot(students, columns.T, preferred_element_type=f32)]
    dynamic_update_slice x16 -> x0, local copies, waits for them, and re-layouts: 16.1 us -> none  [place(): store = lax.dynamic_update_slice(store, block, (start, zero))]
  transfers between devices with their start and end apart: 18 -> 6, of which waited for: 18 -> 6; matrix products, arithmetic and copies ran while one was open for 0% -> 2% of each run, Pallas kernels for 0% -> 0%
where the time goes in v1:
time: 161 us; the launch traced here: 160 us
  waiting for transfers between devices  83.8 us (52%)
  starting transfers between devices  37.4 us (23%)
  blocking collectives  9.2 us (6%)
  local copies, waits for them, and re-layouts  8.51 us (5%)
  matrix products  8.27 us (5%)
  other arithmetic  8.06 us (5%)
  between operations  4.68 us (3%)
    all_to_all x6, waiting for transfers between devices, swap(): return lax.all_to_all(blocks, axes, 0, 0, tiled=True)  83.8 us
    all_to_all x6, starting transfers between devices, swap(): return lax.all_to_all(blocks, axes, 0, 0, tiled=True)  37.4 us
    all_to_all x1, blocking collectives, swap(): return lax.all_to_all(blocks, axes, 0, 0, tiled=True)  9.2 us
    dot_general x1, matrix products, body(): jnp.dot(students, columns.T, preferred_element_type=f32)  3.63 us
  transfers between devices with their start and end apart: 6, of which 6 were waited for; matrix products, arithmetic and copies ran while one was open for 2% of the time, Pallas kernels for 0%

profile of v1, /device:TPU:1, one launch (start us, length us, event | category | flops | bytes accessed | tf_op | source)
XLA Modules:
  0.0 159.9 jit_solution(574327961219696055)
XLA Ops:
  0.6 0.0 copy-start
  0.6 0.0 copy-start.3
  0.7 0.8 convert_bitcast_fusion
  1.5 0.1 copy.39
  1.6 0.8 mul.126
  2.3 1.8 %convert_reduce_fusion = f32[32,768]{1,0:T(8,128)S(1)} fusion(bf16[32,32,768]{2,1,0:T(8,128)(2,1)} %param.5), kind=kLoop, calls=%fused_computation | loop fusion | flops 1548288 | bytes 1671168 | tf_op jit(solution)/shard_map/reduce_sum | solution.py:46
  4.1 0.1 broadcast_multiply_fusion
  4.3 0.0 copy-done
  4.3 0.0 copy-done.3
  4.3 0.5 multiply_reduce_fusion.1
  4.8 0.3 div.128
  5.1 0.1 fusion.16
  5.2 0.1 broadcast_in_dim.27
  5.4 0.1 fusion.48
  5.5 0.1 broadcast_in_dim.26
  5.6 2.0 %concatenate.21 = bf16[16,32,1280]{2,1,0:T(8,128)(2,1)} concatenate(bf16[16,32,1024]{2,1,0:T(8,128)(2,1)S(1)} %broadcast_in_dim.26, bf16[16,32,192]{2,1,0:T(8,128)(2,1)S(1)} %bitcast.45, bf16[16,32,64]{2,1,0:T(8,128)(2,1)S(1)} %broadcast_in_dim.29), dimensions={2} | concatenate | bytes 2621440 | tf_op jit(solution)/shard_map/concatenate | solution.py:61
  7.6 0.0 copy-start.1
  7.6 7.8 %all-to-all-start = ((bf16[16,32,1280]{2,1,0:T(8,128)(2,1)}), bf16[16,32,1280]{2,1,0:T(8,128)(2,1)}, u32[]{:S(2)}, u32[]{:S(2)}) async-start(bf16[16,32,1280]{2,1,0:T(8,128)(2,1)} %concatenate.21), calls=%async_computation | async-start | bytes 2621440 | tf_op jit(solution)/shard_map/all_to_all | solution.py:20
  15.4 0.0 copy-done.1
  15.4 0.1 fusion.14
  15.5 0.1 fusion.15
  15.6 18.6 %all-to-all-done = bf16[16,32,1280]{2,1,0:T(8,128)(2,1)} async-done(((bf16[16,32,1280]{2,1,0:T(8,128)(2,1)}), bf16[16,32,1280]{2,1,0:T(8,128)(2,1)}, u32[]{:S(2)}, u32[]{:S(2)}) %all-to-all-start) | async-done | bytes 1310752 | tf_op jit(solution)/shard_map/all_to_all | solution.py:20
  34.2 1.1 broadcast_in_dim.30
  35.3 11.4 %all-to-all-start.1 = ((bf16[16,32,1024]{2,1,0:T(8,128)(2,1)}), bf16[16,32,1024]{2,1,0:T(8,128)(2,1)S(1)}, u32[]{:S(2)}, u32[]{:S(2)}) async-start(bf16[16,32,1024]{2,1,0:T(8,128)(2,1)} %broadcast_in_dim.30), calls=%async_computation.1 | async-start | bytes 2097152 | tf_op jit(solution)/shard_map/all_to_all | solution.py:20
  46.8 1.0 slice_convert_fusion
  47.8 0.2 fusion.11
  48.1 26.7 %all-to-all-done.1 = bf16[16,32,1024]{2,1,0:T(8,128)(2,1)S(1)} async-done(((bf16[16,32,1024]{2,1,0:T(8,128)(2,1)}), bf16[16,32,1024]{2,1,0:T(8,128)(2,1)S(1)}, u32[]{:S(2)}, u32[]{:S(2)}) %all-to-all-start.1) | async-done | bytes 1048608 | tf_op jit(solution)/shard_map/all_to_all | solution.py:20
  74.7 3.6 %fusion.2 = (f32[]{:T(128)}, f32[512]{0:T(512)S(1)}, f32[512]{0:T(512)S(1)}, f32[512,512]{1,0:T(8,128)}) fusion(s32[512]{0:T(512)S(1)} %fusion.36, s32[512]{0:T(512)S(1)} %fusion.11, bf16[512,1024]{1,0:T(8,128)(2,1)S(1)} %bitcast.40, bf16[512,1280]{1,0:T(8,128)(2,1)} %bitcast.4), kind=kOutput, calls=%fused_computation.9 | convolution fusion | flops 538442752 | bytes 3153924 | tf_op jit(solution)/shard_map/dot_general | solution.py:74
  78.4 9.2 %all_to_all.37 = f32[16,1,512]{2,1,0:T(1,128)S(1)} all-to-all(f32[16,1,512]{2,1,0:T(1,128)S(1)} %broadcast_in_dim.31), channel_id=1, replica_groups=mesh['zh'=4,'y'=4,'x'=4,'zl'=2,'c'=2] {'y','x'}, dimensions={0} | all-to-all | bytes 65536 | tf_op jit(solution)/shard_map/all_to_all | solution.py:20
  87.6 0.6 broadcast_in_dim.32
  88.2 5.0 %all-to-all-start.3 = ((f32[16,1,512]{2,1,0:T(1,128)}), f32[16,1,512]{2,1,0:T(1,128)S(1)}, u32[]{:S(2)}, u32[]{:S(2)}) async-start(f32[16,1,512]{2,1,0:T(1,128)} %broadcast_in_dim.32), calls=%async_computation.3 | async-start | bytes 65536 | tf_op jit(solution)/shard_map/all_to_all | solution.py:20
  93.2 7.3 %all-to-all-done.3 = f32[16,1,512]{2,1,0:T(1,128)S(1)} async-done(((f32[16,1,512]{2,1,0:T(1,128)}), f32[16,1,512]{2,1,0:T(1,128)S(1)}, u32[]{:S(2)}, u32[]{:S(2)}) %all-to-all-start.3) | async-done | bytes 32800 | tf_op jit(solution)/shard_map/all_to_all | solution.py:20
  100.6 3.1 %convolution_convert_fusion = bf16[512,1024]{1,0:T(8,128)(2,1)} fusion(bf16[512,1024]{1,0:T(8,128)(2,1)S(1)} %bitcast.41, f32[512,512]{1,0:T(8,128)} %get-tuple-element.19, s32[512]{0:T(512)S(1)} %fusion.36, f32[512]{0:T(512)S(1)} %reduce_sum.178, f32[512]{0:T(512)S(1)} %reduce_sum.176, s32[512]{0:T(512)S(1)} %fusion.11), kind=kOutput, calls=%fused_computation.2 | convolution fusion | flops 539230208 | bytes 3153920 | tf_op jit(solution)/shard_map/dot_general | solution.py:87
  103.7 3.7 %all-to-all-start.4 = ((bf16[16,32,1024]{2,1,0:T(8,128)(2,1)}), bf16[16,32,1024]{2,1,0:T(8,128)(2,1)S(1)}, u32[]{:S(2)}, u32[]{:S(2)}) async-start(bf16[16,32,1024]{2,1,0:T(8,128)(2,1)} %bitcast.42), calls=%async_computation.4 | async-start | bytes 2097152 | tf_op jit(solution)/shard_map/all_to_all | solution.py:20
  108.0 0.6 log_reduce_fusion.1
  108.6 0.6 log_reduce_fusion
  110.5 13.7 %all-to-all-done.4 = bf16[16,32,1024]{2,1,0:T(8,128)(2,1)S(1)} async-done(((bf16[16,32,1024]{2,1,0:T(8,128)(2,1)}), bf16[16,32,1024]{2,1,0:T(8,128)(2,1)S(1)}, u32[]{:S(2)}, u32[]{:S(2)}) %all-to-all-start.4) | async-done | bytes 1048608 | tf_op jit(solution)/shard_map/all_to_all | solution.py:20
  124.2 0.2 convert_reduce_fusion.1
  124.4 0.2 multiply_reduce_fusion
  124.6 0.1 divide_convert_fusion
  124.8 0.7 multiply_reduce_fusion.2
  125.5 0.1 pad_maximum_fusion.2
  125.6 0.7 pad_maximum_fusion
  126.4 4.2 %all-to-all-start.5 = ((bf16[16,40,256]{2,1,0:T(8,128)(2,1)}), bf16[16,40,256]{2,1,0:T(8,128)(2,1)S(1)}, u32[]{:S(2)}, u32[]{:S(2)}) async-start(bf16[16,40,256]{2,1,0:T(8,128)(2,1)} %pad_maximum_fusion), calls=%async_computation.5 | async-start | bytes 655360 | tf_op jit(solution)/shard_map/all_to_all | solution.py:20
  130.6 1.0 slice_bitcast_fusion
  131.6 0.1 copy.31
  131.7 7.2 %all-to-all-done.5 = bf16[16,40,256]{2,1,0:T(8,128)(2,1)S(1)} async-done(((bf16[16,40,256]{2,1,0:T(8,128)(2,1)}), bf16[16,40,256]{2,1,0:T(8,128)(2,1)S(1)}, u32[]{:S(2)}, u32[]{:S(2)}) %all-to-all-start.5) | async-done | bytes 327712 | tf_op jit(solution)/shard_map/all_to_all | solution.py:20
  138.9 0.1 copy.35
  139.1 0.1 reshape.196
  139.2 0.3 convolution_convert_fusion.1
  139.5 0.8 pad_maximum_fusion.1
  140.4 5.4 %all-to-all-start.6 = ((bf16[16,48,128]{2,1,0:T(8,128)(2,1)}), bf16[16,48,128]{2,1,0:T(8,128)(2,1)S(1)}, u32[]{:S(2)}, u32[]{:S(2)}) async-start(bf16[16,48,128]{2,1,0:T(8,128)(2,1)} %pad_maximum_fusion.1), calls=%async_computation.6 | async-start | bytes 393216 | tf_op jit(solution)/shard_map/all_to_all | solution.py:20
  145.7 0.1 multiply_convert_fusion
  145.8 10.3 %all-to-all-done.6 = bf16[16,48,128]{2,1,0:T(8,128)(2,1)S(1)} async-done(((bf16[16,48,128]{2,1,0:T(8,128)(2,1)}), bf16[16,48,128]{2,1,0:T(8,128)(2,1)S(1)}, u32[]{:S(2)}, u32[]{:S(2)}) %all-to-all-start.6) | async-done | bytes 196640 | tf_op jit(solution)/shard_map/all_to_all | solution.py:20
  156.1 0.0 copy-start.2
  156.1 0.1 slice.53
  156.2 0.1 reshape.197
  156.3 0.0 copy-start.4
  156.3 0.5 slice.43
  157.5 1.3 broadcast_in_dim.38
  158.8 0.0 copy-done.2
  158.8 0.0 copy-done.4
  (30 shorter events, 0.5 us)
Async XLA Ops:
  0.6 3.6 %copy-start = (bf16[768,1024]{1,0:T(8,128)(2,1)S(1)}, bf16[768,1024]{1,0:T(8,128)(2,1)}, u32[]{:S(2)}) copy-start(bf16[768,1024]{1,0:T(8,128)(2,1)} %param.8) | copy-start | bytes 4718596
  0.6 3.6 %copy-start.3 = (f32[768]{0:T(1024)S(1)}, f32[768]{0:T(1024)}, u32[]{:S(2)}) copy-start(f32[768]{0:T(1024)} %param.7) | copy-start | bytes 9220
  7.6 7.8 %copy-start.1 = (bf16[32,1024]{1,0:T(8,128)(2,1)S(1)}, bf16[32,1024]{1,0:T(8,128)(2,1)}, u32[]{:S(2)}) copy-start(bf16[32,1024]{1,0:T(8,128)(2,1)} %param.6) | copy-start | bytes 196612
  7.6 26.6 %all-to-all-start = ((bf16[16,32,1280]{2,1,0:T(8,128)(2,1)}), bf16[16,32,1280]{2,1,0:T(8,128)(2,1)}, u32[]{:S(2)}, u32[]{:S(2)}) async-start(bf16[16,32,1280]{2,1,0:T(8,128)(2,1)} %concatenate.21), calls=%async_computation | async-start | bytes 2621440 | tf_op jit(solution)/shard_map/all_to_all | solution.py:20
  35.3 39.4 %all-to-all-start.1 = ((bf16[16,32,1024]{2,1,0:T(8,128)(2,1)}), bf16[16,32,1024]{2,1,0:T(8,128)(2,1)S(1)}, u32[]{:S(2)}, u32[]{:S(2)}) async-start(bf16[16,32,1024]{2,1,0:T(8,128)(2,1)} %broadcast_in_dim.30), calls=%async_computation.1 | async-start | bytes 2097152 | tf_op jit(solution)/shard_map/all_to_all | solution.py:20
  88.2 12.3 %all-to-all-start.3 = ((f32[16,1,512]{2,1,0:T(1,128)}), f32[16,1,512]{2,1,0:T(1,128)S(1)}, u32[]{:S(2)}, u32[]{:S(2)}) async-start(f32[16,1,512]{2,1,0:T(1,128)} %broadcast_in_dim.32), calls=%async_computation.3 | async-start | bytes 65536 | tf_op jit(solution)/shard_map/all_to_all | solution.py:20
  103.7 20.5 %all-to-all-start.4 = ((bf16[16,32,1024]{2,1,0:T(8,128)(2,1)}), bf16[16,32,1024]{2,1,0:T(8,128)(2,1)S(1)}, u32[]{:S(2)}, u32[]{:S(2)}) async-start(bf16[16,32,1024]{2,1,0:T(8,128)(2,1)} %bitcast.42), calls=%async_computation.4 | async-start | bytes 2097152 | tf_op jit(solution)/shard_map/all_to_all | solution.py:20
  126.4 12.5 %all-to-all-start.5 = ((bf16[16,40,256]{2,1,0:T(8,128)(2,1)}), bf16[16,40,256]{2,1,0:T(8,128)(2,1)S(1)}, u32[]{:S(2)}, u32[]{:S(2)}) async-start(bf16[16,40,256]{2,1,0:T(8,128)(2,1)} %pad_maximum_fusion), calls=%async_computation.5 | async-start | bytes 655360 | tf_op jit(solution)/shard_map/all_to_all | solution.py:20
  140.4 15.7 %all-to-all-start.6 = ((bf16[16,48,128]{2,1,0:T(8,128)(2,1)}), bf16[16,48,128]{2,1,0:T(8,128)(2,1)S(1)}, u32[]{:S(2)}, u32[]{:S(2)}) async-start(bf16[16,48,128]{2,1,0:T(8,128)(2,1)} %pad_maximum_fusion.1), calls=%async_computation.6 | async-start | bytes 393216 | tf_op jit(solution)/shard_map/all_to_all | solution.py:20
  156.1 2.6 %copy-start.2 = (f32[48,128]{1,0:T(8,128)}, f32[48,128]{1,0:T(8,128)S(1)}, u32[]{:S(2)}) copy-start(f32[48,128]{1,0:T(8,128)S(1)} %convert_reduce_fusion.2) | copy-start | bytes 73732
  156.3 2.4 %copy-start.4 = (f32[1024]{0:T(1024)}, f32[1024]{0:T(1024)S(1)}, u32[]{:S(2)}) copy-start(f32[1024]{0:T(1024)S(1)} %reduce_sum.188) | copy-start | bytes 12292

commit v2 on v1

v2 whole, which is shorter than its diff:
```python
import jax
import jax.numpy as jnp
from jax import lax
from jax.experimental import pallas as pl
from jax.experimental.pallas import tpu as pltpu
from jax.sharding import Mesh, PartitionSpec as P

logit_scale = 64.0
norm_eps = 1e-06

AXES = ("zh", "y", "x", "zl", "c")
ROW = ("y", "x")
COL = ("zh", "zl", "c")

D, E, ROWS = 768, 1024, 32
SIDE = 512
MARK = 128
CHUNK = 128
f32, b16 = jnp.float32, jnp.bfloat16
VMEM = pl.BlockSpec(memory_space=pltpu.VMEM)
SMEM = pl.BlockSpec(memory_space=pltpu.SMEM)


def unit_rows(raw):
    length = jnp.sqrt(jnp.sum(raw * raw, axis=-1, keepdims=True) + norm_eps)
    return (raw / length, length)


def swap(blocks, axes):
    return lax.all_to_all(blocks, axes, 0, 0, tiled=True)


def same(block, peers):
    return jnp.broadcast_to(block[None], (peers,) + block.shape)


def halves(value):
    high = value.astype(b16)
    return high, (value - high.astype(f32)).astype(b16)


def other_core(block):
    return lax.ppermute(block, "c", [(0, 1), (1, 0)])


def along_z(block, step):
    pairs = []
    for z in range(8):
        pairs += [(2 * z, 2 * ((z + step) % 8)), (2 * z + 1, 2 * ((z - step) % 8) + 1)]
    return lax.ppermute(block, COL, pairs)


def gather_columns(block):
    chip = jnp.concatenate([block, other_core(block)], axis=0)
    near = [along_z(chip, 1), along_z(chip, 2), along_z(chip, 3), along_z(block, 4)]
    near = jnp.concatenate(near, axis=0)
    return chip, near, other_core(near)


def wanted_mask(marks, shift):
    marks = marks.astype(f32)
    wanted = marks[:, 0:1] * 128.0 + marks[:, 1:2]
    place = lax.broadcasted_iota(jnp.int32, (1, SIDE), 1)
    ids = (place >> 7) * 2048 + shift * 128 + (place & 127)
    return wanted == ids.astype(f32)


def lanes_to_rows(row):
    return jnp.transpose(jnp.broadcast_to(row, (128, row.shape[1])))


def scores_kernel(where, got, head, chip, near, far, expo, teach, row_part, col_part, pos_part):
    z, c, shift = where[0], where[1], where[2]
    up = 1 - 2 * c

    def put(ref, start, zz, cc):
        slot = pl.multiple_of((((zz + 16) & 7) * 2 + cc) * ROWS, ROWS)
        teach[pl.ds(slot, ROWS), :] = ref[start : start + ROWS, :]

    put(chip, 0, z, c)
    put(chip, ROWS, z, 1 - c)
    for ref, cc, sign in ((near, c, -up), (far, 1 - c, up)):
        for k in (1, 2, 3):
            put(ref, (k - 1) * 2 * ROWS, z + sign * k, cc)
            put(ref, (k - 1) * 2 * ROWS + ROWS, z + sign * k, 1 - cc)
        put(ref, 6 * ROWS, z + 4, cc)

    col = jnp.zeros((1, SIDE), f32)
    pos = jnp.zeros((1, SIDE), f32)
    for n in range(SIDE // CHUNK):
        at = slice(n * CHUNK, (n + 1) * CHUNK)
        raw = jnp.dot(got[at, :D], head[...], preferred_element_type=f32)
        student = unit_rows(raw)[0].astype(b16)
        scores = logit_scale * lax.dot_general(
            student, teach[...], (((1,), (1,)), ((), ())), preferred_element_type=f32
        )
        mask = wanted_mask(got[at, D:], shift)
        pos = pos + jnp.sum(jnp.where(mask, scores, 0.0), axis=0, keepdims=True)
        e = jnp.exp(scores)
        expo[at, :] = e
        col = col + jnp.sum(e, axis=0, keepdims=True)
        lanes = sum(e[:, k : k + 128] for k in range(0, SIDE, 128))
        row_part[:, at] = jnp.sum(jnp.transpose(lanes), axis=0, keepdims=True)
    col_part[...] = col
    pos_part[...] = pos


def weights_kernel(where, got, expo, teach, row_in, col_in, terms, row_sums, col_sums):
    shift = where[2]
    rows = jnp.sum(row_in[...], axis=0)
    cols = jnp.sum(col_in[...], axis=0)
    row_sums[...] = rows
    col_sums[...] = cols
    col_inv = 1.0 / cols
    row_inv = lanes_to_rows(1.0 / rows)
    for n in range(SIDE // CHUNK):
        at = slice(n * CHUNK, (n + 1) * CHUNK)
        mask = wanted_mask(got[at, D:], shift)
        scale = col_inv + jnp.concatenate([row_inv[at, :]] * (SIDE // 128), axis=1)
        weights = expo[at, :] * scale - jnp.where(mask, 2.0, 0.0)
        terms[at, :] = jnp.dot(
            weights.astype(b16), teach[...], preferred_element_type=f32
        ).astype(b16)


def shaped(*shape, dtype=f32):
    return jax.ShapeDtypeStruct(shape, dtype)


def body(features, teacher, gain, w_head, positives):
    rows, width = teacher.shape
    depth, window = features.shape[2], features.shape[1]
    nzh, ny, nx, nzl, nc = (lax.axis_size(a) for a in AXES)
    nrow, ncol = ny * nx, nzh * nzl * nc
    total = rows * nrow * ncol
    part_rows, part_cols = depth // (nzh * ny), width // (nx * nzl * nc)
    zh, y, x, zl, c = (lax.axis_index(a) for a in AXES)
    where = jnp.stack([zh * nzl + zl, c, y * nx + x]).astype(jnp.int32)

    teacher_unit = unit_rows(teacher.astype(f32))[0].astype(b16)
    chip, near, far = gather_columns(teacher_unit)

    pooled = jnp.mean(features, axis=1, dtype=f32)
    radius = jnp.sqrt(jnp.mean(pooled * pooled, axis=-1, keepdims=True) + norm_eps)
    scaled = pooled / radius
    normed = (scaled * gain).astype(b16)
    marks = jnp.stack([positives // 128, positives % 128], axis=1).astype(b16)
    marks = jnp.pad(marks, ((0, 0), (0, MARK - 2)))
    got = swap(same(jnp.concatenate([normed, marks], axis=1), nrow), ROW)
    got = got.reshape(nrow * rows, -1)

    raw = jnp.dot(normed, w_head, preferred_element_type=f32)
    unit, length = unit_rows(raw)

    expo, teach, row_part, col_part, pos_part = pl.pallas_call(
        scores_kernel,
        out_shape=[
            shaped(SIDE, SIDE),
            shaped(SIDE, E, dtype=b16),
            shaped(1, SIDE),
            shaped(1, SIDE),
            shaped(1, SIDE),
        ],
        in_specs=[SMEM] + [VMEM] * 5,
        out_specs=[VMEM] * 5,
        compiler_params=pltpu.CompilerParams(vmem_limit_bytes=32 << 20),
        name="scores",
    )(where, got, w_head, chip, near, far)
    row_in = swap(same(row_part, nrow), ROW)
    col_in = swap(same(col_part, ncol), COL)
    terms, row_sums, col_sums = pl.pallas_call(
        weights_kernel,
        out_shape=[shaped(SIDE, E, dtype=b16), shaped(1, SIDE), shaped(1, SIDE)],
        in_specs=[SMEM] + [VMEM] * 5,
        out_specs=[VMEM] * 3,
        compiler_params=pltpu.CompilerParams(vmem_limit_bytes=32 << 20),
        name="weights",
    )(where, got, expo, teach, row_in, col_in)
    loss_part = (
        jnp.sum(jnp.log(row_sums)) / nrow
        + jnp.sum(jnp.log(col_sums)) / ncol
        - 2.0 * jnp.sum(pos_part)
    )

    terms = swap(terms.reshape(nrow, rows, width), ROW)
    grad_unit = logit_scale * jnp.sum(terms.astype(f32), axis=0)
    along = jnp.sum(unit * grad_unit, axis=-1, keepdims=True)
    grad_raw = ((grad_unit - unit * along) / length).astype(b16)
    grad_normed = jnp.dot(grad_raw, w_head.T, preferred_element_type=f32)
    gain_part = jnp.sum(grad_normed * scaled, axis=0)

    wide = width // nx
    pieces = grad_raw.reshape(rows, nx, wide).transpose(1, 0, 2)
    pieces = jnp.broadcast_to(pieces[None], (ny,) + pieces.shape).reshape(nrow, rows, wide)
    extra = jnp.concatenate([gain_part, loss_part[None], jnp.zeros((255,), f32)])
    extra = jnp.concatenate(halves(extra)).reshape(-1, wide)
    back = swap(jnp.concatenate([pieces, same(extra, nrow)], axis=1), ROW)
    grad_raw_rows = back[:, :rows].reshape(nrow * rows, wide)
    extra = jnp.sum(back[:, rows:].astype(f32), axis=0).reshape(2, -1).sum(axis=0)

    normed_rows = got[:, :D].reshape(nrow * rows, nzh, ny, part_rows)
    normed_rows = lax.dynamic_index_in_dim(normed_rows, y, 2, keepdims=False)
    normed_rows = normed_rows.reshape(nrow * rows, nzh * part_rows)
    head = jnp.dot(normed_rows.T, grad_raw_rows, preferred_element_type=f32)
    head = head.reshape(nzh, part_rows, nzl * nc, part_cols).transpose(0, 2, 1, 3)
    head = head.reshape(ncol, part_rows, part_cols).astype(b16)
    high, low = halves(extra.reshape(-1, part_cols))
    side = jnp.concatenate([high, low], axis=0)
    side = jnp.pad(side, ((0, part_rows - side.shape[0]), (0, 0)))
    last = swap(jnp.concatenate([head, same(side, ncol)], axis=2), COL).astype(f32)
    last = jnp.sum(last, axis=0)
    grad_head = last[:, :part_cols]
    side = last[:32, part_cols:].reshape(2, -1).sum(axis=0)
    grad_gain = side[:depth]
    loss = side[depth] / (2.0 * total)

    spread_gain = grad_normed * gain
    inner = jnp.mean(spread_gain * scaled, axis=-1, keepdims=True)
    grad_pooled = (spread_gain - scaled * inner) / radius
    grad_features = jnp.broadcast_to((grad_pooled / window)[:, None, :], features.shape)
    return (loss, grad_features.astype(b16), grad_head, grad_gain)


def solution(mesh):
    fine = Mesh(mesh.devices.reshape(4, 4, 4, 2, 2), AXES)
    in_specs = (P(AXES, None, None), P(AXES, None), P(), P(), P(AXES))
    out_specs = (P(), P(AXES, None, None), P(("zh", "y"), ("x", "zl", "c")), P())
    return jax.shard_map(body, mesh=fine, in_specs=in_specs, out_specs=out_specs, check_vma=False)
```

time: 161 us -> 128 us (0.80)
  waiting for transfers between devices: 83.8 us -> 36.4 us
  blocking collectives: 9.2 us -> 27.4 us
  matrix products: 8.27 us -> 1.46 us
  Pallas kernels: 0 us -> 6.16 us
  local copies, waits for them, and re-layouts: 8.51 us -> 3.81 us
    all_to_all x6 -> x4, waiting for transfers between devices: 83.8 us -> 31.4 us  [swap(): return lax.all_to_all(blocks, axes, 0, 0, tiled=True)]
    all_to_all x1 -> x2, blocking collectives: 9.2 us -> 27.4 us  [swap(): return lax.all_to_all(blocks, axes, 0, 0, tiled=True)]
    ppermute x0 -> x6, starting transfers between devices: none -> 17.6 us  [the longest x4 10.1 us: along_z(): return lax.ppermute(block, COL, pairs)]
    all_to_all x6 -> x4, starting transfers between devices: 37.4 us -> 20.9 us  [swap(): return lax.all_to_all(blocks, axes, 0, 0, tiled=True)]
    dot_general x2 -> x0, matrix products: 6.77 us -> none  [the longest x1 3.63 us: body(): jnp.dot(students, columns.T, preferred_element_type=f32)]
    pallas_call x0 -> x2, Pallas kernels: none -> 6.16 us  [the longest x1 3.73 us: body(): pl.pallas_call(scores_kernel, out_shape=[shaped(SIDE, SIDE), shaped(SIDE,...]
    ppermute x0 -> x6, waiting for transfers between devices: none -> 5.03 us  [the longest x4 3.66 us: along_z(): return lax.ppermute(block, COL, pairs)]
    concatenate x1, local copies, waits for them, and re-layouts: 1.96 us -> 0.01 us  [gather_columns(): near = jnp.concatenate(near, axis=0)]
  transfers between devices with their start and end apart: 6 -> 10, of which waited for: 6 -> 5; matrix products, arithmetic and copies ran while one was open for 2% -> 4% of each run, Pallas kernels for 0% -> 0%
where the time goes in v2:
time: 128 us; the launch traced here: 127 us
  starting transfers between devices  38.6 us (30%)
  waiting for transfers between devices  36.4 us (28%)
  blocking collectives  27.4 us (21%)
  other arithmetic  8.84 us (7%)
  Pallas kernels  6.16 us (5%)
  between operations  4.76 us (4%)
  local copies, waits for them, and re-layouts  3.81 us (3%)
  matrix products  1.46 us (1%)
    all_to_all x4, waiting for transfers between devices, swap(): return lax.all_to_all(blocks, axes, 0, 0, tiled=True)  31.4 us
    all_to_all x2, blocking collectives, swap(): return lax.all_to_all(blocks, axes, 0, 0, tiled=True)  27.4 us
    all_to_all x4, starting transfers between devices, swap(): return lax.all_to_all(blocks, axes, 0, 0, tiled=True)  20.9 us
    ppermute x4, starting transfers between devices, along_z(): return lax.ppermute(block, COL, pairs)  10.1 us
    ppermute x2, starting transfers between devices, other_core(): return lax.ppermute(block, 'c', [(0, 1), (1, 0)])  7.53 us
    pallas_call x1, Pallas kernels, body(): pl.pallas_call(scores_kernel, out_shape=[shaped(SIDE, SIDE), shaped(SIDE,...  3.73 us
    ppermute x4, waiting for transfers between devices, along_z(): return lax.ppermute(block, COL, pairs)  3.66 us
  transfers between devices with their start and end apart: 10, of which 5 were waited for; matrix products, arithmetic and copies ran while one was open for 4% of the time, Pallas kernels for 0%

profile of v2, /device:TPU:1, one launch (start us, length us, event | category | flops | bytes accessed | tf_op | source)
XLA Modules:
  0.0 127.4 jit_solution(814287084433235240)
XLA Ops:
  0.6 0.0 copy-start.6
  0.6 0.0 copy-start.8
  0.7 1.0 fusion.2
  1.6 0.9 fusion.3
  2.6 3.3 %collective-permute-start = (bf16[32,1024]{1,0:T(8,128)(2,1)S(1)}, bf16[32,1024]{1,0:T(8,128)(2,1)S(1)}, u32[]{:S(2)}, u32[]{:S(2)}) collective-permute-start(bf16[32,1024]{1,0:T(8,128)(2,1)S(1)} %fusion.3), channel_id=1, source_target_pairs={{0,1},{1,0},{2,3},{3,2},{4,5},{5,4},{6,7},{7,6},{8,9},{9,8},{10,11... | collective-permute-start | bytes 196616 | tf_op jit(solution)/shard_map/ppermute | solution.py:43
  5.9 5.2 %collective-permute-start.4 = (bf16[32,1024]{1,0:T(8,128)(2,1)S(1)}, bf16[32,1024]{1,0:T(8,128)(2,1)S(1)}, u32[]{:S(2)}, u32[]{:S(2)}) collective-permute-start(bf16[32,1024]{1,0:T(8,128)(2,1)S(1)} %fusion.3), channel_id=1, source_target_pairs={{0,128},{1,129},{2,130},{3,131},{64,192},{65,193},{66,194},{67,195... | collective-permute-start | bytes 196616 | tf_op jit(solution)/shard_map/ppermute | solution.py:50
  11.1 1.8 %convert_reduce_fusion = f32[32,768]{1,0:T(8,128)S(1)} fusion(bf16[32,32,768]{2,1,0:T(8,128)(2,1)} %param.5), kind=kLoop, calls=%fused_computation | loop fusion | flops 1548288 | bytes 1671168 | tf_op jit(solution)/shard_map/reduce_sum | solution.py:143
  12.9 0.1 multiply_reduce_fusion.4
  13.0 0.1 multiply_convert_fusion.1
  13.1 0.0 copy-done.8
  13.1 0.0 copy-start.3
  13.2 0.0 collective-permute-done
  13.2 0.1 collective-permute-start.1
  13.3 0.1 copy.21
  13.4 0.0 collective-permute-start.2
  13.4 1.0 broadcast_in_dim.22
  14.4 0.0 copy-done.1
  14.4 6.9 %all-to-all-start = ((bf16[16,32,896]{2,1,0:T(8,128)(2,1)}), bf16[16,32,896]{2,1,0:T(8,128)(2,1)S(1)}, u32[]{:S(2)}, u32[]{:S(2)}) async-start(bf16[16,32,896]{2,1,0:T(8,128)(2,1)} %broadcast_in_dim.22), calls=%async_computation | async-start | bytes 1835008 | tf_op jit(solution)/shard_map/all_to_all | solution.py:30
  21.3 4.8 %collective-permute-start.3 = (bf16[64,1024]{1,0:T(8,128)(2,1)S(1)}, bf16[64,1024]{1,0:T(8,128)(2,1)S(1)}, u32[]{:S(2)}, u32[]{:S(2)}) collective-permute-start(bf16[64,1024]{1,0:T(8,128)(2,1)S(1)} %pad_maximum_fusion.2.chip), channel_id=1, source_target_pairs={{0,66},{1,131},{2,128},{3,193},{64,130},{65,195},{66,192},{67,1},{... | collective-permute-start | bytes 393224 | tf_op jit(solution)/shard_map/ppermute | solution.py:50
  26.1 0.0 collective-permute-done.1
  26.1 0.0 collective-permute-done.2
  26.2 3.7 %collective-permute-done.3 = bf16[64,1024]{1,0:T(8,128)(2,1)S(1)} collective-permute-done((bf16[64,1024]{1,0:T(8,128)(2,1)S(1)}, bf16[64,1024]{1,0:T(8,128)(2,1)S(1)}, u32[]{:S(2)}, u32[]{:S(2)}) %collective-permute-start.3) | collective-permute-done | bytes 131104 | tf_op jit(solution)/shard_map/ppermute | solution.py:50
  29.8 0.0 collective-permute-done.4
  29.9 4.2 %collective-permute-start.5 = (bf16[224,1024]{1,0:T(8,128)(2,1)S(1)}, bf16[224,1024]{1,0:T(8,128)(2,1)S(1)}, u32[]{:S(2)}, u32[]{:S(2)}) collective-permute-start(bf16[224,1024]{1,0:T(8,128)(2,1)S(1)} %constant_dynamic-update-slice_fusion.near), channel_id=1, source_target_pairs={{0,1},{1,0},{2,3},{3,2},{4,5},{5,4},{6,7},{7,6},{8,9},{9,8},{10,11... | collective-permute-start | bytes 1376264 | tf_op jit(solution)/shard_map/ppermute | solution.py:43
  34.1 0.1 pad_add_fusion.where
  34.2 1.4 %collective-permute-done.5.far = bf16[224,1024]{1,0:T(8,128)(2,1)S(1)} collective-permute-done((bf16[224,1024]{1,0:T(8,128)(2,1)S(1)}, bf16[224,1024]{1,0:T(8,128)(2,1)S(1)}, u32[]{:S(2)}, u32[]{:S(2)}) %collective-permute-start.5) | collective-permute-done | bytes 458784 | tf_op jit(solution)/shard_map/ppermute | solution.py:43
  35.5 0.0 all-to-all-done
  35.5 0.0 copy-done
  35.5 3.7 %scores.1 = (f32[512,512]{1,0:T(8,128)S(1)}, bf16[512,1024]{1,0:T(8,128)(2,1)S(1)}, f32[1,512]{1,0:T(1,128)S(1)}, f32[1,512]{1,0:T(1,128)S(1)}, f32[1,512]{1,0:T(1,128)S(1)}) custom-call(s32[3]{0:T(128)S(1)} %pad_add_fusion.where, bf16[512,896]{1,0:T(8,128)(2,1)S(1)} %bitcast.43, bf16[768,1024]{1,0:T(8,128)(2,1)S(1)} %copy-done, ...), custom_call_target="tpu_custom_call" | custom-call | tf_op jit(solution)/shard_map/scores/pallas_call | solution.py:155
  39.3 13.1 %all_to_all.30.row_in = f32[16,1,512]{2,1,0:T(1,128)S(1)} all-to-all(f32[16,1,512]{2,1,0:T(1,128)S(1)} %broadcast_in_dim.24), channel_id=1, replica_groups=mesh['zh'=4,'y'=4,'x'=4,'zl'=2,'c'=2] {'y','x'}, dimensions={0} | all-to-all | bytes 65536 | tf_op jit(solution)/shard_map/all_to_all | solution.py:30
  52.4 14.3 %all_to_all.31.col_in = f32[16,1,512]{2,1,0:T(1,128)S(1)} all-to-all(f32[16,1,512]{2,1,0:T(1,128)S(1)} %broadcast_in_dim.26), channel_id=1, replica_groups=mesh['zh'=4,'y'=4,'x'=4,'zl'=2,'c'=2] {'zh','zl','c'}, dimensions={0} | all-to-all | bytes 65536 | tf_op jit(solution)/shard_map/all_to_all | solution.py:30
  66.7 2.4 %weights.1 = (bf16[512,1024]{1,0:T(8,128)(2,1)}, f32[1,512]{1,0:T(1,128)S(1)}, f32[1,512]{1,0:T(1,128)S(1)}) custom-call(s32[3]{0:T(128)S(1)} %pad_add_fusion.where, bf16[512,896]{1,0:T(8,128)(2,1)S(1)} %bitcast.44, f32[512,512]{1,0:T(8,128)S(1)} %get-tuple-element.12.expo, bf16[512,1024]{1,0:T(8,128)(2,1)S(1)} %get-tuple-element.13.teach, ...), custom_call_target="tpu_custom_call" | custom-call | tf_op jit(solution)/shard_map/weights/pallas_call | solution.py:171
  69.1 4.5 %all-to-all-start.3 = ((bf16[16,32,1024]{2,1,0:T(8,128)(2,1)}), bf16[16,32,1024]{2,1,0:T(8,128)(2,1)}, u32[]{:S(2)}, u32[]{:S(2)}) async-start(bf16[16,32,1024]{2,1,0:T(8,128)(2,1)} %bitcast.14), calls=%async_computation.3 | async-start | bytes 2097152 | tf_op jit(solution)/shard_map/all_to_all | solution.py:30
  73.6 0.0 copy-done.4
  73.6 0.0 copy-start.2
  73.6 0.5 multiply_reduce_fusion.1
  74.1 0.6 reduce_sum.144
  75.4 0.6 log_reduce_fusion
  77.3 13.2 %all-to-all-done.3 = bf16[16,32,1024]{2,1,0:T(8,128)(2,1)} async-done(((bf16[16,32,1024]{2,1,0:T(8,128)(2,1)}), bf16[16,32,1024]{2,1,0:T(8,128)(2,1)}, u32[]{:S(2)}, u32[]{:S(2)}) %all-to-all-start.3) | async-done | bytes 1048608 | tf_op jit(solution)/shard_map/all_to_all | solution.py:30
  90.5 1.4 %convert_reduce_fusion.1 = f32[32,1024]{1,0:T(8,128)S(1)} fusion(bf16[16,32,1024]{2,1,0:T(8,128)(2,1)} %all-to-all-done.3), kind=kLoop, calls=%fused_computation.1 | loop fusion | flops 1015808 | bytes 1179648 | tf_op jit(solution)/shard_map/reduce_sum | solution.py:186
  91.9 0.2 multiply_reduce_fusion
  92.1 0.1 divide_convert_fusion
  92.2 0.0 copy-done.2
  92.2 0.7 multiply_reduce_fusion.2
  93.0 0.1 pad_maximum_fusion.3
  93.1 0.7 pad_maximum_fusion
  93.9 4.2 %all-to-all-start.4 = ((bf16[16,40,256]{2,1,0:T(8,128)(2,1)}), bf16[16,40,256]{2,1,0:T(8,128)(2,1)S(1)}, u32[]{:S(2)}, u32[]{:S(2)}) async-start(bf16[16,40,256]{2,1,0:T(8,128)(2,1)} %pad_maximum_fusion), calls=%async_computation.4 | async-start | bytes 655360 | tf_op jit(solution)/shard_map/all_to_all | solution.py:30
  98.1 0.1 slice.28
  98.2 0.3 copy.22
  98.5 7.9 %all-to-all-done.4 = bf16[16,40,256]{2,1,0:T(8,128)(2,1)S(1)} async-done(((bf16[16,40,256]{2,1,0:T(8,128)(2,1)}), bf16[16,40,256]{2,1,0:T(8,128)(2,1)S(1)}, u32[]{:S(2)}, u32[]{:S(2)}) %all-to-all-start.4) | async-done | bytes 327712 | tf_op jit(solution)/shard_map/all_to_all | solution.py:30
  106.4 0.1 copy.24
  106.7 0.1 reshape.95
  106.7 0.3 convolution_convert_fusion
  107.1 0.8 pad_maximum_fusion.1
  107.9 5.4 %all-to-all-start.5 = ((bf16[16,48,128]{2,1,0:T(8,128)(2,1)}), bf16[16,48,128]{2,1,0:T(8,128)(2,1)S(1)}, u32[]{:S(2)}, u32[]{:S(2)}) async-start(bf16[16,48,128]{2,1,0:T(8,128)(2,1)} %pad_maximum_fusion.1), calls=%async_computation.5 | async-start | bytes 393216 | tf_op jit(solution)/shard_map/all_to_all | solution.py:30
  113.2 0.1 multiply_convert_fusion
  113.3 10.3 %all-to-all-done.5 = bf16[16,48,128]{2,1,0:T(8,128)(2,1)S(1)} async-done(((bf16[16,48,128]{2,1,0:T(8,128)(2,1)}), bf16[16,48,128]{2,1,0:T(8,128)(2,1)S(1)}, u32[]{:S(2)}, u32[]{:S(2)}) %all-to-all-start.5) | async-done | bytes 196640 | tf_op jit(solution)/shard_map/all_to_all | solution.py:30
  123.6 0.0 copy-start.5
  123.7 0.1 slice.31
  123.7 0.1 reshape.96
  123.8 0.0 copy-start.7
  123.8 0.5 slice.25
  125.0 1.3 broadcast_in_dim.32
  126.3 0.0 copy-done.5
  (37 shorter events, 0.4 us)
Async XLA Ops:
  0.6 12.4 %copy-start.6 = (f32[768]{0:T(1024)S(1)}, f32[768]{0:T(1024)}, u32[]{:S(2)}) copy-start(f32[768]{0:T(1024)} %param.7) | copy-start | bytes 9220
  0.6 12.5 %copy-start.8 = (s32[32]{0:T(128)S(1)}, s32[32]{0:T(128)}, u32[]{:S(2)}) copy-start(s32[32]{0:T(128)} %param.9) | copy-start | bytes 388
  2.6 10.6 %collective-permute-start = (bf16[32,1024]{1,0:T(8,128)(2,1)S(1)}, bf16[32,1024]{1,0:T(8,128)(2,1)S(1)}, u32[]{:S(2)}, u32[]{:S(2)}) collective-permute-start(bf16[32,1024]{1,0:T(8,128)(2,1)S(1)} %fusion.3), channel_id=1, source_target_pairs={{0,1},{1,0},{2,3},{3,2},{4,5},{5,4},{6,7},{7,6},{8,9},{9,8},{10,11... | collective-permute-start | bytes 196616 | tf_op jit(solution)/shard_map/ppermute | solution.py:43
  5.9 24.0 %collective-permute-start.4 = (bf16[32,1024]{1,0:T(8,128)(2,1)S(1)}, bf16[32,1024]{1,0:T(8,128)(2,1)S(1)}, u32[]{:S(2)}, u32[]{:S(2)}) collective-permute-start(bf16[32,1024]{1,0:T(8,128)(2,1)S(1)} %fusion.3), channel_id=1, source_target_pairs={{0,128},{1,129},{2,130},{3,131},{64,192},{65,193},{66,194},{67,195... | collective-permute-start | bytes 196616 | tf_op jit(solution)/shard_map/ppermute | solution.py:50
  12.9 1.5 %copy-start.1 = (f32[32,768]{1,0:T(8,128)}, f32[32,768]{1,0:T(8,128)S(1)}, u32[]{:S(2)}) copy-start(f32[32,768]{1,0:T(8,128)S(1)} %convert_reduce_fusion) | copy-start | bytes 294916
  13.1 1.3 %copy-start.3 = (bf16[32,768]{1,0:T(8,128)(2,1)}, bf16[32,768]{1,0:T(8,128)(2,1)S(1)}, u32[]{:S(2)}) copy-start(bf16[32,768]{1,0:T(8,128)(2,1)S(1)} %multiply_convert_fusion.1) | copy-start | bytes 147460
  13.2 12.9 %collective-permute-start.1 = (bf16[64,1024]{1,0:T(8,128)(2,1)S(1)}, bf16[64,1024]{1,0:T(8,128)(2,1)S(1)}, u32[]{:S(2)}, u32[]{:S(2)}) collective-permute-start(bf16[64,1024]{1,0:T(8,128)(2,1)S(1)} %pad_maximum_fusion.2.chip), channel_id=1, source_target_pairs={{0,2},{1,195},{2,64},{3,1},{64,66},{65,3},{66,128},{67,65},{128,13... | collective-permute-start | bytes 393224 | tf_op jit(solution)/shard_map/ppermute | solution.py:50
  13.4 12.7 %collective-permute-start.2 = (bf16[64,1024]{1,0:T(8,128)(2,1)S(1)}, bf16[64,1024]{1,0:T(8,128)(2,1)S(1)}, u32[]{:S(2)}, u32[]{:S(2)}) collective-permute-start(bf16[64,1024]{1,0:T(8,128)(2,1)S(1)} %pad_maximum_fusion.2.chip), channel_id=1, source_target_pairs={{0,64},{1,193},{2,66},{3,195},{64,128},{65,1},{66,130},{67,3},{128... | collective-permute-start | bytes 393224 | tf_op jit(solution)/shard_map/ppermute | solution.py:50
  14.4 21.1 %copy-start = (bf16[768,1024]{1,0:T(8,128)(2,1)S(1)}, bf16[768,1024]{1,0:T(8,128)(2,1)}, u32[]{:S(2)}) copy-start(bf16[768,1024]{1,0:T(8,128)(2,1)} %head.1) | copy-start | bytes 4718596
  14.4 21.1 %all-to-all-start = ((bf16[16,32,896]{2,1,0:T(8,128)(2,1)}), bf16[16,32,896]{2,1,0:T(8,128)(2,1)S(1)}, u32[]{:S(2)}, u32[]{:S(2)}) async-start(bf16[16,32,896]{2,1,0:T(8,128)(2,1)} %broadcast_in_dim.22), calls=%async_computation | async-start | bytes 1835008 | tf_op jit(solution)/shard_map/all_to_all | solution.py:30
  21.3 8.5 %collective-permute-start.3 = (bf16[64,1024]{1,0:T(8,128)(2,1)S(1)}, bf16[64,1024]{1,0:T(8,128)(2,1)S(1)}, u32[]{:S(2)}, u32[]{:S(2)}) collective-permute-start(bf16[64,1024]{1,0:T(8,128)(2,1)S(1)} %pad_maximum_fusion.2.chip), channel_id=1, source_target_pairs={{0,66},{1,131},{2,128},{3,193},{64,130},{65,195},{66,192},{67,1},{... | collective-permute-start | bytes 393224 | tf_op jit(solution)/shard_map/ppermute | solution.py:50
  29.9 5.7 %collective-permute-start.5 = (bf16[224,1024]{1,0:T(8,128)(2,1)S(1)}, bf16[224,1024]{1,0:T(8,128)(2,1)S(1)}, u32[]{:S(2)}, u32[]{:S(2)}) collective-permute-start(bf16[224,1024]{1,0:T(8,128)(2,1)S(1)} %constant_dynamic-update-slice_fusion.near), channel_id=1, source_target_pairs={{0,1},{1,0},{2,3},{3,2},{4,5},{5,4},{6,7},{7,6},{8,9},{9,8},{10,11... | collective-permute-start | bytes 1376264 | tf_op jit(solution)/shard_map/ppermute | solution.py:43
  69.1 4.5 %copy-start.4 = (bf16[32,768]{1,0:T(8,128)(2,1)S(1)}, bf16[32,768]{1,0:T(8,128)(2,1)}, u32[]{:S(2)}) copy-start(bf16[32,768]{1,0:T(8,128)(2,1)} %copy-done.3) | copy-start | bytes 147460
  69.1 21.4 %all-to-all-start.3 = ((bf16[16,32,1024]{2,1,0:T(8,128)(2,1)}), bf16[16,32,1024]{2,1,0:T(8,128)(2,1)}, u32[]{:S(2)}, u32[]{:S(2)}) async-start(bf16[16,32,1024]{2,1,0:T(8,128)(2,1)} %bitcast.14), calls=%async_computation.3 | async-start | bytes 2097152 | tf_op jit(solution)/shard_map/all_to_all | solution.py:30
  73.6 18.6 %copy-start.2 = (f32[32,768]{1,0:T(8,128)S(1)}, f32[32,768]{1,0:T(8,128)}, u32[]{:S(2)}) copy-start(f32[32,768]{1,0:T(8,128)} %copy-done.1) | copy-start | bytes 294916
  93.9 12.5 %all-to-all-start.4 = ((bf16[16,40,256]{2,1,0:T(8,128)(2,1)}), bf16[16,40,256]{2,1,0:T(8,128)(2,1)S(1)}, u32[]{:S(2)}, u32[]{:S(2)}) async-start(bf16[16,40,256]{2,1,0:T(8,128)(2,1)} %pad_maximum_fusion), calls=%async_computation.4 | async-start | bytes 655360 | tf_op jit(solution)/shard_map/all_to_all | solution.py:30
  107.9 15.7 %all-to-all-start.5 = ((bf16[16,48,128]{2,1,0:T(8,128)(2,1)}), bf16[16,48,128]{2,1,0:T(8,128)(2,1)S(1)}, u32[]{:S(2)}, u32[]{:S(2)}) async-start(bf16[16,48,128]{2,1,0:T(8,128)(2,1)} %pad_maximum_fusion.1), calls=%async_computation.5 | async-start | bytes 393216 | tf_op jit(solution)/shard_map/all_to_all | solution.py:30
  123.6 2.6 %copy-start.5 = (f32[48,128]{1,0:T(8,128)}, f32[48,128]{1,0:T(8,128)S(1)}, u32[]{:S(2)}) copy-start(f32[48,128]{1,0:T(8,128)S(1)} %convert_reduce_fusion.2) | copy-start | bytes 73732
  123.8 2.4 %copy-start.7 = (f32[1024]{0:T(1024)}, f32[1024]{0:T(1024)S(1)}, u32[]{:S(2)}) copy-start(f32[1024]{0:T(1024)S(1)} %reduce_sum.148) | copy-start | bytes 12292

commit v3 on v1

v3 whole, which is shorter than its diff:
```python
import jax
import jax.numpy as jnp
from jax import lax
from jax.experimental import pallas as pl
from jax.experimental.pallas import tpu as pltpu
from jax.sharding import Mesh, PartitionSpec as P

logit_scale = 64.0
norm_eps = 1e-06

AXES = ("zh", "y", "x", "zl", "c")
ROW = ("x", "zl")
CHIPS = ("zh", "y")

D, E, OWN, WIN = 768, 1024, 32, 32
NROW, NCHIP, NCOL = 8, 16, 32
SIDE = NROW * OWN
HALF = NCHIP * OWN
MARK = 128
CHUNK = 128
f32, b16 = jnp.float32, jnp.bfloat16
VMEM = pl.BlockSpec(memory_space=pltpu.VMEM)
SMEM = pl.BlockSpec(memory_space=pltpu.SMEM)
ANY = pl.BlockSpec(memory_space=pl.ANY)
PARAMS = pltpu.CompilerParams(vmem_limit_bytes=32 << 20)


def shaped(*shape, dtype=f32):
    return jax.ShapeDtypeStruct(shape, dtype)


def unit_rows(raw):
    length = jnp.sqrt(jnp.sum(raw * raw, axis=-1, keepdims=True) + norm_eps)
    return (raw / length, length)


def swap(blocks, axes):
    return lax.all_to_all(blocks, axes, 0, 0, tiled=True)


def spread(block, axes):
    peers = lax.axis_size(axes)
    return swap(jnp.broadcast_to(block[None], (peers,) + block.shape), axes)


def other(block, axis):
    return lax.ppermute(block, axis, [(0, 1), (1, 0)])


def along_x(block, step):
    return lax.ppermute(block, "x", [(i, (i + step) % 4) for i in range(4)])


def halves(value):
    high = value.astype(b16)
    return high, (value - high.astype(f32)).astype(b16)


def product(left, right, left_dim, right_dim):
    dims = (((left_dim,), (right_dim,)), ((), ()))
    return lax.dot_general(left, right, dims, preferred_element_type=f32)


def teacher_kernel(teacher, out):
    out[...] = unit_rows(teacher[...].astype(f32))[0].astype(b16)


def student_kernel(where, mine, pair, one, two, three, head, rows, student):
    x, zl = where[0], where[1]

    def put(ref, start, xx, zz):
        slot = pl.multiple_of((((xx + 4) & 3) * 2 + zz) * OWN, OWN)
        rows[pl.ds(slot, OWN), :] = ref[start : start + OWN, :]

    put(mine, 0, x, zl)
    put(pair, 0, x, 1 - zl)
    for k, ref in ((1, one), (2, two), (3, three)):
        put(ref, 0, x - k, zl)
        put(ref, OWN, x - k, 1 - zl)
    for n in range(SIDE // CHUNK):
        at = slice(n * CHUNK, (n + 1) * CHUNK)
        raw = jnp.dot(rows[at, :D], head[...], preferred_element_type=f32)
        student[at, :] = unit_rows(raw)[0].astype(b16)


def wanted_mask(marks, where, core):
    marks = marks.astype(f32)
    wanted = marks[:, 0:1] * 128.0 + marks[:, 1:2]
    place = lax.broadcasted_iota(jnp.int32, (1, HALF), 1)
    ids = (place >> 7) * 512 + ((place >> 5) & 3) * 2048 + (place & 31)
    ids = ids + where[0] * 128 + where[1] * 64 + core * 32
    return wanted == ids.astype(f32)


def scores_kernel(where, student, rows, mine, pair, expo, row_part, col_part, pos_part):
    core = where[2]
    for part, (ref, cc) in enumerate(((mine, core), (pair, 1 - core))):
        col = jnp.zeros((1, HALF), f32)
        pos = jnp.zeros((1, HALF), f32)
        for n in range(SIDE // CHUNK):
            at = slice(n * CHUNK, (n + 1) * CHUNK)
            scores = logit_scale * product(student[at, :], ref[...], 1, 1)
            mask = wanted_mask(rows[at, D:], where, cc)
            pos = pos + jnp.sum(jnp.where(mask, scores, 0.0), axis=0, keepdims=True)
            e = jnp.exp(scores)
            expo[at, part * HALF : (part + 1) * HALF] = e
            col = col + jnp.sum(e, axis=0, keepdims=True)
            lanes = sum(e[:, k : k + 128] for k in range(0, HALF, 128))
            if part == 0:
                row_part[at, :] = lanes
            else:
                row_part[at, :] += lanes
        col_part[:, pl.ds(pl.multiple_of(cc * HALF, HALF), HALF)] = col
        pos_part[:, part * HALF : (part + 1) * HALF] = pos


def plain_kernel(expo, row_part, mine, pair, terms):
    for n in range(SIDE // CHUNK):
        at = slice(n * CHUNK, (n + 1) * CHUNK)
        left = expo[at, :].astype(b16)
        out = product(left[:, :HALF], mine[...], 1, 0) + product(left[:, HALF:], pair[...], 1, 0)
        terms[at, :E] = out.astype(b16)
        high, low = halves(jnp.sum(row_part[at, :], axis=1, keepdims=True))
        lane = lax.broadcasted_iota(jnp.int32, (CHUNK, MARK), 1)
        high, low = high.astype(f32), low.astype(f32)
        terms[at, 2 * E :] = jnp.where(lane < 64, high, low).astype(b16)


def scaled_kernel(where, rows, expo, mine, pair, col_in, pos_part, _, terms, tail, sums):
    core = where[2]
    cols = jnp.sum(col_in[...], axis=0)
    sums[...] = cols
    tail[...] = jnp.log(cols) * (1.0 / NCOL) - 2.0 * pos_part[...]
    for n in range(SIDE // CHUNK):
        at = slice(n * CHUNK, (n + 1) * CHUNK)
        out = jnp.zeros((CHUNK, E), f32)
        for part, (ref, cc) in enumerate(((mine, core), (pair, 1 - core))):
            inv = 1.0 / sums[:, pl.ds(pl.multiple_of(cc * HALF, HALF), HALF)]
            mask = wanted_mask(rows[at, D:], where, cc)
            e = expo[at, part * HALF : (part + 1) * HALF]
            weights = (e * inv - jnp.where(mask, 2.0, 0.0)).astype(b16)
            out = out + product(weights, ref[...], 1, 0)
        terms[at, E : 2 * E] = out.astype(b16)


def rows_kernel(terms, unit, length, scaled, radius, gain, head, tail, sent, pooled_grad):
    plain = jnp.zeros((OWN, E), f32)
    weighted = jnp.zeros((OWN, E), f32)
    sums = jnp.zeros((OWN, MARK), f32)
    for s in range(NROW):
        plain = plain + terms[s, :, :E].astype(f32)
        weighted = weighted + terms[s, :, E : 2 * E].astype(f32)
        sums = sums + terms[s, :, 2 * E :].astype(f32)
    row_sums = sums[:, 0:1] + sums[:, 64:65]
    unit_ = unit[...]
    grad_unit = logit_scale * (plain / row_sums + weighted)
    along = jnp.sum(unit_ * grad_unit, axis=-1, keepdims=True)
    grad_raw = ((grad_unit - unit_ * along) / length[...]).astype(b16)
    grad_normed = product(grad_raw, head[...], 1, 1)
    scaled_ = scaled[...]
    gain_part = jnp.sum(grad_normed * scaled_, axis=0, keepdims=True)
    loss = jnp.sum(jnp.log(row_sums), axis=0, keepdims=True)
    loss = loss + jnp.sum(tail[...], axis=1, keepdims=True)
    pieces = [gain_part[:, k * 128 : (k + 1) * 128] for k in range(D // 128)]
    pieces += [jnp.broadcast_to(loss, (1, 128)), jnp.zeros((1, 128), f32)]
    extra = jnp.concatenate(halves(jnp.concatenate(pieces, axis=0)), axis=0)
    for s in range(NROW):
        sent[s, :OWN, :] = grad_raw[:, s * 128 : (s + 1) * 128]
        sent[s, OWN:, :] = extra
    spread_gain = grad_normed * gain[...]
    inner = jnp.mean(spread_gain * scaled_, axis=-1, keepdims=True)
    grad = (spread_gain - scaled_ * inner) / radius[...]
    pooled_grad[...] = (grad / WIN).astype(b16)


def head_kernel(back, rows, sent):
    grad_raw = back[:, :OWN, :].reshape(SIDE, 128)
    head = product(rows[:, :D], grad_raw, 0, 0).astype(b16)
    extra = jnp.sum(back[:, OWN : OWN + 8, :].astype(f32), axis=0)
    extra = extra + jnp.sum(back[:, OWN + 8 :, :].astype(f32), axis=0)
    extra = jnp.concatenate(halves(extra), axis=0)
    for g in range(NCHIP):
        sent[g, :48, :] = head[g * 48 : (g + 1) * 48, :]
        sent[g, 48:, :] = extra


def last_kernel(back, _, out):
    total = jnp.sum(back[...].astype(f32), axis=0)
    out[:48, :] = total[:48]
    out[48:, :] = total[48:56] + total[56:]


def call(kernel, out, n_in, name, where=False, specs=None, **options):
    specs = specs or ([SMEM] if where else []) + [VMEM] * n_in
    return pl.pallas_call(
        kernel,
        out_shape=out,
        in_specs=specs,
        out_specs=[VMEM] * len(out) if isinstance(out, list) else VMEM,
        compiler_params=PARAMS,
        name=name,
        **options,
    )


def body(features, teacher, gain, w_head, positives):
    x, zl, c = (lax.axis_index(a) for a in ("x", "zl", "c"))
    where = jnp.stack([x, zl, c]).astype(jnp.int32)
    total = OWN * NROW * NCOL

    mine = call(teacher_kernel, shaped(OWN, E, dtype=b16), 1, "teacher")(teacher)
    mine = spread(mine, "zh").reshape(4 * OWN, E)
    mine = spread(mine, "y").reshape(HALF, E)
    pair = other(mine, "c")

    pooled = jnp.mean(features, axis=1, dtype=f32)
    radius = jnp.sqrt(jnp.mean(pooled * pooled, axis=-1, keepdims=True) + norm_eps)
    scaled = pooled / radius
    normed = (scaled * gain).astype(b16)
    marks = jnp.stack([positives // 128, positives % 128], axis=1).astype(b16)
    own = jnp.concatenate([normed, jnp.pad(marks, ((0, 0), (0, MARK - 2)))], axis=1)
    near = other(own, "zl")
    both = jnp.concatenate([own, near], axis=0)
    rows, student = call(
        student_kernel,
        [shaped(SIDE, D + MARK, dtype=b16), shaped(SIDE, E, dtype=b16)],
        6,
        "student",
        True,
    )(where, own, near, along_x(both, 1), along_x(both, 2), along_x(both, 3), w_head)
    raw = jnp.dot(normed, w_head, preferred_element_type=f32)
    unit, length = unit_rows(raw)

    expo, row_part, col_part, pos_part = call(
        scores_kernel,
        [shaped(SIDE, 2 * HALF), shaped(SIDE, 128), shaped(1, 2 * HALF), shaped(1, 2 * HALF)],
        4,
        "scores",
        True,
    )(where, student, rows, mine, pair)
    col_in = spread(col_part + other(col_part, "c"), CHIPS)
    message = shaped(SIDE, 2 * E + MARK, dtype=b16)
    terms = call(plain_kernel, message, 4, "plain")(expo, row_part, mine, pair)
    terms, tail, _ = call(
        scaled_kernel,
        [message, shaped(1, 2 * HALF), shaped(1, 2 * HALF)],
        7,
        "scaled",
        True,
        input_output_aliases={7: 0},
    )(where, rows, expo, mine, pair, col_in, pos_part, terms)

    terms = swap(terms.reshape(NROW, OWN, 2 * E + MARK), ROW)
    sent, pooled_grad = call(
        rows_kernel, [shaped(NROW, 48, 128, dtype=b16), shaped(OWN, D, dtype=b16)], 8, "rows"
    )(terms, unit, length, scaled, radius, gain[None], w_head, tail)
    grad_features = jnp.broadcast_to(pooled_grad[:, None, :], features.shape)

    back = swap(sent, ROW)
    sent = call(head_kernel, shaped(NCHIP, 64, 128, dtype=b16), 2, "head")(back, rows)
    back = swap(sent, CHIPS)
    last = call(last_kernel, shaped(56, 128), 2, "last", specs=[VMEM, ANY])(back, grad_features)
    last = last + other(last, "c")
    grad_head = lax.dynamic_slice(last, (0, c * 64), (48, 64))
    return (last[54, 0] / (2.0 * total), grad_features, grad_head, last[48:54].reshape(D))


def solution(mesh):
    fine = Mesh(mesh.devices.reshape(4, 4, 4, 2, 2), AXES)
    in_specs = (P(AXES, None, None), P(AXES, None), P(), P(), P(AXES))
    out_specs = (P(), P(AXES, None, None), P(("zh", "y"), ("x", "zl", "c")), P())
    return jax.shard_map(body, mesh=fine, in_specs=in_specs, out_specs=out_specs, check_vma=False)
```

time: 161 us -> 137 us (0.85)
  waiting for transfers between devices: 83.8 us -> 36.2 us
  blocking collectives: 9.2 us -> 41.9 us
  Pallas kernels: 0 us -> 11 us
  starting transfers between devices: 37.4 us -> 29 us
  matrix products: 8.27 us -> 0.48 us
  other arithmetic: 8.06 us -> 2.35 us
  local copies, waits for them, and re-layouts: 8.51 us -> 13 us
  between operations: 4.68 us -> 2.65 us
    all_to_all x6 -> x3, waiting for transfers between devices: 83.8 us -> 28.3 us  [swap(): return lax.all_to_all(blocks, axes, 0, 0, tiled=True)]
    all_to_all x1 -> x3, blocking collectives: 9.2 us -> 41.9 us  [swap(): return lax.all_to_all(blocks, axes, 0, 0, tiled=True)]
    all_to_all x6 -> x3, starting transfers between devices: 37.4 us -> 13.1 us  [swap(): return lax.all_to_all(blocks, axes, 0, 0, tiled=True)]
    ppermute x0 -> x7, starting transfers between devices: none -> 16 us  [the longest x4 11.1 us: other(): return lax.ppermute(block, axis, [(0, 1), (1, 0)])]
    pallas_call x0 -> x8, Pallas kernels: none -> 11 us  [the longest x1 2.82 us: body(): call(scores_kernel, [shaped(SIDE, 2 * HALF), shaped(SIDE, 128), shaped(1,...]
    unnamed x11 -> x30, local copies, waits for them, and re-layouts: 0.14 us -> 9.02 us
    ppermute x0 -> x7, waiting for transfers between devices: none -> 7.88 us  [the longest x4 4.04 us: other(): return lax.ppermute(block, axis, [(0, 1), (1, 0)])]
    dot_general x4 -> x0, matrix products: 7.74 us -> none  [the longest x1 3.63 us: body(): jnp.dot(students, columns.T, preferred_element_type=f32)]
  transfers between devices with their start and end apart: 6 -> 10, of which waited for: 6 -> 8; matrix products, arithmetic and copies ran while one was open for 2% -> 2% of each run, Pallas kernels for 0% -> 2%
where the time goes in v3:
time: 137 us
  blocking collectives  41.9 us (31%)
  waiting for transfers between devices  36.2 us (26%)
  starting transfers between devices  29 us (21%)
  local copies, waits for them, and re-layouts  13 us (9%)
  Pallas kernels  11 us (8%)
  between operations  2.65 us (2%)
  other arithmetic  2.35 us (2%)
    all_to_all x3, blocking collectives, swap(): return lax.all_to_all(blocks, axes, 0, 0, tiled=True)  41.9 us
    all_to_all x3, waiting for transfers between devices, swap(): return lax.all_to_all(blocks, axes, 0, 0, tiled=True)  28.3 us
    all_to_all x3, starting transfers between devices, swap(): return lax.all_to_all(blocks, axes, 0, 0, tiled=True)  13.1 us
    ppermute x4, starting transfers between devices, other(): return lax.ppermute(block, axis, [(0, 1), (1, 0)])  11.1 us
    unnamed x30, local copies, waits for them, and re-layouts  9.02 us
    ppermute x3, starting transfers between devices, along_x(): return lax.ppermute(block, 'x', [(i, (i + step) % 4) for i in range(4)])  4.89 us
    ppermute x4, waiting for transfers between devices, other(): return lax.ppermute(block, axis, [(0, 1), (1, 0)])  4.04 us
    ppermute x3, waiting for transfers between devices, along_x(): return lax.ppermute(block, 'x', [(i, (i + step) % 4) for i in range(4)])  3.84 us
  transfers between devices with their start and end apart: 10, of which 8 were waited for; matrix products, arithmetic and copies ran while one was open for 2% of the time, Pallas kernels for 2%

profile of v3, /device:TPU:1, one launch (start us, length us, event | category | flops | bytes accessed | tf_op | source)
XLA Modules:
  0.0 136.6 jit_solution(13798304439743644299)
XLA Ops:
  0.6 0.0 copy-start.10
  0.6 0.8 copy-done.10
  1.5 0.1 teacher.2
  1.6 17.9 %all_to_all.30 = bf16[4,32,1024]{2,1,0:T(8,128)(2,1)S(1)} all-to-all(bf16[4,32,1024]{2,1,0:T(8,128)(2,1)S(1)} %broadcast_in_dim.14), channel_id=1, replica_groups=mesh['zh'=4,'y'=4,'x'=4,'zl'=2,'c'=2] {'zh'}, dimensions={0} | all-to-all | bytes 524288 | tf_op jit(solution)/shard_map/all_to_all | solution.py:38
  19.5 1.1 broadcast_in_dim.16
  20.6 4.3 %all-to-all-start.1 = ((bf16[4,128,1024]{2,1,0:T(8,128)(2,1)}), bf16[4,128,1024]{2,1,0:T(8,128)(2,1)S(1)}, u32[]{:S(2)}, u32[]{:S(2)}) async-start(bf16[4,128,1024]{2,1,0:T(8,128)(2,1)} %broadcast_in_dim.16), calls=%async_computation.1 | async-start | bytes 2097152 | tf_op jit(solution)/shard_map/all_to_all | solution.py:38
  24.9 1.9 %convert_reduce_fusion = f32[32,768]{1,0:T(8,128)S(1)} fusion(bf16[32,32,768]{2,1,0:T(8,128)(2,1)} %param.5), kind=kLoop, calls=%fused_computation | loop fusion | flops 1548288 | bytes 1671168 | tf_op jit(solution)/shard_map/reduce_sum | solution.py:216
  26.8 0.0 copy-done.14
  26.8 9.6 %all-to-all-done.1 = bf16[4,128,1024]{2,1,0:T(8,128)(2,1)S(1)} async-done(((bf16[4,128,1024]{2,1,0:T(8,128)(2,1)}), bf16[4,128,1024]{2,1,0:T(8,128)(2,1)S(1)}, u32[]{:S(2)}, u32[]{:S(2)}) %all-to-all-start.1) | async-done | bytes 1048608 | tf_op jit(solution)/shard_map/all_to_all | solution.py:38
  36.5 4.5 %collective-permute-start.4 = (bf16[512,1024]{1,0:T(8,128)(2,1)S(1)}, bf16[512,1024]{1,0:T(8,128)(2,1)}, u32[]{:S(2)}, u32[]{:S(2)}) collective-permute-start(bf16[512,1024]{1,0:T(8,128)(2,1)S(1)} %bitcast.20), channel_id=1, source_target_pairs={{0,1},{1,0},{2,3},{3,2},{4,5},{5,4},{6,7},{7,6},{8,9},{9,8},{10,11... | collective-permute-start | bytes 3145736 | tf_op jit(solution)/shard_map/ppermute | solution.py:47
  41.0 0.1 copy.14
  41.1 0.1 multiply_reduce_fusion.1
  41.2 0.0 copy-done.13
  41.2 0.1 multiply_convert_fusion
  41.3 0.0 copy-start.11
  41.3 1.3 collective-permute-start
  42.6 2.4 %collective-permute-done.pair = bf16[32,896]{1,0:T(8,128)(2,1)S(1)} collective-permute-done((bf16[32,896]{1,0:T(8,128)(2,1)S(1)}, bf16[32,896]{1,0:T(8,128)(2,1)S(1)}, u32[]{:S(2)}, u32[]{:S(2)}) %collective-permute-start) | collective-permute-done | bytes 57376 | tf_op jit(solution)/shard_map/ppermute | solution.py:47
  45.0 1.3 collective-permute-start.1
  46.3 0.0 copy-done.11
  46.3 2.5 %collective-permute-start.2 = (bf16[64,896]{1,0:T(8,128)(2,1)S(1)}, bf16[64,896]{1,0:T(8,128)(2,1)S(1)}, u32[]{:S(2)}, u32[]{:S(2)}) collective-permute-start(bf16[64,896]{1,0:T(8,128)(2,1)S(1)} %pad_maximum_fusion), channel_id=1, source_target_pairs={{0,8},{4,12},{8,0},{12,4},{1,9},{5,13},{9,1},{13,5},{2,10},{6,14},... | collective-permute-start | bytes 344072 | tf_op jit(solution)/shard_map/ppermute | solution.py:51
  48.7 1.2 collective-permute-start.3
  49.9 0.1 pad_add_fusion.where
  50.0 0.0 collective-permute-done.1.one
  50.0 3.3 %collective-permute-done.2.two = bf16[64,896]{1,0:T(8,128)(2,1)S(1)} collective-permute-done((bf16[64,896]{1,0:T(8,128)(2,1)S(1)}, bf16[64,896]{1,0:T(8,128)(2,1)S(1)}, u32[]{:S(2)}, u32[]{:S(2)}) %collective-permute-start.2) | collective-permute-done | bytes 114720 | tf_op jit(solution)/shard_map/ppermute | solution.py:51
  53.3 0.5 collective-permute-done.3.three
  53.8 0.6 copy-done.8
  54.4 0.0 copy-done
  54.4 0.9 copy-done.9
  55.3 1.3 student.1
  56.6 0.0 collective-permute-done.4.pair
  56.6 2.8 %scores.1 = (f32[256,1024]{1,0:T(8,128)S(1)}, f32[256,128]{1,0:T(8,128)S(1)}, f32[1,1024]{1,0:T(1,128)S(1)}, f32[1,1024]{1,0:T(1,128)S(1)}) custom-call(s32[3]{0:T(128)S(1)} %pad_add_fusion.where, bf16[256,1024]{1,0:T(8,128)(2,1)S(1)} %get-tuple-element.15.student, bf16[256,896]{1,0:T(8,128)(2,1)S(1)} %get-tuple-element.14.rows, ...), custom_call_target="tpu_custom_call" | custom-call | tf_op jit(solution)/shard_map/scores/pallas_call | solution.py:234
  59.4 0.0 copy-start.5
  59.5 0.9 copy-done.5
  60.4 1.5 %collective-permute-start.5 = (f32[1,1024]{1,0:T(1,128)S(1)}, f32[1,1024]{1,0:T(1,128)S(1)}, u32[]{:S(2)}, u32[]{:S(2)}) collective-permute-start(f32[1,1024]{1,0:T(1,128)S(1)} %get-tuple-element.17), channel_id=1, source_target_pairs={{0,1},{1,0},{2,3},{3,2},{4,5},{5,4},{6,7},{7,6},{8,9},{9,8},{10,11... | collective-permute-start | bytes 12296 | tf_op jit(solution)/shard_map/ppermute | solution.py:47
  61.9 0.8 collective-permute-done.5
  62.7 0.7 broadcast_in_dim.18
  63.4 4.4 %all-to-all-start.2 = ((f32[16,1,1024]{2,1,0:T(1,128)}), f32[16,1,1024]{2,1,0:T(1,128)S(1)}, u32[]{:S(2)}, u32[]{:S(2)}) async-start(f32[16,1,1024]{2,1,0:T(1,128)} %broadcast_in_dim.18), calls=%async_computation.2 | async-start | bytes 131072 | tf_op jit(solution)/shard_map/all_to_all | solution.py:38
  67.8 0.0 copy-start.6
  67.8 1.2 copy-done.6
  69.0 2.0 %plain.1._ = bf16[256,2176]{1,0:T(8,128)(2,1)S(1)} custom-call(f32[256,1024]{1,0:T(8,128)S(1)} %copy-done.6, f32[256,128]{1,0:T(8,128)S(1)} %get-tuple-element.19.row_part, bf16[512,1024]{1,0:T(8,128)(2,1)S(1)} %bitcast.22, bf16[512,1024]{1,0:T(8,128)(2,1)} %collective-permute-done.4.pair), custom_call_target="tpu_custom_call" | custom-call | tf_op jit(solution)/shard_map/plain/pallas_call | solution.py:243
  70.9 0.0 copy-start.1
  71.0 1.0 copy-done.1
  71.9 4.8 %all-to-all-done.2.col_in = f32[16,1,1024]{2,1,0:T(1,128)S(1)} async-done(((f32[16,1,1024]{2,1,0:T(1,128)}), f32[16,1,1024]{2,1,0:T(1,128)S(1)}, u32[]{:S(2)}, u32[]{:S(2)}) %all-to-all-start.2) | async-done | bytes 65568 | tf_op jit(solution)/shard_map/all_to_all | solution.py:38
  76.7 1.2 copy-done.2
  78.0 1.2 copy-done.7
  79.2 2.4 %scaled.1 = (bf16[256,2176]{1,0:T(8,128)(2,1)S(1)}, f32[1,1024]{1,0:T(1,128)S(1)}, f32[1,1024]{1,0:T(1,128)}) custom-call(s32[3]{0:T(128)S(1)} %pad_add_fusion.where, bf16[256,896]{1,0:T(8,128)(2,1)S(1)} %get-tuple-element.14.rows, f32[256,1024]{1,0:T(8,128)S(1)} %copy-done.7, bf16[512,1024]{1,0:T(8,128)(2,1)S(1)} %bitcast.23, ...), custom_call_target="tpu_custom_call", output_to_operand_aliasing={{0}: (7, {})} | custom-call | tf_op jit(solution)/shard_map/scaled/pallas_call | solution.py:244
  81.6 1.0 copy-done.3
  82.6 4.4 %all-to-all-start.3 = ((bf16[8,32,2176]{2,1,0:T(8,128)(2,1)}), bf16[8,32,2176]{2,1,0:T(8,128)(2,1)}, u32[]{:S(2)}, u32[]{:S(2)}) async-start(bf16[8,32,2176]{2,1,0:T(8,128)(2,1)} %bitcast.24), calls=%async_computation.3 | async-start | bytes 2228224 | tf_op jit(solution)/shard_map/all_to_all | solution.py:38
  87.0 0.5 multiply_reduce_fusion
  87.5 0.1 copy.15.length
  87.6 0.1 copy.16.radius
  87.7 0.1 broadcast_divide_fusion.unit
  87.8 13.9 %all-to-all-done.3.terms = bf16[8,32,2176]{2,1,0:T(8,128)(2,1)} async-done(((bf16[8,32,2176]{2,1,0:T(8,128)(2,1)}), bf16[8,32,2176]{2,1,0:T(8,128)(2,1)}, u32[]{:S(2)}, u32[]{:S(2)}) %all-to-all-start.3) | async-done | bytes 1114144 | tf_op jit(solution)/shard_map/all_to_all | solution.py:38
  101.7 2.1 %rows.1 = (bf16[8,48,128]{2,1,0:T(8,128)(2,1)S(1)}, bf16[32,768]{1,0:T(8,128)(2,1)S(1)}) custom-call(bf16[8,32,2176]{2,1,0:T(8,128)(2,1)} %all-to-all-done.3.terms, f32[32,1024]{1,0:T(8,128)S(1)} %broadcast_divide_fusion.unit, f32[32,1]{1,0:T(8,128)S(1)} %copy.15.length, f32[32,768]{1,0:T(8,128)S(1)} %get-tuple-element.25.scaled, f32[32,1]{1,0:T(8,128)S(1)} %copy.16.radius, ...), custom_call_target="tpu_custom_call" | custom-call | tf_op jit(solution)/shard_map/rows/pallas_call | solution.py:254
  103.8 9.1 %all_to_all.31.back = bf16[8,48,128]{2,1,0:T(8,128)(2,1)S(1)} all-to-all(bf16[8,48,128]{2,1,0:T(8,128)(2,1)S(1)} %get-tuple-element.22), channel_id=1, replica_groups=mesh['zh'=4,'y'=4,'x'=4,'zl'=2,'c'=2] {'x','zl'}, dimensions={0} | all-to-all | bytes 196608 | tf_op jit(solution)/shard_map/all_to_all | solution.py:38
  112.9 0.3 head.5
  113.2 14.9 %all_to_all.32.back = bf16[16,64,128]{2,1,0:T(8,128)(2,1)S(1)} all-to-all(bf16[16,64,128]{2,1,0:T(8,128)(2,1)S(1)} %head.5), channel_id=1, replica_groups=mesh['zh'=4,'y'=4,'x'=4,'zl'=2,'c'=2] {'zh','y'}, dimensions={0} | all-to-all | bytes 524288 | tf_op jit(solution)/shard_map/all_to_all | solution.py:38
  128.1 0.1 broadcast_in_dim.39._
  128.2 0.0 copy-start.4
  128.3 3.8 %collective-permute-start.6 = (f32[56,128]{1,0:T(8,128)S(1)}, f32[56,128]{1,0:T(8,128)S(1)}, u32[]{:S(2)}, u32[]{:S(2)}) collective-permute-start(f32[56,128]{1,0:T(8,128)S(1)} %last.1), channel_id=1, source_target_pairs={{0,1},{1,0},{2,3},{3,2},{4,5},{5,4},{6,7},{7,6},{8,9},{9,8},{10,11... | collective-permute-start | bytes 86024 | tf_op jit(solution)/shard_map/ppermute | solution.py:47
  132.1 0.9 collective-permute-done.6
  133.0 0.6 slice_bitcast_fusion
  133.6 0.5 slice.8
  134.1 0.7 constant_dynamic-slice_fusion
  (23 shorter events, 0.2 us)
Async XLA Ops:
  0.6 0.8 copy-start.10
  20.6 6.2 %copy-start.14 = (s32[32]{0:T(128)S(1)}, s32[32]{0:T(128)}, u32[]{:S(2)}) copy-start(s32[32]{0:T(128)} %param.9) | copy-start | bytes 388
  20.6 20.6 %copy-start.13 = (f32[768]{0:T(1024)S(1)}, f32[768]{0:T(1024)}, u32[]{:S(2)}) copy-start(f32[768]{0:T(1024)} %param.7) | copy-start | bytes 9220
  20.6 15.9 %all-to-all-start.1 = ((bf16[4,128,1024]{2,1,0:T(8,128)(2,1)}), bf16[4,128,1024]{2,1,0:T(8,128)(2,1)S(1)}, u32[]{:S(2)}, u32[]{:S(2)}) async-start(bf16[4,128,1024]{2,1,0:T(8,128)(2,1)} %broadcast_in_dim.16), calls=%async_computation.1 | async-start | bytes 2097152 | tf_op jit(solution)/shard_map/all_to_all | solution.py:38
  24.9 29.5 %copy-start = (bf16[768,1024]{1,0:T(8,128)(2,1)S(1)}, bf16[768,1024]{1,0:T(8,128)(2,1)}, u32[]{:S(2)}) copy-start(bf16[768,1024]{1,0:T(8,128)(2,1)} %head.4) | copy-start | bytes 4718596
  36.5 20.1 %collective-permute-start.4 = (bf16[512,1024]{1,0:T(8,128)(2,1)S(1)}, bf16[512,1024]{1,0:T(8,128)(2,1)}, u32[]{:S(2)}, u32[]{:S(2)}) collective-permute-start(bf16[512,1024]{1,0:T(8,128)(2,1)S(1)} %bitcast.20), channel_id=1, source_target_pairs={{0,1},{1,0},{2,3},{3,2},{4,5},{5,4},{6,7},{7,6},{8,9},{9,8},{10,11... | collective-permute-start | bytes 3145736 | tf_op jit(solution)/shard_map/ppermute | solution.py:47
  41.3 5.0 %copy-start.11 = (bf16[32,768]{1,0:T(8,128)(2,1)}, bf16[32,768]{1,0:T(8,128)(2,1)S(1)}, u32[]{:S(2)}) copy-start(bf16[32,768]{1,0:T(8,128)(2,1)S(1)} %get-tuple-element.24) | copy-start | bytes 147460
  41.3 3.6 %collective-permute-start = (bf16[32,896]{1,0:T(8,128)(2,1)S(1)}, bf16[32,896]{1,0:T(8,128)(2,1)S(1)}, u32[]{:S(2)}, u32[]{:S(2)}) collective-permute-start(bf16[32,896]{1,0:T(8,128)(2,1)S(1)} %pad_maximum_fusion.1.mine), channel_id=1, source_target_pairs={{0,2},{2,0},{1,3},{3,1},{4,6},{6,4},{5,7},{7,5},{8,10},{10,8},{9,1... | collective-permute-start | bytes 172040 | tf_op jit(solution)/shard_map/ppermute | solution.py:47
  45.0 5.0 %collective-permute-start.1 = (bf16[64,896]{1,0:T(8,128)(2,1)S(1)}, bf16[64,896]{1,0:T(8,128)(2,1)S(1)}, u32[]{:S(2)}, u32[]{:S(2)}) collective-permute-start(bf16[64,896]{1,0:T(8,128)(2,1)S(1)} %pad_maximum_fusion), channel_id=1, source_target_pairs={{0,4},{4,8},{8,12},{12,0},{1,5},{5,9},{9,13},{13,1},{2,6},{6,10},{... | collective-permute-start | bytes 344072 | tf_op jit(solution)/shard_map/ppermute | solution.py:51
  46.3 7.0 %collective-permute-start.2 = (bf16[64,896]{1,0:T(8,128)(2,1)S(1)}, bf16[64,896]{1,0:T(8,128)(2,1)S(1)}, u32[]{:S(2)}, u32[]{:S(2)}) collective-permute-start(bf16[64,896]{1,0:T(8,128)(2,1)S(1)} %pad_maximum_fusion), channel_id=1, source_target_pairs={{0,8},{4,12},{8,0},{12,4},{1,9},{5,13},{9,1},{13,5},{2,10},{6,14},... | collective-permute-start | bytes 344072 | tf_op jit(solution)/shard_map/ppermute | solution.py:51
  48.7 5.1 %collective-permute-start.3 = (bf16[64,896]{1,0:T(8,128)(2,1)S(1)}, bf16[64,896]{1,0:T(8,128)(2,1)S(1)}, u32[]{:S(2)}, u32[]{:S(2)}) collective-permute-start(bf16[64,896]{1,0:T(8,128)(2,1)S(1)} %pad_maximum_fusion), channel_id=1, source_target_pairs={{0,12},{4,0},{8,4},{12,8},{1,13},{5,1},{9,5},{13,9},{2,14},{6,2},{... | collective-permute-start | bytes 344072 | tf_op jit(solution)/shard_map/ppermute | solution.py:51
  53.8 0.6 copy-start.8
  54.4 0.9 copy-start.9
  59.4 1.0 copy-start.5
  60.4 2.3 %collective-permute-start.5 = (f32[1,1024]{1,0:T(1,128)S(1)}, f32[1,1024]{1,0:T(1,128)S(1)}, u32[]{:S(2)}, u32[]{:S(2)}) collective-permute-start(f32[1,1024]{1,0:T(1,128)S(1)} %get-tuple-element.17), channel_id=1, source_target_pairs={{0,1},{1,0},{2,3},{3,2},{4,5},{5,4},{6,7},{7,6},{8,9},{9,8},{10,11... | collective-permute-start | bytes 12296 | tf_op jit(solution)/shard_map/ppermute | solution.py:47
  63.4 13.3 %all-to-all-start.2 = ((f32[16,1,1024]{2,1,0:T(1,128)}), f32[16,1,1024]{2,1,0:T(1,128)S(1)}, u32[]{:S(2)}, u32[]{:S(2)}) async-start(f32[16,1,1024]{2,1,0:T(1,128)} %broadcast_in_dim.18), calls=%async_computation.2 | async-start | bytes 131072 | tf_op jit(solution)/shard_map/all_to_all | solution.py:38
  67.8 1.2 copy-start.6
  70.9 1.0 copy-start.1
  76.7 1.2 copy-start.2
  78.0 1.2 copy-start.7
  81.6 1.0 copy-start.3
  82.6 4.4 %copy-start.12 = (bf16[32,768]{1,0:T(8,128)(2,1)S(1)}, bf16[32,768]{1,0:T(8,128)(2,1)}, u32[]{:S(2)}) copy-start(bf16[32,768]{1,0:T(8,128)(2,1)} %copy-done.11) | copy-start | bytes 147460
  82.6 19.1 %all-to-all-start.3 = ((bf16[8,32,2176]{2,1,0:T(8,128)(2,1)}), bf16[8,32,2176]{2,1,0:T(8,128)(2,1)}, u32[]{:S(2)}, u32[]{:S(2)}) async-start(bf16[8,32,2176]{2,1,0:T(8,128)(2,1)} %bitcast.24), calls=%async_computation.3 | async-start | bytes 2228224 | tf_op jit(solution)/shard_map/all_to_all | solution.py:38
  128.2 7.2 %copy-start.4 = (bf16[32,32,768]{2,1,0:T(8,128)(2,1)}, bf16[32,32,768]{2,1,0:T(8,128)(2,1)S(1)}, u32[]{:S(2)}) copy-start(bf16[32,32,768]{2,1,0:T(8,128)(2,1)S(1)} %broadcast_in_dim.39._) | copy-start | bytes 4718596
  128.3 4.7 %collective-permute-start.6 = (f32[56,128]{1,0:T(8,128)S(1)}, f32[56,128]{1,0:T(8,128)S(1)}, u32[]{:S(2)}, u32[]{:S(2)}) collective-permute-start(f32[56,128]{1,0:T(8,128)S(1)} %last.1), channel_id=1, source_target_pairs={{0,1},{1,0},{2,3},{3,2},{4,5},{5,4},{6,7},{7,6},{8,9},{9,8},{10,11... | collective-permute-start | bytes 86024 | tf_op jit(solution)/shard_map/ppermute | solution.py:47

commit v4 on v3

v4 whole, which is shorter than its diff:
```python
import jax
import jax.numpy as jnp
from jax import lax
from jax.experimental import pallas as pl
from jax.experimental.pallas import tpu as pltpu
from jax.sharding import Mesh, PartitionSpec as P

logit_scale = 64.0
norm_eps = 1e-06

AXES = ("zh", "y", "x", "zl", "c")
ROW = ("x", "zl")
CHIPS = ("zh", "y")

D, E, OWN, WIN = 768, 1024, 32, 32
NROW, NCHIP, NCOL = 8, 16, 32
SIDE = NROW * OWN
HALF = NCHIP * OWN
MARK = 128
CHUNK = 128
BLOCK = 4 * OWN
f32, b16 = jnp.float32, jnp.bfloat16
SPACES = {
    "V": pl.BlockSpec(memory_space=pltpu.VMEM),
    "S": pl.BlockSpec(memory_space=pltpu.SMEM),
    "H": pl.BlockSpec(memory_space=pltpu.HBM),
    "A": pl.BlockSpec(memory_space=pl.ANY),
}
SMALL, SCORES = 12 << 20, 12 << 20


def shaped(*shape, dtype=f32):
    return jax.ShapeDtypeStruct(shape, dtype)


def unit_rows(raw):
    length = jnp.sqrt(jnp.sum(raw * raw, axis=-1, keepdims=True) + norm_eps)
    return (raw / length, length)


def swap(blocks, axes):
    return lax.all_to_all(blocks, axes, 0, 0, tiled=True)


def spread(block, axes):
    peers = lax.axis_size(axes)
    return swap(jnp.broadcast_to(block[None], (peers,) + block.shape), axes)


def other(block, axis):
    return lax.ppermute(block, axis, [(0, 1), (1, 0)])


def along(block, axis, step):
    return lax.ppermute(block, axis, [(i, (i + step) % 4) for i in range(4)])


def halves(value):
    high = value.astype(b16)
    return high, (value - high.astype(f32)).astype(b16)


def product(left, right, left_dim, right_dim):
    dims = (((left_dim,), (right_dim,)), ((), ()))
    return lax.dot_general(left, right, dims, preferred_element_type=f32)


def teacher_kernel(teacher, out):
    out[...] = unit_rows(teacher[...].astype(f32))[0].astype(b16)


def flat(gain):
    return jnp.concatenate([gain[k : k + 1, :] for k in range(D // 128)], axis=1)


def norm_kernel(features, places, gain, sent, scaled, radius):
    for n in range(0, OWN, 8):
        at = slice(n, n + 8)
        pooled = jnp.sum(features[at].astype(f32), axis=1) * (1.0 / WIN)
        size = jnp.sqrt(jnp.mean(pooled * pooled, axis=-1, keepdims=True) + norm_eps)
        radius[at, :] = size
        scaled[at, :] = pooled / size
    value = (scaled[...] * flat(gain)).astype(b16)
    place = places[...]
    lane = lax.broadcasted_iota(jnp.int32, place.shape, 1)
    marks = jnp.where(lane == 0, place >> 7, place & 127).astype(f32).astype(b16)
    for s in range(NROW):
        sent[s, :, :D] = value
        sent[s, :, D:] = marks


def position():
    return [lax.axis_index(a) for a in ("y", "x", "zl", "c", "zh")]


def student_kernel(rows, head, student, unit, length, full, sizes):
    raw = jnp.dot(rows[:, :D], head[...], preferred_element_type=f32)
    full[...], sizes[...] = unit_rows(raw)
    student[...] = full[...].astype(b16)
    where = position()
    own = pl.ds(pl.multiple_of((where[1] * 2 + where[2]) * OWN, OWN), OWN)
    unit[...] = full[own, :]
    length[...] = sizes[own, :]


def place(where, k):
    core = where[3] if k % 2 == 0 else 1 - where[3]
    y = (where[0] + (0, 3, 1, 2)[k // 2]) & 3
    return core, y


def wanted_mask(marks, where, k):
    core, y = place(where, k)
    marks = marks.astype(f32)
    wanted = marks[:, 0:1] * 128.0 + marks[:, 1:2]
    lane = lax.broadcasted_iota(jnp.int32, (1, BLOCK), 1)
    ids = (lane >> 5) * 2048 + (lane & 31) + y * 512 + where[1] * 128 + where[2] * 64 + core * 32
    return wanted == ids.astype(f32)


def fetch(where, sides, teach, sems):
    copies = []
    for k in range(8):
        for n in range(4):
            slot = pl.multiple_of(((where[4] + 4 - n) & 3) * OWN, OWN)
            here = sides[k % 2].at[pl.ds(k // 2 * BLOCK + n * OWN, OWN), :]
            there = teach.at[pl.ds(k * BLOCK + slot, OWN), :]
            copies.append(pltpu.make_async_copy(here, there, sems.at[4 * k + n]))
            copies[-1].start()
    return copies


def scores_kernel(student, rows, near, pair, teach, expo, terms, col_part, pos_part, sems):
    where = position()
    copies = fetch(where, (near, pair), teach, sems)
    lanes = [jnp.zeros((CHUNK, 128), f32) for _ in range(SIDE // CHUNK)]
    pos = jnp.zeros((1, BLOCK), f32)
    for k in range(0, 8, 2):
        for copy in copies[4 * k : 4 * k + 8]:
            copy.wait()
        both = product(student[...], teach[k * BLOCK : (k + 2) * BLOCK, :], 1, 1)
        for j in (k, k + 1):
            col = jnp.zeros((1, BLOCK), f32)
            for n in range(SIDE // CHUNK):
                at = slice(n * CHUNK, (n + 1) * CHUNK)
                value = logit_scale * both[at, (j - k) * BLOCK : (j - k + 1) * BLOCK]
                mask = wanted_mask(rows[at, D:], where, j)
                pos = pos + jnp.sum(jnp.where(mask, value, 0.0), axis=0, keepdims=True)
                e = jnp.exp(value)
                expo[at, j * BLOCK : (j + 1) * BLOCK] = e.astype(b16)
                col = col + jnp.sum(e, axis=0, keepdims=True)
                lanes[n] = lanes[n] + e
            core, y = place(where, j)
            col_part[pl.ds(core * 4 + y, 1), :] = col
    pos_part[...] = pos
    for n in range(SIDE // CHUNK):
        at = slice(n * CHUNK, (n + 1) * CHUNK)
        high, low = halves(jnp.sum(lanes[n], axis=1, keepdims=True))
        lane = lax.broadcasted_iota(jnp.int32, (CHUNK, MARK), 1)
        terms[at, E : E + MARK] = jnp.where(lane < 64, high.astype(f32), low.astype(f32)).astype(b16)
    terms[:, :E] = product(expo[...], teach[...], 1, 0).astype(b16)


def cols_kernel(mine, pair, sent):
    total = mine[...] + pair[...]
    for g in range(NCHIP):
        sent[g] = total


def scaled_kernel(rows, col_in, pos_part, expo, teach, _, terms, tail, weights, inv):
    where = position()
    cols = jnp.sum(col_in[...], axis=0)
    logs = jnp.sum(jnp.log(cols), axis=0, keepdims=True)
    tail[...] = logs * (1.0 / NCOL) - 2.0 * pos_part[...]
    inv[...] = 1.0 / cols
    for k in range(8):
        core, y = place(where, k)
        scale = inv[pl.ds(core * 4 + y, 1), :]
        at = slice(k * BLOCK, (k + 1) * BLOCK)
        mask = wanted_mask(rows[:, D:], where, k)
        value = expo[:, at].astype(f32) * scale - jnp.where(mask, 2.0, 0.0)
        weights[:, at] = value.astype(b16)
    terms[:, E + MARK :] = product(weights[...], teach[...], 1, 0).astype(b16)


def rows_kernel(terms, unit, length, scaled, radius, gain, head, tail, sent, pooled_grad):
    plain = jnp.zeros((OWN, E), f32)
    weighted = jnp.zeros((OWN, E), f32)
    sums = jnp.zeros((OWN, MARK), f32)
    for s in range(NROW):
        plain = plain + terms[s, :, :E].astype(f32)
        sums = sums + terms[s, :, E : E + MARK].astype(f32)
        weighted = weighted + terms[s, :, E + MARK :].astype(f32)
    row_sums = sums[:, 0:1] + sums[:, 64:65]
    unit_ = unit[...]
    grad_unit = logit_scale * (plain / row_sums + weighted)
    along = jnp.sum(unit_ * grad_unit, axis=-1, keepdims=True)
    grad_raw = ((grad_unit - unit_ * along) / length[...]).astype(b16)
    grad_normed = product(grad_raw, head[...], 1, 1)
    scaled_ = scaled[...]
    gain_part = jnp.sum(grad_normed * scaled_, axis=0, keepdims=True)
    loss = jnp.sum(jnp.log(row_sums), axis=0, keepdims=True)
    loss = loss + jnp.sum(tail[...], axis=1, keepdims=True)
    pieces = [gain_part[:, k * 128 : (k + 1) * 128] for k in range(D // 128)]
    pieces += [jnp.broadcast_to(loss, (1, 128)), jnp.zeros((1, 128), f32)]
    extra = jnp.concatenate(halves(jnp.concatenate(pieces, axis=0)), axis=0)
    for s in range(NROW):
        sent[s, :OWN, :] = grad_raw[:, s * 128 : (s + 1) * 128]
        sent[s, OWN:, :] = extra
    spread_gain = grad_normed * flat(gain)
    inner = jnp.mean(spread_gain * scaled_, axis=-1, keepdims=True)
    grad = (spread_gain - scaled_ * inner) / radius[...]
    pooled_grad[...] = (grad / WIN).astype(b16)


def head_kernel(back, rows, sent):
    grad_raw = back[:, :OWN, :].reshape(SIDE, 128)
    head = product(rows[:, :D], grad_raw, 0, 0).astype(b16)
    extra = jnp.sum(back[:, OWN : OWN + 8, :].astype(f32), axis=0)
    extra = extra + jnp.sum(back[:, OWN + 8 :, :].astype(f32), axis=0)
    extra = jnp.concatenate(halves(extra), axis=0)
    for g in range(NCHIP):
        sent[g, :48, :] = head[g * 48 : (g + 1) * 48, :]
        sent[g, 48:, :] = extra


def last_kernel(back, _, out):
    total = jnp.sum(back[...].astype(f32), axis=0)
    out[:48, :] = total[:48]
    out[48:, :] = total[48:56] + total[56:]


def out_kernel(mine, pair, head, gain, loss):
    total = mine[...] + pair[...]
    head[...] = jnp.where(position()[3] == 0, total[:48, :64], total[:48, 64:])
    gain[...] = total[48 : 48 + D // 128, :]
    loss[...] = total[54:55, :] * (1.0 / (2.0 * OWN * NROW * NCOL))


def call(kernel, out, ins, name, outs=None, limit=SMALL, **options):
    out_specs = [SPACES[k] for k in outs or "V" * (len(out) if isinstance(out, list) else 1)]
    return pl.pallas_call(
        kernel,
        out_shape=out,
        in_specs=[SPACES[k] for k in ins],
        out_specs=out_specs if isinstance(out, list) else out_specs[0],
        compiler_params=pltpu.CompilerParams(vmem_limit_bytes=limit),
        name=name,
        **options,
    )


def body(features, teacher, gain, w_head, positives):
    wide = 2 * HALF

    mine = call(teacher_kernel, shaped(OWN, E, dtype=b16), "V", "teacher")(teacher)
    mine = jnp.concatenate([mine] + [along(mine, "zh", k) for k in (1, 2, 3)], axis=0)

    places = jnp.broadcast_to(positives[:, None], (OWN, MARK))
    gain = gain.reshape(D // 128, 128)
    own, scaled, radius = call(
        norm_kernel,
        [
            shaped(NROW, OWN, D + MARK, dtype=b16),
            shaped(OWN, D),
            shaped(OWN, 1),
        ],
        "VVV",
        "norm",
    )(features, places, gain)

    mine, own = lax.optimization_barrier((mine, own))
    up, down = along(mine, "y", 1), along(mine, "y", 3)
    far = along(up, "y", 1)
    rows = swap(own, ROW).reshape(SIDE, D + MARK)
    student, unit, length = call(
        student_kernel,
        [shaped(SIDE, E, dtype=b16), shaped(OWN, E), shaped(OWN, 1)],
        "VV",
        "student",
        scratch_shapes=[pltpu.VMEM((SIDE, E), f32), pltpu.VMEM((SIDE, 1), f32)],
    )(rows, w_head)
    far, student = lax.optimization_barrier((far, student))
    near = jnp.concatenate([mine, up, down, far], axis=0)
    pair = other(near, "c")

    message = shaped(SIDE, 2 * E + MARK, dtype=b16)
    teach, expo, terms, col_part, pos_part = call(
        scores_kernel,
        [shaped(wide, E, dtype=b16), shaped(SIDE, wide, dtype=b16), message]
        + [shaped(8, 128), shaped(1, 128)],
        "VVAA",
        "scores",
        limit=SCORES,
        scratch_shapes=[pltpu.SemaphoreType.DMA((32,))],
    )(student, rows, near, pair)
    col_in = call(cols_kernel, shaped(NCHIP, 8, 128), "VV", "cols")(col_part, other(col_part, "c"))
    col_in = swap(col_in, CHIPS)
    terms, tail = call(
        scaled_kernel,
        [message, shaped(1, 128)],
        "VVVVVV",
        "scaled",
        input_output_aliases={5: 0},
        scratch_shapes=[pltpu.VMEM((SIDE, wide), b16), pltpu.VMEM((8, 128), f32)],
    )(rows, col_in, pos_part, expo, teach, terms)

    terms = swap(terms.reshape(NROW, OWN, 2 * E + MARK), ROW)
    sent, pooled_grad = call(
        rows_kernel,
        [shaped(NROW, 48, 128, dtype=b16), shaped(OWN, D, dtype=b16)],
        "V" * 8,
        "rows",
    )(terms, unit, length, scaled, radius, gain, w_head, tail)
    grad_features = jnp.broadcast_to(pooled_grad[:, None, :], features.shape)

    back = swap(sent, ROW)
    sent = call(head_kernel, shaped(NCHIP, 64, 128, dtype=b16), "VV", "head")(back, rows)
    back = swap(sent, CHIPS)
    last = call(last_kernel, shaped(56, 128), "VA", "last")(back, grad_features)
    grad_head, grad_gain, loss = call(
        out_kernel, [shaped(48, 64), shaped(D // 128, 128), shaped(1, 128)], "VV", "out"
    )(last, other(last, "c"))
    return (loss[0, 0], grad_features, grad_head, grad_gain.reshape(D))


def solution(mesh):
    fine = Mesh(mesh.devices.reshape(4, 4, 4, 2, 2), AXES)
    in_specs = (P(AXES, None, None), P(AXES, None), P(), P(), P(AXES))
    out_specs = (P(), P(AXES, None, None), P(("zh", "y"), ("x", "zl", "c")), P())
    return jax.shard_map(body, mesh=fine, in_specs=in_specs, out_specs=out_specs, check_vma=False)
```

time: 137 us -> 115 us (0.84)
  waiting for transfers between devices: 36.2 us -> 13.2 us
  blocking collectives: 41.9 us -> 55.4 us
  local copies, waits for them, and re-layouts: 13 us -> 5.76 us
  other arithmetic: 2.35 us -> 0.02 us
  between operations: 2.65 us -> 0.77 us
    all_to_all x3 -> x1, waiting for transfers between devices: 28.3 us -> 0.01 us  [swap(): return lax.all_to_all(blocks, axes, 0, 0, tiled=True)]
    all_to_all x3 -> x4, blocking collectives: 41.9 us -> 55.4 us  [swap(): return lax.all_to_all(blocks, axes, 0, 0, tiled=True)]
    all_to_all x3 -> x1, starting transfers between devices: 13.1 us -> 4.72 us  [swap(): return lax.all_to_all(blocks, axes, 0, 0, tiled=True)]
    ppermute x3 -> x6, starting transfers between devices: 4.89 us -> 13 us  [along(): return lax.ppermute(block, axis, [(i, (i + step) % 4) for i in range(4)])]
    ppermute x3 -> x6, waiting for transfers between devices: 3.84 us -> 9.24 us  [along(): return lax.ppermute(block, axis, [(i, (i + step) % 4) for i in range(4)])]
    unnamed x30 -> x15, local copies, waits for them, and re-layouts: 9.02 us -> 3.96 us
    reduce_sum x2 -> x0, other arithmetic: 2.03 us -> none  [the longest x1 1.91 us: body(): pooled = jnp.mean(features, axis=1, dtype=f32)]
    pallas_call x7 -> x9, Pallas kernels: 8.89 us -> 9.9 us  [the longest x1 5.53 us: body(): call(scores_kernel, [shaped(wide, E, dtype=b16), shaped(SIDE, wide, dtype...]
  transfers between devices with their start and end apart: 10 -> 10, of which waited for: 8 -> 6; matrix products, arithmetic and copies ran while one was open for 2% -> 2% of each run, Pallas kernels for 2% -> 2%
where the time goes in v4:
time: 115 us
  blocking collectives  55.4 us (48%)
  starting transfers between devices  28.6 us (25%)
  waiting for transfers between devices  13.2 us (11%)
  Pallas kernels  10.8 us (9%)
  local copies, waits for them, and re-layouts  5.76 us (5%)
    all_to_all x4, blocking collectives, swap(): return lax.all_to_all(blocks, axes, 0, 0, tiled=True)  55.4 us
    ppermute x6, starting transfers between devices, along(): return lax.ppermute(block, axis, [(i, (i + step) % 4) for i in range(4)])  13 us
    ppermute x3, starting transfers between devices, other(): return lax.ppermute(block, axis, [(0, 1), (1, 0)])  10.9 us
    ppermute x6, waiting for transfers between devices, along(): return lax.ppermute(block, axis, [(i, (i + step) % 4) for i in range(4)])  9.24 us
    pallas_call x1, Pallas kernels, body(): call(scores_kernel, [shaped(wide, E, dtype=b16), shaped(SIDE, wide, dtype...  5.53 us
    all_to_all x1, starting transfers between devices, swap(): return lax.all_to_all(blocks, axes, 0, 0, tiled=True)  4.72 us
    ppermute x3, waiting for transfers between devices, other(): return lax.ppermute(block, axis, [(0, 1), (1, 0)])  3.96 us
    unnamed x15, local copies, waits for them, and re-layouts  3.96 us
  transfers between devices with their start and end apart: 10, of which 6 were waited for; matrix products, arithmetic and copies ran while one was open for 2% of the time, Pallas kernels for 2%

profile of v4, /device:TPU:1, one launch (start us, length us, event | category | flops | bytes accessed | tf_op | source)
XLA Modules:
  0.0 114.6 jit_solution(6065109999848927962)
XLA Ops:
  0.6 0.0 copy-start.3
  0.6 0.8 copy-done.3
  1.5 0.1 teacher.2
  1.6 6.9 %collective-permute-start.2 = (bf16[32,1024]{1,0:T(8,128)(2,1)S(1)}, bf16[32,1024]{1,0:T(8,128)(2,1)S(1)}, u32[]{:S(2)}, u32[]{:S(2)}) collective-permute-start(bf16[32,1024]{1,0:T(8,128)(2,1)S(1)} %teacher.2), channel_id=1, source_target_pairs={{0,192},{64,0},{128,64},{192,128},{1,193},{65,1},{129,65},{193,129... | collective-permute-start | bytes 196616 | tf_op jit(solution)/shard_map/ppermute | solution.py:55
  8.5 1.0 collective-permute-start.1
  9.5 2.3 %collective-permute-start = (bf16[32,1024]{1,0:T(8,128)(2,1)S(1)}, bf16[32,1024]{1,0:T(8,128)(2,1)S(1)}, u32[]{:S(2)}, u32[]{:S(2)}) collective-permute-start(bf16[32,1024]{1,0:T(8,128)(2,1)S(1)} %teacher.2), channel_id=1, source_target_pairs={{0,64},{64,128},{128,192},{192,0},{1,65},{65,129},{129,193},{193,1... | collective-permute-start | bytes 196616 | tf_op jit(solution)/shard_map/ppermute | solution.py:55
  11.8 0.7 broadcast_in_dim.4.places
  12.5 0.0 copy-start.2
  12.5 1.4 %copy-done.2 = bf16[32,32,768]{2,1,0:T(8,128)(2,1)S(1)} copy-done((bf16[32,32,768]{2,1,0:T(8,128)(2,1)S(1)}, bf16[32,32,768]{2,1,0:T(8,128)(2,1)}, u32[]{:S(2)}) %copy-start.2) | copy-done | bytes 1572888
  13.9 0.0 copy-start.4
  13.9 0.7 copy-done.4
  14.6 1.3 %norm.1 = (bf16[8,32,896]{2,1,0:T(8,128)(2,1)}, f32[32,768]{1,0:T(8,128)S(1)}, f32[32,1]{1,0:T(8,128)S(1)}) custom-call(bf16[32,32,768]{2,1,0:T(8,128)(2,1)S(1)} %copy-done.2, s32[32,128]{1,0:T(8,128)S(1)} %broadcast_in_dim.4.places, f32[6,128]{1,0:T(8,128)S(1)} %bitcast.11), custom_call_target="tpu_custom_call" | custom-call | tf_op jit(solution)/shard_map/norm/pallas_call | solution.py:261
  15.9 0.0 copy-start.1
  15.9 0.0 collective-permute-done.2
  15.9 0.0 collective-permute-done.1
  15.9 0.5 collective-permute-done
  16.5 4.7 %all-to-all-start = ((bf16[8,32,896]{2,1,0:T(8,128)(2,1)}), bf16[8,32,896]{2,1,0:T(8,128)(2,1)S(1)}, u32[]{:S(2)}, u32[]{:S(2)}) async-start(bf16[8,32,896]{2,1,0:T(8,128)(2,1)} %get-tuple-element.27), calls=%async_computation | async-start | bytes 917504 | tf_op jit(solution)/shard_map/all_to_all | solution.py:42
  21.2 1.3 %collective-permute-start.3 = (bf16[128,1024]{1,0:T(8,128)(2,1)S(1)}, bf16[128,1024]{1,0:T(8,128)(2,1)}, u32[]{:S(2)}, u32[]{:S(2)}) collective-permute-start(bf16[128,1024]{1,0:T(8,128)(2,1)S(1)} %pad_maximum_fusion), channel_id=1, source_target_pairs={{0,16},{16,32},{32,48},{48,0},{1,17},{17,33},{33,49},{49,1},{2,18}... | collective-permute-start | bytes 786440 | tf_op jit(solution)/shard_map/ppermute | solution.py:55
  22.5 1.5 %collective-permute-start.5 = (bf16[128,1024]{1,0:T(8,128)(2,1)S(1)}, bf16[128,1024]{1,0:T(8,128)(2,1)S(1)}, u32[]{:S(2)}, u32[]{:S(2)}) collective-permute-start(bf16[128,1024]{1,0:T(8,128)(2,1)S(1)} %pad_maximum_fusion), channel_id=1, source_target_pairs={{0,48},{16,0},{32,16},{48,32},{1,49},{17,1},{33,17},{49,33},{2,50}... | collective-permute-start | bytes 786440 | tf_op jit(solution)/shard_map/ppermute | solution.py:55
  24.0 3.8 %collective-permute-done.3 = bf16[128,1024]{1,0:T(8,128)(2,1)} collective-permute-done((bf16[128,1024]{1,0:T(8,128)(2,1)S(1)}, bf16[128,1024]{1,0:T(8,128)(2,1)}, u32[]{:S(2)}, u32[]{:S(2)}) %collective-permute-start.3) | collective-permute-done | bytes 262176 | tf_op jit(solution)/shard_map/ppermute | solution.py:55
  27.8 0.0 collective-permute-start.4
  27.8 1.0 constant_dynamic-update-slice_fusion.2
  28.8 0.0 collective-permute-done.5
  28.9 0.0 all-to-all-done
  28.9 0.0 copy-done.1
  28.9 0.7 student.1
  29.6 4.9 %collective-permute-done.4 = bf16[128,1024]{1,0:T(8,128)(2,1)} collective-permute-done((bf16[128,1024]{1,0:T(8,128)(2,1)}, bf16[128,1024]{1,0:T(8,128)(2,1)}, u32[]{:S(2)}, u32[]{:S(2)}) %collective-permute-start.4) | collective-permute-done | bytes 262176 | tf_op jit(solution)/shard_map/ppermute | solution.py:55
  34.5 1.0 constant_dynamic-update-slice_fusion.near
  35.5 5.1 %collective-permute-start.6 = (bf16[512,1024]{1,0:T(8,128)(2,1)S(1)}, bf16[512,1024]{1,0:T(8,128)(2,1)S(1)}, u32[]{:S(2)}, u32[]{:S(2)}) collective-permute-start(bf16[512,1024]{1,0:T(8,128)(2,1)S(1)} %constant_dynamic-update-slice_fusion.near), channel_id=1, source_target_pairs={{0,1},{1,0},{2,3},{3,2},{4,5},{5,4},{6,7},{7,6},{8,9},{9,8},{10,11... | collective-permute-start | bytes 3145736 | tf_op jit(solution)/shard_map/ppermute | solution.py:51
  40.6 2.3 %collective-permute-done.6.pair = bf16[512,1024]{1,0:T(8,128)(2,1)S(1)} collective-permute-done((bf16[512,1024]{1,0:T(8,128)(2,1)S(1)}, bf16[512,1024]{1,0:T(8,128)(2,1)S(1)}, u32[]{:S(2)}, u32[]{:S(2)}) %collective-permute-start.6) | collective-permute-done | bytes 1048608 | tf_op jit(solution)/shard_map/ppermute | solution.py:51
  42.9 5.5 %scores.1 = (bf16[1024,1024]{1,0:T(8,128)(2,1)S(1)}, bf16[256,1024]{1,0:T(8,128)(2,1)S(1)}, bf16[256,2176]{1,0:T(8,128)(2,1)S(1)}, f32[8,128]{1,0:T(8,128)S(1)}, f32[1,128]{1,0:T(1,128)S(1)}) custom-call(bf16[256,1024]{1,0:T(8,128)(2,1)S(1)} %get-tuple-element.30.student, bf16[256,896]{1,0:T(8,128)(2,1)S(1)} %bitcast.7, ...), custom_call_target="tpu_custom_call" | custom-call | tf_op jit(solution)/shard_map/scores/pallas_call | solution.py:288
  48.5 0.5 collective-permute-start.7
  48.9 0.8 collective-permute-done.7.pair
  49.8 14.9 %all_to_all.25.col_in = f32[16,8,128]{2,1,0:T(8,128)S(1)} all-to-all(f32[16,8,128]{2,1,0:T(8,128)S(1)} %cols.1), channel_id=1, replica_groups=mesh['zh'=4,'y'=4,'x'=4,'zl'=2,'c'=2] {'zh','y'}, dimensions={0} | all-to-all | bytes 131072 | tf_op jit(solution)/shard_map/all_to_all | solution.py:42
  64.7 1.2 %scaled.1 = (bf16[256,2176]{1,0:T(8,128)(2,1)S(1)}, f32[1,128]{1,0:T(1,128)S(1)}) custom-call(bf16[256,896]{1,0:T(8,128)(2,1)S(1)} %bitcast.8, f32[16,8,128]{2,1,0:T(8,128)S(1)} %all_to_all.25.col_in, f32[1,128]{1,0:T(1,128)S(1)} %get-tuple-element.33.pos_part, bf16[256,1024]{1,0:T(8,128)(2,1)S(1)} %get-tuple-element.34.expo, ...), custom_call_target="tpu_custom_call", output_to_operand_aliasing={{0}: (5, {})} | custom-call | tf_op jit(solution)/shard_map/scaled/pallas_call | solution.py:299
  65.9 0.0 copy-start.5
  65.9 19.3 %all_to_all.26.terms = bf16[8,32,2176]{2,1,0:T(8,128)(2,1)S(1)} all-to-all(bf16[8,32,2176]{2,1,0:T(8,128)(2,1)S(1)} %bitcast.10), channel_id=1, replica_groups=mesh['zh'=4,'y'=4,'x'=4,'zl'=2,'c'=2] {'x','zl'}, dimensions={0} | all-to-all | bytes 2228224 | tf_op jit(solution)/shard_map/all_to_all | solution.py:42
  85.2 0.0 copy-done.5
  85.2 0.9 rows.1
  86.1 8.1 %all_to_all.27.back = bf16[8,48,128]{2,1,0:T(8,128)(2,1)S(1)} all-to-all(bf16[8,48,128]{2,1,0:T(8,128)(2,1)S(1)} %get-tuple-element.43), channel_id=1, replica_groups=mesh['zh'=4,'y'=4,'x'=4,'zl'=2,'c'=2] {'x','zl'}, dimensions={0} | all-to-all | bytes 196608 | tf_op jit(solution)/shard_map/all_to_all | solution.py:42
  94.2 0.3 head.5
  94.5 13.1 %all_to_all.28.back = bf16[16,64,128]{2,1,0:T(8,128)(2,1)S(1)} all-to-all(bf16[16,64,128]{2,1,0:T(8,128)(2,1)S(1)} %head.5), channel_id=1, replica_groups=mesh['zh'=4,'y'=4,'x'=4,'zl'=2,'c'=2] {'zh','y'}, dimensions={0} | all-to-all | bytes 524288 | tf_op jit(solution)/shard_map/all_to_all | solution.py:42
  107.6 0.1 broadcast_in_dim.5._
  107.7 0.0 copy-start
  107.8 5.3 %collective-permute-start.8 = (f32[56,128]{1,0:T(8,128)S(1)}, f32[56,128]{1,0:T(8,128)S(1)}, u32[]{:S(2)}, u32[]{:S(2)}) collective-permute-start(f32[56,128]{1,0:T(8,128)S(1)} %last.1.mine), channel_id=1, source_target_pairs={{0,1},{1,0},{2,3},{3,2},{4,5},{5,4},{6,7},{7,6},{8,9},{9,8},{10,11... | collective-permute-start | bytes 86024 | tf_op jit(solution)/shard_map/ppermute | solution.py:51
  113.0 0.9 collective-permute-done.8.pair
  113.9 0.7 out.1
  114.6 0.0 copy-done
  (5 shorter events, 0.1 us)
Async XLA Ops:
  0.6 0.8 copy-start.3
  1.6 14.3 %collective-permute-start.2 = (bf16[32,1024]{1,0:T(8,128)(2,1)S(1)}, bf16[32,1024]{1,0:T(8,128)(2,1)S(1)}, u32[]{:S(2)}, u32[]{:S(2)}) collective-permute-start(bf16[32,1024]{1,0:T(8,128)(2,1)S(1)} %teacher.2), channel_id=1, source_target_pairs={{0,192},{64,0},{128,64},{192,128},{1,193},{65,1},{129,65},{193,129... | collective-permute-start | bytes 196616 | tf_op jit(solution)/shard_map/ppermute | solution.py:55
  8.5 7.4 %collective-permute-start.1 = (bf16[32,1024]{1,0:T(8,128)(2,1)S(1)}, bf16[32,1024]{1,0:T(8,128)(2,1)S(1)}, u32[]{:S(2)}, u32[]{:S(2)}) collective-permute-start(bf16[32,1024]{1,0:T(8,128)(2,1)S(1)} %teacher.2), channel_id=1, source_target_pairs={{0,128},{64,192},{128,0},{192,64},{1,129},{65,193},{129,1},{193,65... | collective-permute-start | bytes 196616 | tf_op jit(solution)/shard_map/ppermute | solution.py:55
  9.5 6.9 %collective-permute-start = (bf16[32,1024]{1,0:T(8,128)(2,1)S(1)}, bf16[32,1024]{1,0:T(8,128)(2,1)S(1)}, u32[]{:S(2)}, u32[]{:S(2)}) collective-permute-start(bf16[32,1024]{1,0:T(8,128)(2,1)S(1)} %teacher.2), channel_id=1, source_target_pairs={{0,64},{64,128},{128,192},{192,0},{1,65},{65,129},{129,193},{193,1... | collective-permute-start | bytes 196616 | tf_op jit(solution)/shard_map/ppermute | solution.py:55
  12.5 1.4 %copy-start.2 = (bf16[32,32,768]{2,1,0:T(8,128)(2,1)S(1)}, bf16[32,32,768]{2,1,0:T(8,128)(2,1)}, u32[]{:S(2)}) copy-start(bf16[32,32,768]{2,1,0:T(8,128)(2,1)} %features.1) | copy-start | bytes 4718596
  13.9 0.7 copy-start.4
  15.9 13.0 %copy-start.1 = (bf16[768,1024]{1,0:T(8,128)(2,1)S(1)}, bf16[768,1024]{1,0:T(8,128)(2,1)}, u32[]{:S(2)}) copy-start(bf16[768,1024]{1,0:T(8,128)(2,1)} %head.4) | copy-start | bytes 4718596
  16.5 12.4 %all-to-all-start = ((bf16[8,32,896]{2,1,0:T(8,128)(2,1)}), bf16[8,32,896]{2,1,0:T(8,128)(2,1)S(1)}, u32[]{:S(2)}, u32[]{:S(2)}) async-start(bf16[8,32,896]{2,1,0:T(8,128)(2,1)} %get-tuple-element.27), calls=%async_computation | async-start | bytes 917504 | tf_op jit(solution)/shard_map/all_to_all | solution.py:42
  21.2 6.6 %collective-permute-start.3 = (bf16[128,1024]{1,0:T(8,128)(2,1)S(1)}, bf16[128,1024]{1,0:T(8,128)(2,1)}, u32[]{:S(2)}, u32[]{:S(2)}) collective-permute-start(bf16[128,1024]{1,0:T(8,128)(2,1)S(1)} %pad_maximum_fusion), channel_id=1, source_target_pairs={{0,16},{16,32},{32,48},{48,0},{1,17},{17,33},{33,49},{49,1},{2,18}... | collective-permute-start | bytes 786440 | tf_op jit(solution)/shard_map/ppermute | solution.py:55
  22.5 6.3 %collective-permute-start.5 = (bf16[128,1024]{1,0:T(8,128)(2,1)S(1)}, bf16[128,1024]{1,0:T(8,128)(2,1)S(1)}, u32[]{:S(2)}, u32[]{:S(2)}) collective-permute-start(bf16[128,1024]{1,0:T(8,128)(2,1)S(1)} %pad_maximum_fusion), channel_id=1, source_target_pairs={{0,48},{16,0},{32,16},{48,32},{1,49},{17,1},{33,17},{49,33},{2,50}... | collective-permute-start | bytes 786440 | tf_op jit(solution)/shard_map/ppermute | solution.py:55
  27.8 6.7 %collective-permute-start.4 = (bf16[128,1024]{1,0:T(8,128)(2,1)}, bf16[128,1024]{1,0:T(8,128)(2,1)}, u32[]{:S(2)}, u32[]{:S(2)}) collective-permute-start(bf16[128,1024]{1,0:T(8,128)(2,1)} %collective-permute-done.3), channel_id=1, source_target_pairs={{0,16},{16,32},{32,48},{48,0},{1,17},{17,33},{33,49},{49,1},{2,18}... | collective-permute-start | bytes 786440 | tf_op jit(solution)/shard_map/ppermute | solution.py:55
  35.5 7.4 %collective-permute-start.6 = (bf16[512,1024]{1,0:T(8,128)(2,1)S(1)}, bf16[512,1024]{1,0:T(8,128)(2,1)S(1)}, u32[]{:S(2)}, u32[]{:S(2)}) collective-permute-start(bf16[512,1024]{1,0:T(8,128)(2,1)S(1)} %constant_dynamic-update-slice_fusion.near), channel_id=1, source_target_pairs={{0,1},{1,0},{2,3},{3,2},{4,5},{5,4},{6,7},{7,6},{8,9},{9,8},{10,11... | collective-permute-start | bytes 3145736 | tf_op jit(solution)/shard_map/ppermute | solution.py:51
  48.5 1.3 %collective-permute-start.7 = (f32[8,128]{1,0:T(8,128)S(1)}, f32[8,128]{1,0:T(8,128)S(1)}, u32[]{:S(2)}, u32[]{:S(2)}) collective-permute-start(f32[8,128]{1,0:T(8,128)S(1)} %get-tuple-element.32.mine), channel_id=1, source_target_pairs={{0,1},{1,0},{2,3},{3,2},{4,5},{5,4},{6,7},{7,6},{8,9},{9,8},{10,11... | collective-permute-start | bytes 12296 | tf_op jit(solution)/shard_map/ppermute | solution.py:51
  65.9 19.3 %copy-start.5 = (f32[768]{0:T(1024)S(1)}, f32[768]{0:T(1024)}, u32[]{:S(2)}) copy-start(f32[768]{0:T(1024)} %param.7) | copy-start | bytes 9220
  107.7 6.9 %copy-start = (bf16[32,32,768]{2,1,0:T(8,128)(2,1)}, bf16[32,32,768]{2,1,0:T(8,128)(2,1)S(1)}, u32[]{:S(2)}) copy-start(bf16[32,32,768]{2,1,0:T(8,128)(2,1)S(1)} %broadcast_in_dim.5._) | copy-start | bytes 4718596
  107.8 6.1 %collective-permute-start.8 = (f32[56,128]{1,0:T(8,128)S(1)}, f32[56,128]{1,0:T(8,128)S(1)}, u32[]{:S(2)}, u32[]{:S(2)}) collective-permute-start(f32[56,128]{1,0:T(8,128)S(1)} %last.1.mine), channel_id=1, source_target_pairs={{0,1},{1,0},{2,3},{3,2},{4,5},{5,4},{6,7},{7,6},{8,9},{9,8},{10,11... | collective-permute-start | bytes 86024 | tf_op jit(solution)/shard_map/ppermute | solution.py:51

commit v5 on v4

--- a/solution.py
+++ b/solution.py
@@ -26,7 +26,7 @@
     "H": pl.BlockSpec(memory_space=pltpu.HBM),
     "A": pl.BlockSpec(memory_space=pl.ANY),
 }
-SMALL, SCORES = 12 << 20, 12 << 20
+LIMIT = 12 << 20
 
 
 def shaped(*shape, dtype=f32):
@@ -55,6 +55,10 @@
     return lax.ppermute(block, axis, [(i, (i + step) % 4) for i in range(4)])
 
 
+def across(block, flip):
+    return lax.ppermute(block, "x", [(i, i ^ flip) for i in range(4)])
+
+
 def halves(value):
     high = value.astype(b16)
     return high, (value - high.astype(f32)).astype(b16)
@@ -73,7 +77,7 @@
     return jnp.concatenate([gain[k : k + 1, :] for k in range(D // 128)], axis=1)
 
 
-def norm_kernel(features, places, gain, sent, scaled, radius):
+def norm_kernel(features, places, gain, own, scaled, radius):
     for n in range(0, OWN, 8):
         at = slice(n, n + 8)
         pooled = jnp.sum(features[at].astype(f32), axis=1) * (1.0 / WIN)
@@ -84,28 +88,34 @@
     place = places[...]
     lane = lax.broadcasted_iota(jnp.int32, place.shape, 1)
     marks = jnp.where(lane == 0, place >> 7, place & 127).astype(f32).astype(b16)
-    for s in range(NROW):
-        sent[s, :, :D] = value
-        sent[s, :, D:] = marks
+    own[:, :D] = value
+    own[:, D:] = marks
 
 
 def position():
     return [lax.axis_index(a) for a in ("y", "x", "zl", "c", "zh")]
 
 
-def student_kernel(rows, head, student, unit, length, full, sizes):
+def student_kernel(four, rest, head, rows, student, unit, length, full, sizes):
+    where = position()
+    x, zl = where[1], where[2]
+
+    def slot(x_, zl_):
+        return pl.ds(pl.multiple_of((((x_ + 4) & 3) * 2 + zl_) * OWN, OWN), OWN)
+
+    for k, (ref, start) in enumerate(((four, 0), (four, 64), (rest, 64), (rest, 0))):
+        rows[slot(x ^ k, zl), :] = ref[start : start + OWN, :]
+        rows[slot(x ^ k, 1 - zl), :] = ref[start + OWN : start + 2 * OWN, :]
     raw = jnp.dot(rows[:, :D], head[...], preferred_element_type=f32)
     full[...], sizes[...] = unit_rows(raw)
     student[...] = full[...].astype(b16)
-    where = position()
-    own = pl.ds(pl.multiple_of((where[1] * 2 + where[2]) * OWN, OWN), OWN)
-    unit[...] = full[own, :]
-    length[...] = sizes[own, :]
+    unit[...] = full[slot(x, zl), :]
+    length[...] = sizes[slot(x, zl), :]
 
 
 def place(where, k):
-    core = where[3] if k % 2 == 0 else 1 - where[3]
-    y = (where[0] + (0, 3, 1, 2)[k // 2]) & 3
+    core = where[3] if k < 4 else 1 - where[3]
+    y = (where[0] + (0, 3, 1, 2)[k % 4]) & 3
     return core, y
 
 
@@ -114,30 +124,19 @@
     marks = marks.astype(f32)
     wanted = marks[:, 0:1] * 128.0 + marks[:, 1:2]
     lane = lax.broadcasted_iota(jnp.int32, (1, BLOCK), 1)
-    ids = (lane >> 5) * 2048 + (lane & 31) + y * 512 + where[1] * 128 + where[2] * 64 + core * 32
+    ids = (((lane >> 5) + where[4]) & 3) * 2048 + (lane & 31)
+    ids = ids + y * 512 + where[1] * 128 + where[2] * 64 + core * 32
     return wanted == ids.astype(f32)
 
 
-def fetch(where, sides, teach, sems):
-    copies = []
-    for k in range(8):
-        for n in range(4):
-            slot = pl.multiple_of(((where[4] + 4 - n) & 3) * OWN, OWN)
-            here = sides[k % 2].at[pl.ds(k // 2 * BLOCK + n * OWN, OWN), :]
-            there = teach.at[pl.ds(k * BLOCK + slot, OWN), :]
-            copies.append(pltpu.make_async_copy(here, there, sems.at[4 * k + n]))
-            copies[-1].start()
-    return copies
-
-
-def scores_kernel(student, rows, near, pair, teach, expo, terms, col_part, pos_part, sems):
+def scores_kernel(student, rows, *refs):
+    blocks, (teach, expo, terms, col_part, pos_part) = refs[:8], refs[8:]
     where = position()
-    copies = fetch(where, (near, pair), teach, sems)
+    for k, block in enumerate(blocks):
+        teach[k * BLOCK : (k + 1) * BLOCK, :] = block[...]
     lanes = [jnp.zeros((CHUNK, 128), f32) for _ in range(SIDE // CHUNK)]
     pos = jnp.zeros((1, BLOCK), f32)
     for k in range(0, 8, 2):
-        for copy in copies[4 * k : 4 * k + 8]:
-            copy.wait()
         both = product(student[...], teach[k * BLOCK : (k + 2) * BLOCK, :], 1, 1)
         for j in (k, k + 1):
             col = jnp.zeros((1, BLOCK), f32)
@@ -152,6 +151,7 @@
                 lanes[n] = lanes[n] + e
             core, y = place(where, j)
             col_part[pl.ds(core * 4 + y, 1), :] = col
+    col_part[...] = pltpu.roll(col_part[...], where[4] * OWN, 1)
     pos_part[...] = pos
     for n in range(SIDE // CHUNK):
         at = slice(n * CHUNK, (n + 1) * CHUNK)
@@ -172,7 +172,7 @@
     cols = jnp.sum(col_in[...], axis=0)
     logs = jnp.sum(jnp.log(cols), axis=0, keepdims=True)
     tail[...] = logs * (1.0 / NCOL) - 2.0 * pos_part[...]
-    inv[...] = 1.0 / cols
+    inv[...] = pltpu.roll(1.0 / cols, ((4 - where[4]) & 3) * OWN, 1)
     for k in range(8):
         core, y = place(where, k)
         scale = inv[pl.ds(core * 4 + y, 1), :]
@@ -237,14 +237,14 @@
     loss[...] = total[54:55, :] * (1.0 / (2.0 * OWN * NROW * NCOL))
 
 
-def call(kernel, out, ins, name, outs=None, limit=SMALL, **options):
+def call(kernel, out, ins, name, outs=None, **options):
     out_specs = [SPACES[k] for k in outs or "V" * (len(out) if isinstance(out, list) else 1)]
     return pl.pallas_call(
         kernel,
         out_shape=out,
         in_specs=[SPACES[k] for k in ins],
         out_specs=out_specs if isinstance(out, list) else out_specs[0],
-        compiler_params=pltpu.CompilerParams(vmem_limit_bytes=limit),
+        compiler_params=pltpu.CompilerParams(vmem_limit_bytes=LIMIT),
         name=name,
         **options,
     )
@@ -254,14 +254,14 @@
     wide = 2 * HALF
 
     mine = call(teacher_kernel, shaped(OWN, E, dtype=b16), "V", "teacher")(teacher)
-    mine = jnp.concatenate([mine] + [along(mine, "zh", k) for k in (1, 2, 3)], axis=0)
+    mine = jnp.concatenate([mine] + [along(mine, "zh", k) for k in (3, 2, 1)], axis=0)
 
     places = jnp.broadcast_to(positives[:, None], (OWN, MARK))
     gain = gain.reshape(D // 128, 128)
     own, scaled, radius = call(
         norm_kernel,
         [
-            shaped(NROW, OWN, D + MARK, dtype=b16),
+            shaped(OWN, D + MARK, dtype=b16),
             shaped(OWN, D),
             shaped(OWN, 1),
         ],
@@ -272,28 +272,29 @@
     mine, own = lax.optimization_barrier((mine, own))
     up, down = along(mine, "y", 1), along(mine, "y", 3)
     far = along(up, "y", 1)
-    rows = swap(own, ROW).reshape(SIDE, D + MARK)
-    student, unit, length = call(
+
+    four = jnp.concatenate([own, other(own, "zl")], axis=0)
+    four = jnp.concatenate([four, across(four, 1)], axis=0)
+    rows, student, unit, length = call(
         student_kernel,
-        [shaped(SIDE, E, dtype=b16), shaped(OWN, E), shaped(OWN, 1)],
-        "VV",
+        [shaped(SIDE, D + MARK, dtype=b16), shaped(SIDE, E, dtype=b16)]
+        + [shaped(OWN, E), shaped(OWN, 1)],
+        "VVV",
         "student",
         scratch_shapes=[pltpu.VMEM((SIDE, E), f32), pltpu.VMEM((SIDE, 1), f32)],
-    )(rows, w_head)
+    )(four, across(four, 3), w_head)
     far, student = lax.optimization_barrier((far, student))
-    near = jnp.concatenate([mine, up, down, far], axis=0)
-    pair = other(near, "c")
+    blocks = [mine, up, down, far]
+    blocks += [other(block, "c") for block in blocks]
 
     message = shaped(SIDE, 2 * E + MARK, dtype=b16)
     teach, expo, terms, col_part, pos_part = call(
         scores_kernel,
         [shaped(wide, E, dtype=b16), shaped(SIDE, wide, dtype=b16), message]
         + [shaped(8, 128), shaped(1, 128)],
-        "VVAA",
+        "V" * 10,
         "scores",
-        limit=SCORES,
-        scratch_shapes=[pltpu.SemaphoreType.DMA((32,))],
-    )(student, rows, near, pair)
+    )(student, rows, *blocks)
     col_in = call(cols_kernel, shaped(NCHIP, 8, 128), "VV", "cols")(col_part, other(col_part, "c"))
     col_in = swap(col_in, CHIPS)
     terms, tail = call(

time: 115 us -> 107 us (0.930)
  Pallas kernels: 10.8 us -> 6.16 us
  waiting for transfers between devices: 13.2 us -> 9.9 us
  local copies, waits for them, and re-layouts: 5.76 us -> 3.81 us
  starting transfers between devices: 28.6 us -> 30.2 us
    ppermute x6, waiting for transfers between devices: 9.24 us -> 3.67 us  [along(): return lax.ppermute(block, axis, [(i, (i + step) % 4) for i in range(4)])]
    all_to_all x1 -> x0, starting transfers between devices: 4.72 us -> none  [swap(): return lax.all_to_all(blocks, axes, 0, 0, tiled=True)]
    pallas_call x1, Pallas kernels: 5.53 us -> 1.65 us  [body(): call(scores_kernel, [shaped(wide, E, dtype=b16), shaped(SIDE, wide, dtype...]
    ppermute x0 -> x2, starting transfers between devices: none -> 3.86 us  [across(): return lax.ppermute(block, 'x', [(i, i ^ flip) for i in range(4)])]
    ppermute x6, starting transfers between devices: 13 us -> 15.5 us  [along(): return lax.ppermute(block, axis, [(i, (i + step) % 4) for i in range(4)])]
    ppermute x0 -> x2, waiting for transfers between devices: none -> 1.75 us  [across(): return lax.ppermute(block, 'x', [(i, i ^ flip) for i in range(4)])]
    unnamed x15 -> x14, local copies, waits for them, and re-layouts: 3.96 us -> 2.96 us
    ppermute x3 -> x7, waiting for transfers between devices: 3.96 us -> 4.48 us  [other(): return lax.ppermute(block, axis, [(0, 1), (1, 0)])]
  transfers between devices with their start and end apart: 10 -> 15, of which waited for: 6 -> 8; matrix products, arithmetic and copies ran while one was open for 2% -> 1% of each run, Pallas kernels for 2% -> 1%
where the time goes in v5:
time: 107 us; the launch traced here: 106 us
  blocking collectives  55.5 us (52%)
  starting transfers between devices  30.2 us (28%)
  waiting for transfers between devices  9.9 us (9%)
  Pallas kernels  6.16 us (6%)
  local copies, waits for them, and re-layouts  3.81 us (4%)
    all_to_all x4, blocking collectives, swap(): return lax.all_to_all(blocks, axes, 0, 0, tiled=True)  55.5 us
    ppermute x6, starting transfers between devices, along(): return lax.ppermute(block, axis, [(i, (i + step) % 4) for i in range(4)])  15.5 us
    ppermute x7, starting transfers between devices, other(): return lax.ppermute(block, axis, [(0, 1), (1, 0)])  10.8 us
    ppermute x7, waiting for transfers between devices, other(): return lax.ppermute(block, axis, [(0, 1), (1, 0)])  4.48 us
    ppermute x2, starting transfers between devices, across(): return lax.ppermute(block, 'x', [(i, i ^ flip) for i in range(4)])  3.86 us
    ppermute x6, waiting for transfers between devices, along(): return lax.ppermute(block, axis, [(i, (i + step) % 4) for i in range(4)])  3.67 us
    unnamed x14, local copies, waits for them, and re-layouts  2.96 us
  transfers between devices with their start and end apart: 15, of which 8 were waited for; matrix products, arithmetic and copies ran while one was open for 1% of the time, Pallas kernels for 1%

profile of v5, /device:TPU:1, one launch (start us, length us, event | category | flops | bytes accessed | tf_op | source)
XLA Modules:
  0.0 106.3 jit_solution(16572912300964360183)
XLA Ops:
  0.6 0.0 copy-start.3
  0.6 0.8 copy-done.3
  1.5 0.0 copy-start.1
  1.5 0.1 teacher.2
  1.6 3.9 %collective-permute-start.2 = (bf16[32,1024]{1,0:T(8,128)(2,1)S(1)}, bf16[32,1024]{1,0:T(8,128)(2,1)S(1)}, u32[]{:S(2)}, u32[]{:S(2)}) collective-permute-start(bf16[32,1024]{1,0:T(8,128)(2,1)S(1)} %teacher.2), channel_id=1, source_target_pairs={{0,64},{64,128},{128,192},{192,0},{1,65},{65,129},{129,193},{193,1... | collective-permute-start | bytes 196616 | tf_op jit(solution)/shard_map/ppermute | solution.py:55
  5.5 5.1 %collective-permute-start.1 = (bf16[32,1024]{1,0:T(8,128)(2,1)S(1)}, bf16[32,1024]{1,0:T(8,128)(2,1)S(1)}, u32[]{:S(2)}, u32[]{:S(2)}) collective-permute-start(bf16[32,1024]{1,0:T(8,128)(2,1)S(1)} %teacher.2), channel_id=1, source_target_pairs={{0,128},{64,192},{128,0},{192,64},{1,129},{65,193},{129,1},{193,65... | collective-permute-start | bytes 196616 | tf_op jit(solution)/shard_map/ppermute | solution.py:55
  10.6 2.4 %collective-permute-start = (bf16[32,1024]{1,0:T(8,128)(2,1)S(1)}, bf16[32,1024]{1,0:T(8,128)(2,1)S(1)}, u32[]{:S(2)}, u32[]{:S(2)}) collective-permute-start(bf16[32,1024]{1,0:T(8,128)(2,1)S(1)} %teacher.2), channel_id=1, source_target_pairs={{0,192},{64,0},{128,64},{192,128},{1,193},{65,1},{129,65},{193,129... | collective-permute-start | bytes 196616 | tf_op jit(solution)/shard_map/ppermute | solution.py:55
  13.0 0.7 broadcast_in_dim.4.places
  13.7 0.0 copy-start.2
  13.7 1.4 %copy-done.2 = bf16[32,32,768]{2,1,0:T(8,128)(2,1)S(1)} copy-done((bf16[32,32,768]{2,1,0:T(8,128)(2,1)S(1)}, bf16[32,32,768]{2,1,0:T(8,128)(2,1)}, u32[]{:S(2)}) %copy-start.2) | copy-done | bytes 1572888
  15.1 0.0 copy-start.4
  15.1 0.7 copy-done.4
  15.8 0.5 norm.1
  16.3 0.0 collective-permute-done.2
  16.3 0.0 collective-permute-done.1
  16.4 1.9 %collective-permute-done = bf16[32,1024]{1,0:T(8,128)(2,1)S(1)} collective-permute-done((bf16[32,1024]{1,0:T(8,128)(2,1)S(1)}, bf16[32,1024]{1,0:T(8,128)(2,1)S(1)}, u32[]{:S(2)}, u32[]{:S(2)}) %collective-permute-start) | collective-permute-done | bytes 65568 | tf_op jit(solution)/shard_map/ppermute | solution.py:55
  18.3 0.1 collective-permute-start.3
  18.4 1.4 %collective-permute-start.6 = (bf16[128,1024]{1,0:T(8,128)(2,1)S(1)}, bf16[128,1024]{1,0:T(8,128)(2,1)S(1)}, u32[]{:S(2)}, u32[]{:S(2)}) collective-permute-start(bf16[128,1024]{1,0:T(8,128)(2,1)S(1)} %pad_maximum_fusion.refs_0_), channel_id=1, source_target_pairs={{0,16},{16,32},{32,48},{48,0},{1,17},{17,33},{33,49},{49,1},{2,18}... | collective-permute-start | bytes 786440 | tf_op jit(solution)/shard_map/ppermute | solution.py:55
  19.8 1.6 %collective-permute-done.3 = bf16[32,896]{1,0:T(8,128)(2,1)S(1)} collective-permute-done((bf16[32,896]{1,0:T(8,128)(2,1)S(1)}, bf16[32,896]{1,0:T(8,128)(2,1)S(1)}, u32[]{:S(2)}, u32[]{:S(2)}) %collective-permute-start.3) | collective-permute-done | bytes 57376 | tf_op jit(solution)/shard_map/ppermute | solution.py:51
  21.4 1.3 %collective-permute-start.4 = (bf16[64,896]{1,0:T(8,128)(2,1)S(1)}, bf16[64,896]{1,0:T(8,128)(2,1)S(1)}, u32[]{:S(2)}, u32[]{:S(2)}) collective-permute-start(bf16[64,896]{1,0:T(8,128)(2,1)S(1)} %pad_maximum_fusion.1), channel_id=1, source_target_pairs={{0,4},{4,0},{8,12},{12,8},{1,5},{5,1},{9,13},{13,9},{2,6},{6,2},{1... | collective-permute-start | bytes 344072 | tf_op jit(solution)/shard_map/ppermute | solution.py:59
  22.7 2.7 %collective-permute-start.8 = (bf16[128,1024]{1,0:T(8,128)(2,1)S(1)}, bf16[128,1024]{1,0:T(8,128)(2,1)S(1)}, u32[]{:S(2)}, u32[]{:S(2)}) collective-permute-start(bf16[128,1024]{1,0:T(8,128)(2,1)S(1)} %pad_maximum_fusion.refs_0_), channel_id=1, source_target_pairs={{0,48},{16,0},{32,16},{48,32},{1,49},{17,1},{33,17},{49,33},{2,50}... | collective-permute-start | bytes 786440 | tf_op jit(solution)/shard_map/ppermute | solution.py:55
  25.5 1.6 %collective-permute-done.6.refs_1_ = bf16[128,1024]{1,0:T(8,128)(2,1)S(1)} collective-permute-done((bf16[128,1024]{1,0:T(8,128)(2,1)S(1)}, bf16[128,1024]{1,0:T(8,128)(2,1)S(1)}, u32[]{:S(2)}, u32[]{:S(2)}) %collective-permute-start.6) | collective-permute-done | bytes 262176 | tf_op jit(solution)/shard_map/ppermute | solution.py:55
  27.1 0.0 collective-permute-start.7
  27.1 0.0 collective-permute-done.4
  27.1 2.6 %collective-permute-start.5 = (bf16[128,896]{1,0:T(8,128)(2,1)S(1)}, bf16[128,896]{1,0:T(8,128)(2,1)S(1)}, u32[]{:S(2)}, u32[]{:S(2)}) collective-permute-start(bf16[128,896]{1,0:T(8,128)(2,1)S(1)} %constant_dynamic-update-slice_fusion.four), channel_id=1, source_target_pairs={{0,12},{4,8},{8,4},{12,0},{1,13},{5,9},{9,5},{13,1},{2,14},{6,10},... | collective-permute-start | bytes 688136 | tf_op jit(solution)/shard_map/ppermute | solution.py:59
  29.7 1.9 %collective-permute-start.9 = (bf16[128,1024]{1,0:T(8,128)(2,1)S(1)}, bf16[128,1024]{1,0:T(8,128)(2,1)S(1)}, u32[]{:S(2)}, u32[]{:S(2)}) collective-permute-start(bf16[128,1024]{1,0:T(8,128)(2,1)S(1)} %pad_maximum_fusion.refs_0_), channel_id=1, source_target_pairs={{0,1},{1,0},{2,3},{3,2},{4,5},{5,4},{6,7},{7,6},{8,9},{9,8},{10,11... | collective-permute-start | bytes 786440 | tf_op jit(solution)/shard_map/ppermute | solution.py:51
  31.6 0.0 collective-permute-start.10
  31.6 0.0 collective-permute-done.8.refs_2_
  31.6 0.5 collective-permute-start.11
  32.1 1.7 %collective-permute-done.5.rest = bf16[128,896]{1,0:T(8,128)(2,1)S(1)} collective-permute-done((bf16[128,896]{1,0:T(8,128)(2,1)S(1)}, bf16[128,896]{1,0:T(8,128)(2,1)S(1)}, u32[]{:S(2)}, u32[]{:S(2)}) %collective-permute-start.5) | collective-permute-done | bytes 229408 | tf_op jit(solution)/shard_map/ppermute | solution.py:59
  33.9 0.0 copy-done.1
  33.9 0.8 student.1
  34.7 0.1 collective-permute-done.7.refs_3_
  34.8 2.5 %collective-permute-start.12 = (bf16[128,1024]{1,0:T(8,128)(2,1)S(1)}, bf16[128,1024]{1,0:T(8,128)(2,1)S(1)}, u32[]{:S(2)}, u32[]{:S(2)}) collective-permute-start(bf16[128,1024]{1,0:T(8,128)(2,1)S(1)} %collective-permute-done.7.refs_3_), channel_id=1, source_target_pairs={{0,1},{1,0},{2,3},{3,2},{4,5},{5,4},{6,7},{7,6},{8,9},{9,8},{10,11... | collective-permute-start | bytes 786440 | tf_op jit(solution)/shard_map/ppermute | solution.py:51
  37.3 0.0 collective-permute-done.9.refs_4_
  37.3 0.0 collective-permute-done.11.refs_6_
  37.3 0.0 collective-permute-done.10.refs_5_
  37.3 1.1 %collective-permute-done.12.refs_7_ = bf16[128,1024]{1,0:T(8,128)(2,1)S(1)} collective-permute-done((bf16[128,1024]{1,0:T(8,128)(2,1)S(1)}, bf16[128,1024]{1,0:T(8,128)(2,1)S(1)}, u32[]{:S(2)}, u32[]{:S(2)}) %collective-permute-start.12) | collective-permute-done | bytes 262176 | tf_op jit(solution)/shard_map/ppermute | solution.py:51
  38.5 1.6 %scores.1 = (bf16[1024,1024]{1,0:T(8,128)(2,1)S(1)}, bf16[256,1024]{1,0:T(8,128)(2,1)S(1)}, bf16[256,2176]{1,0:T(8,128)(2,1)S(1)}, f32[8,128]{1,0:T(8,128)S(1)}, f32[1,128]{1,0:T(1,128)S(1)}) custom-call(bf16[256,1024]{1,0:T(8,128)(2,1)S(1)} %get-tuple-element.32.student, bf16[256,896]{1,0:T(8,128)(2,1)S(1)} %get-tuple-element.29.rows, ...), custom_call_target="tpu_custom_call" | custom-call | tf_op jit(solution)/shard_map/scores/pallas_call | solution.py:291
  40.1 0.5 collective-permute-start.13
  40.6 0.8 collective-permute-done.13.pair
  41.4 15.6 %all_to_all.20.col_in = f32[16,8,128]{2,1,0:T(8,128)S(1)} all-to-all(f32[16,8,128]{2,1,0:T(8,128)S(1)} %cols.1), channel_id=1, replica_groups=mesh['zh'=4,'y'=4,'x'=4,'zl'=2,'c'=2] {'zh','y'}, dimensions={0} | all-to-all | bytes 131072 | tf_op jit(solution)/shard_map/all_to_all | solution.py:42
  57.0 1.2 %scaled.1 = (bf16[256,2176]{1,0:T(8,128)(2,1)S(1)}, f32[1,128]{1,0:T(1,128)S(1)}) custom-call(bf16[256,896]{1,0:T(8,128)(2,1)S(1)} %get-tuple-element.29.rows, f32[16,8,128]{2,1,0:T(8,128)S(1)} %all_to_all.20.col_in, f32[1,128]{1,0:T(1,128)S(1)} %get-tuple-element.35.pos_part, ...), custom_call_target="tpu_custom_call", output_to_operand_aliasing={{0}: (5, {})} | custom-call | tf_op jit(solution)/shard_map/scaled/pallas_call | solution.py:300
  58.2 0.0 copy-start.5
  58.2 18.7 %all_to_all.21.terms = bf16[8,32,2176]{2,1,0:T(8,128)(2,1)S(1)} all-to-all(bf16[8,32,2176]{2,1,0:T(8,128)(2,1)S(1)} %bitcast.5), channel_id=1, replica_groups=mesh['zh'=4,'y'=4,'x'=4,'zl'=2,'c'=2] {'x','zl'}, dimensions={0} | all-to-all | bytes 2228224 | tf_op jit(solution)/shard_map/all_to_all | solution.py:42
  76.9 0.0 copy-done.5
  76.9 0.9 rows.1
  77.8 8.1 %all_to_all.22.back = bf16[8,48,128]{2,1,0:T(8,128)(2,1)S(1)} all-to-all(bf16[8,48,128]{2,1,0:T(8,128)(2,1)S(1)} %get-tuple-element.45), channel_id=1, replica_groups=mesh['zh'=4,'y'=4,'x'=4,'zl'=2,'c'=2] {'x','zl'}, dimensions={0} | all-to-all | bytes 196608 | tf_op jit(solution)/shard_map/all_to_all | solution.py:42
  85.9 0.3 head.5
  86.2 13.1 %all_to_all.23.back = bf16[16,64,128]{2,1,0:T(8,128)(2,1)S(1)} all-to-all(bf16[16,64,128]{2,1,0:T(8,128)(2,1)S(1)} %head.5), channel_id=1, replica_groups=mesh['zh'=4,'y'=4,'x'=4,'zl'=2,'c'=2] {'zh','y'}, dimensions={0} | all-to-all | bytes 524288 | tf_op jit(solution)/shard_map/all_to_all | solution.py:42
  99.3 0.1 broadcast_in_dim.5._
  99.4 0.0 copy-start
  99.5 5.3 %collective-permute-start.14 = (f32[56,128]{1,0:T(8,128)S(1)}, f32[56,128]{1,0:T(8,128)S(1)}, u32[]{:S(2)}, u32[]{:S(2)}) collective-permute-start(f32[56,128]{1,0:T(8,128)S(1)} %last.1.mine), channel_id=1, source_target_pairs={{0,1},{1,0},{2,3},{3,2},{4,5},{5,4},{6,7},{7,6},{8,9},{9,8},{10,11... | collective-permute-start | bytes 86024 | tf_op jit(solution)/shard_map/ppermute | solution.py:51
  104.7 0.9 collective-permute-done.14.pair
  105.6 0.7 out.1
  106.3 0.0 copy-done
  (7 shorter events, 0.1 us)
Async XLA Ops:
  0.6 0.8 copy-start.3
  1.5 32.4 %copy-start.1 = (bf16[768,1024]{1,0:T(8,128)(2,1)S(1)}, bf16[768,1024]{1,0:T(8,128)(2,1)}, u32[]{:S(2)}) copy-start(bf16[768,1024]{1,0:T(8,128)(2,1)} %head.4) | copy-start | bytes 4718596
  1.6 14.8 %collective-permute-start.2 = (bf16[32,1024]{1,0:T(8,128)(2,1)S(1)}, bf16[32,1024]{1,0:T(8,128)(2,1)S(1)}, u32[]{:S(2)}, u32[]{:S(2)}) collective-permute-start(bf16[32,1024]{1,0:T(8,128)(2,1)S(1)} %teacher.2), channel_id=1, source_target_pairs={{0,64},{64,128},{128,192},{192,0},{1,65},{65,129},{129,193},{193,1... | collective-permute-start | bytes 196616 | tf_op jit(solution)/shard_map/ppermute | solution.py:55
  5.5 10.9 %collective-permute-start.1 = (bf16[32,1024]{1,0:T(8,128)(2,1)S(1)}, bf16[32,1024]{1,0:T(8,128)(2,1)S(1)}, u32[]{:S(2)}, u32[]{:S(2)}) collective-permute-start(bf16[32,1024]{1,0:T(8,128)(2,1)S(1)} %teacher.2), channel_id=1, source_target_pairs={{0,128},{64,192},{128,0},{192,64},{1,129},{65,193},{129,1},{193,65... | collective-permute-start | bytes 196616 | tf_op jit(solution)/shard_map/ppermute | solution.py:55
  10.6 7.7 %collective-permute-start = (bf16[32,1024]{1,0:T(8,128)(2,1)S(1)}, bf16[32,1024]{1,0:T(8,128)(2,1)S(1)}, u32[]{:S(2)}, u32[]{:S(2)}) collective-permute-start(bf16[32,1024]{1,0:T(8,128)(2,1)S(1)} %teacher.2), channel_id=1, source_target_pairs={{0,192},{64,0},{128,64},{192,128},{1,193},{65,1},{129,65},{193,129... | collective-permute-start | bytes 196616 | tf_op jit(solution)/shard_map/ppermute | solution.py:55
  13.7 1.4 %copy-start.2 = (bf16[32,32,768]{2,1,0:T(8,128)(2,1)S(1)}, bf16[32,32,768]{2,1,0:T(8,128)(2,1)}, u32[]{:S(2)}) copy-start(bf16[32,32,768]{2,1,0:T(8,128)(2,1)} %features.1) | copy-start | bytes 4718596
  15.1 0.7 copy-start.4
  18.3 3.1 %collective-permute-start.3 = (bf16[32,896]{1,0:T(8,128)(2,1)S(1)}, bf16[32,896]{1,0:T(8,128)(2,1)S(1)}, u32[]{:S(2)}, u32[]{:S(2)}) collective-permute-start(bf16[32,896]{1,0:T(8,128)(2,1)S(1)} %get-tuple-element.28), channel_id=1, source_target_pairs={{0,2},{2,0},{1,3},{3,1},{4,6},{6,4},{5,7},{7,5},{8,10},{10,8},{9,1... | collective-permute-start | bytes 172040 | tf_op jit(solution)/shard_map/ppermute | solution.py:51
  18.4 8.7 %collective-permute-start.6 = (bf16[128,1024]{1,0:T(8,128)(2,1)S(1)}, bf16[128,1024]{1,0:T(8,128)(2,1)S(1)}, u32[]{:S(2)}, u32[]{:S(2)}) collective-permute-start(bf16[128,1024]{1,0:T(8,128)(2,1)S(1)} %pad_maximum_fusion.refs_0_), channel_id=1, source_target_pairs={{0,16},{16,32},{32,48},{48,0},{1,17},{17,33},{33,49},{49,1},{2,18}... | collective-permute-start | bytes 786440 | tf_op jit(solution)/shard_map/ppermute | solution.py:55
  21.4 5.7 %collective-permute-start.4 = (bf16[64,896]{1,0:T(8,128)(2,1)S(1)}, bf16[64,896]{1,0:T(8,128)(2,1)S(1)}, u32[]{:S(2)}, u32[]{:S(2)}) collective-permute-start(bf16[64,896]{1,0:T(8,128)(2,1)S(1)} %pad_maximum_fusion.1), channel_id=1, source_target_pairs={{0,4},{4,0},{8,12},{12,8},{1,5},{5,1},{9,13},{13,9},{2,6},{6,2},{1... | collective-permute-start | bytes 344072 | tf_op jit(solution)/shard_map/ppermute | solution.py:59
  22.7 8.9 %collective-permute-start.8 = (bf16[128,1024]{1,0:T(8,128)(2,1)S(1)}, bf16[128,1024]{1,0:T(8,128)(2,1)S(1)}, u32[]{:S(2)}, u32[]{:S(2)}) collective-permute-start(bf16[128,1024]{1,0:T(8,128)(2,1)S(1)} %pad_maximum_fusion.refs_0_), channel_id=1, source_target_pairs={{0,48},{16,0},{32,16},{48,32},{1,49},{17,1},{33,17},{49,33},{2,50}... | collective-permute-start | bytes 786440 | tf_op jit(solution)/shard_map/ppermute | solution.py:55
  27.1 7.7 %collective-permute-start.7 = (bf16[128,1024]{1,0:T(8,128)(2,1)S(1)}, bf16[128,1024]{1,0:T(8,128)(2,1)S(1)}, u32[]{:S(2)}, u32[]{:S(2)}) collective-permute-start(bf16[128,1024]{1,0:T(8,128)(2,1)S(1)} %collective-permute-done.6.refs_1_), channel_id=1, source_target_pairs={{0,16},{16,32},{32,48},{48,0},{1,17},{17,33},{33,49},{49,1},{2,18}... | collective-permute-start | bytes 786440 | tf_op jit(solution)/shard_map/ppermute | solution.py:55
  27.1 6.7 %collective-permute-start.5 = (bf16[128,896]{1,0:T(8,128)(2,1)S(1)}, bf16[128,896]{1,0:T(8,128)(2,1)S(1)}, u32[]{:S(2)}, u32[]{:S(2)}) collective-permute-start(bf16[128,896]{1,0:T(8,128)(2,1)S(1)} %constant_dynamic-update-slice_fusion.four), channel_id=1, source_target_pairs={{0,12},{4,8},{8,4},{12,0},{1,13},{5,9},{9,5},{13,1},{2,14},{6,10},... | collective-permute-start | bytes 688136 | tf_op jit(solution)/shard_map/ppermute | solution.py:59
  29.7 7.6 %collective-permute-start.9 = (bf16[128,1024]{1,0:T(8,128)(2,1)S(1)}, bf16[128,1024]{1,0:T(8,128)(2,1)S(1)}, u32[]{:S(2)}, u32[]{:S(2)}) collective-permute-start(bf16[128,1024]{1,0:T(8,128)(2,1)S(1)} %pad_maximum_fusion.refs_0_), channel_id=1, source_target_pairs={{0,1},{1,0},{2,3},{3,2},{4,5},{5,4},{6,7},{7,6},{8,9},{9,8},{10,11... | collective-permute-start | bytes 786440 | tf_op jit(solution)/shard_map/ppermute | solution.py:51
  31.6 5.7 %collective-permute-start.10 = (bf16[128,1024]{1,0:T(8,128)(2,1)S(1)}, bf16[128,1024]{1,0:T(8,128)(2,1)S(1)}, u32[]{:S(2)}, u32[]{:S(2)}) collective-permute-start(bf16[128,1024]{1,0:T(8,128)(2,1)S(1)} %collective-permute-done.6.refs_1_), channel_id=1, source_target_pairs={{0,1},{1,0},{2,3},{3,2},{4,5},{5,4},{6,7},{7,6},{8,9},{9,8},{10,11... | collective-permute-start | bytes 786440 | tf_op jit(solution)/shard_map/ppermute | solution.py:51
  31.6 5.7 %collective-permute-start.11 = (bf16[128,1024]{1,0:T(8,128)(2,1)S(1)}, bf16[128,1024]{1,0:T(8,128)(2,1)S(1)}, u32[]{:S(2)}, u32[]{:S(2)}) collective-permute-start(bf16[128,1024]{1,0:T(8,128)(2,1)S(1)} %collective-permute-done.8.refs_2_), channel_id=1, source_target_pairs={{0,1},{1,0},{2,3},{3,2},{4,5},{5,4},{6,7},{7,6},{8,9},{9,8},{10,11... | collective-permute-start | bytes 786440 | tf_op jit(solution)/shard_map/ppermute | solution.py:51
  34.8 3.7 %collective-permute-start.12 = (bf16[128,1024]{1,0:T(8,128)(2,1)S(1)}, bf16[128,1024]{1,0:T(8,128)(2,1)S(1)}, u32[]{:S(2)}, u32[]{:S(2)}) collective-permute-start(bf16[128,1024]{1,0:T(8,128)(2,1)S(1)} %collective-permute-done.7.refs_3_), channel_id=1, source_target_pairs={{0,1},{1,0},{2,3},{3,2},{4,5},{5,4},{6,7},{7,6},{8,9},{9,8},{10,11... | collective-permute-start | bytes 786440 | tf_op jit(solution)/shard_map/ppermute | solution.py:51
  40.1 1.3 %collective-permute-start.13 = (f32[8,128]{1,0:T(8,128)S(1)}, f32[8,128]{1,0:T(8,128)S(1)}, u32[]{:S(2)}, u32[]{:S(2)}) collective-permute-start(f32[8,128]{1,0:T(8,128)S(1)} %get-tuple-element.34.mine), channel_id=1, source_target_pairs={{0,1},{1,0},{2,3},{3,2},{4,5},{5,4},{6,7},{7,6},{8,9},{9,8},{10,11... | collective-permute-start | bytes 12296 | tf_op jit(solution)/shard_map/ppermute | solution.py:51
  58.2 18.7 %copy-start.5 = (f32[768]{0:T(1024)S(1)}, f32[768]{0:T(1024)}, u32[]{:S(2)}) copy-start(f32[768]{0:T(1024)} %param.7) | copy-start | bytes 9220
  99.4 6.9 %copy-start = (bf16[32,32,768]{2,1,0:T(8,128)(2,1)}, bf16[32,32,768]{2,1,0:T(8,128)(2,1)S(1)}, u32[]{:S(2)}) copy-start(bf16[32,32,768]{2,1,0:T(8,128)(2,1)S(1)} %broadcast_in_dim.5._) | copy-start | bytes 4718596
  99.5 6.1 %collective-permute-start.14 = (f32[56,128]{1,0:T(8,128)S(1)}, f32[56,128]{1,0:T(8,128)S(1)}, u32[]{:S(2)}, u32[]{:S(2)}) collective-permute-start(f32[56,128]{1,0:T(8,128)S(1)} %last.1.mine), channel_id=1, source_target_pairs={{0,1},{1,0},{2,3},{3,2},{4,5},{5,4},{6,7},{7,6},{8,9},{9,8},{10,11... | collective-permute-start | bytes 86024 | tf_op jit(solution)/shard_map/ppermute | solution.py:51

commit v6 on v5

--- a/solution.py
+++ b/solution.py
@@ -77,19 +77,19 @@
     return jnp.concatenate([gain[k : k + 1, :] for k in range(D // 128)], axis=1)
 
 
-def norm_kernel(features, places, gain, own, scaled, radius):
+def norm_kernel(features, positives, gain, own, scaled, radius):
     for n in range(0, OWN, 8):
         at = slice(n, n + 8)
         pooled = jnp.sum(features[at].astype(f32), axis=1) * (1.0 / WIN)
         size = jnp.sqrt(jnp.mean(pooled * pooled, axis=-1, keepdims=True) + norm_eps)
         radius[at, :] = size
         scaled[at, :] = pooled / size
-    value = (scaled[...] * flat(gain)).astype(b16)
-    place = places[...]
-    lane = lax.broadcasted_iota(jnp.int32, place.shape, 1)
-    marks = jnp.where(lane == 0, place >> 7, place & 127).astype(f32).astype(b16)
-    own[:, :D] = value
-    own[:, D:] = marks
+    own[:, :D] = (scaled[...] * flat(gain)).astype(b16)
+    row = lax.broadcasted_iota(jnp.int32, (OWN, OWN), 0)
+    col = lax.broadcasted_iota(jnp.int32, (OWN, OWN), 1)
+    place = jnp.sum(jnp.where(row == col, positives[...], 0), axis=1, keepdims=True)
+    lane = lax.broadcasted_iota(jnp.int32, (OWN, MARK), 1)
+    own[:, D:] = jnp.where(lane == 0, place >> 7, place & 127).astype(f32).astype(b16)
 
 
 def position():
@@ -237,14 +237,14 @@
     loss[...] = total[54:55, :] * (1.0 / (2.0 * OWN * NROW * NCOL))
 
 
-def call(kernel, out, ins, name, outs=None, **options):
+def call(kernel, out, ins, name, outs=None, limit=LIMIT, **options):
     out_specs = [SPACES[k] for k in outs or "V" * (len(out) if isinstance(out, list) else 1)]
     return pl.pallas_call(
         kernel,
         out_shape=out,
         in_specs=[SPACES[k] for k in ins],
         out_specs=out_specs if isinstance(out, list) else out_specs[0],
-        compiler_params=pltpu.CompilerParams(vmem_limit_bytes=LIMIT),
+        compiler_params=pltpu.CompilerParams(vmem_limit_bytes=limit),
         name=name,
         **options,
     )
@@ -256,7 +256,6 @@
     mine = call(teacher_kernel, shaped(OWN, E, dtype=b16), "V", "teacher")(teacher)
     mine = jnp.concatenate([mine] + [along(mine, "zh", k) for k in (3, 2, 1)], axis=0)
 
-    places = jnp.broadcast_to(positives[:, None], (OWN, MARK))
     gain = gain.reshape(D // 128, 128)
     own, scaled, radius = call(
         norm_kernel,
@@ -267,7 +266,7 @@
         ],
         "VVV",
         "norm",
-    )(features, places, gain)
+    )(features, positives[None], gain)
 
     mine, own = lax.optimization_barrier((mine, own))
     up, down = along(mine, "y", 1), along(mine, "y", 3)
@@ -275,6 +274,8 @@
 
     four = jnp.concatenate([own, other(own, "zl")], axis=0)
     four = jnp.concatenate([four, across(four, 1)], axis=0)
+    rest = across(four, 3)
+    far, rest = lax.optimization_barrier((far, rest))
     rows, student, unit, length = call(
         student_kernel,
         [shaped(SIDE, D + MARK, dtype=b16), shaped(SIDE, E, dtype=b16)]
@@ -282,8 +283,7 @@
         "VVV",
         "student",
         scratch_shapes=[pltpu.VMEM((SIDE, E), f32), pltpu.VMEM((SIDE, 1), f32)],
-    )(four, across(four, 3), w_head)
-    far, student = lax.optimization_barrier((far, student))
+    )(four, rest, w_head)
     blocks = [mine, up, down, far]
     blocks += [other(block, "c") for block in blocks]
 

time: 107 us -> 106 us (level)
    unnamed x14 -> x16, local copies, waits for them, and re-layouts: 2.96 us -> 3.61 us
  transfers between devices with their start and end apart: 15 -> 15, of which waited for: 8 -> 8; matrix products, arithmetic and copies ran while one was open for 1% -> 0% of each run, Pallas kernels for 1% -> 1%
where the time goes in v6:
time: 106 us; the launch traced here: 105 us
  blocking collectives  54.8 us (52%)
  starting transfers between devices  29.8 us (28%)
  waiting for transfers between devices  10.1 us (10%)
  Pallas kernels  6.18 us (6%)
  local copies, waits for them, and re-layouts  3.74 us (4%)
    all_to_all x4, blocking collectives, swap(): return lax.all_to_all(blocks, axes, 0, 0, tiled=True)  54.8 us
    ppermute x6, starting transfers between devices, along(): return lax.ppermute(block, axis, [(i, (i + step) % 4) for i in range(4)])  15.5 us
    ppermute x7, starting transfers between devices, other(): return lax.ppermute(block, axis, [(0, 1), (1, 0)])  10.4 us
    ppermute x6, waiting for transfers between devices, along(): return lax.ppermute(block, axis, [(i, (i + step) % 4) for i in range(4)])  4.56 us
    ppermute x2, starting transfers between devices, across(): return lax.ppermute(block, 'x', [(i, i ^ flip) for i in range(4)])  3.86 us
    ppermute x7, waiting for transfers between devices, other(): return lax.ppermute(block, axis, [(0, 1), (1, 0)])  3.68 us
    unnamed x16, local copies, waits for them, and re-layouts  3.61 us
  transfers between devices with their start and end apart: 15, of which 8 were waited for; matrix products, arithmetic and copies ran while one was open for 0% of the time, Pallas kernels for 1%

profile of v6, /device:TPU:1, one launch (start us, length us, event | category | flops | bytes accessed | tf_op | source)
XLA Modules:
  0.0 105.4 jit_solution(2843022578612092378)
XLA Ops:
  0.6 0.0 copy-start.3
  0.6 0.8 copy-done.3
  1.5 0.0 copy-start.1
  1.5 0.1 teacher.2
  1.6 3.9 %collective-permute-start.2 = (bf16[32,1024]{1,0:T(8,128)(2,1)S(1)}, bf16[32,1024]{1,0:T(8,128)(2,1)S(1)}, u32[]{:S(2)}, u32[]{:S(2)}) collective-permute-start(bf16[32,1024]{1,0:T(8,128)(2,1)S(1)} %teacher.2), channel_id=1, source_target_pairs={{0,64},{64,128},{128,192},{192,0},{1,65},{65,129},{129,193},{193,1... | collective-permute-start | bytes 196616 | tf_op jit(solution)/shard_map/ppermute | solution.py:55
  5.5 5.1 %collective-permute-start.1 = (bf16[32,1024]{1,0:T(8,128)(2,1)S(1)}, bf16[32,1024]{1,0:T(8,128)(2,1)S(1)}, u32[]{:S(2)}, u32[]{:S(2)}) collective-permute-start(bf16[32,1024]{1,0:T(8,128)(2,1)S(1)} %teacher.2), channel_id=1, source_target_pairs={{0,128},{64,192},{128,0},{192,64},{1,129},{65,193},{129,1},{193,65... | collective-permute-start | bytes 196616 | tf_op jit(solution)/shard_map/ppermute | solution.py:55
  10.6 2.4 %collective-permute-start = (bf16[32,1024]{1,0:T(8,128)(2,1)S(1)}, bf16[32,1024]{1,0:T(8,128)(2,1)S(1)}, u32[]{:S(2)}, u32[]{:S(2)}) collective-permute-start(bf16[32,1024]{1,0:T(8,128)(2,1)S(1)} %teacher.2), channel_id=1, source_target_pairs={{0,192},{64,0},{128,64},{192,128},{1,193},{65,1},{129,65},{193,129... | collective-permute-start | bytes 196616 | tf_op jit(solution)/shard_map/ppermute | solution.py:55
  13.0 0.0 copy-start.2
  13.0 1.4 %copy-done.2 = bf16[32,32,768]{2,1,0:T(8,128)(2,1)S(1)} copy-done((bf16[32,32,768]{2,1,0:T(8,128)(2,1)S(1)}, bf16[32,32,768]{2,1,0:T(8,128)(2,1)}, u32[]{:S(2)}) %copy-start.2) | copy-done | bytes 1572888
  14.4 0.0 copy-start.4
  14.4 0.7 copy-done.4
  15.1 0.0 copy-start.6
  15.1 0.7 copy-done.6
  15.7 0.5 norm.1
  16.3 0.0 collective-permute-done.2
  16.3 0.0 collective-permute-done.1
  16.3 2.0 %collective-permute-done = bf16[32,1024]{1,0:T(8,128)(2,1)S(1)} collective-permute-done((bf16[32,1024]{1,0:T(8,128)(2,1)S(1)}, bf16[32,1024]{1,0:T(8,128)(2,1)S(1)}, u32[]{:S(2)}, u32[]{:S(2)}) %collective-permute-start) | collective-permute-done | bytes 65568 | tf_op jit(solution)/shard_map/ppermute | solution.py:55
  18.3 0.1 collective-permute-start.3
  18.4 1.4 %collective-permute-start.5 = (bf16[128,1024]{1,0:T(8,128)(2,1)S(1)}, bf16[128,1024]{1,0:T(8,128)(2,1)S(1)}, u32[]{:S(2)}, u32[]{:S(2)}) collective-permute-start(bf16[128,1024]{1,0:T(8,128)(2,1)S(1)} %pad_maximum_fusion.refs_0_), channel_id=1, source_target_pairs={{0,16},{16,32},{32,48},{48,0},{1,17},{17,33},{33,49},{49,1},{2,18}... | collective-permute-start | bytes 786440 | tf_op jit(solution)/shard_map/ppermute | solution.py:55
  19.8 1.6 %collective-permute-done.3 = bf16[32,896]{1,0:T(8,128)(2,1)S(1)} collective-permute-done((bf16[32,896]{1,0:T(8,128)(2,1)S(1)}, bf16[32,896]{1,0:T(8,128)(2,1)S(1)}, u32[]{:S(2)}, u32[]{:S(2)}) %collective-permute-start.3) | collective-permute-done | bytes 57376 | tf_op jit(solution)/shard_map/ppermute | solution.py:51
  21.4 1.3 %collective-permute-start.4 = (bf16[64,896]{1,0:T(8,128)(2,1)S(1)}, bf16[64,896]{1,0:T(8,128)(2,1)S(1)}, u32[]{:S(2)}, u32[]{:S(2)}) collective-permute-start(bf16[64,896]{1,0:T(8,128)(2,1)S(1)} %pad_maximum_fusion.1), channel_id=1, source_target_pairs={{0,4},{4,0},{8,12},{12,8},{1,5},{5,1},{9,13},{13,9},{2,6},{6,2},{1... | collective-permute-start | bytes 344072 | tf_op jit(solution)/shard_map/ppermute | solution.py:59
  22.7 2.7 %collective-permute-start.8 = (bf16[128,1024]{1,0:T(8,128)(2,1)S(1)}, bf16[128,1024]{1,0:T(8,128)(2,1)S(1)}, u32[]{:S(2)}, u32[]{:S(2)}) collective-permute-start(bf16[128,1024]{1,0:T(8,128)(2,1)S(1)} %pad_maximum_fusion.refs_0_), channel_id=1, source_target_pairs={{0,48},{16,0},{32,16},{48,32},{1,49},{17,1},{33,17},{49,33},{2,50}... | collective-permute-start | bytes 786440 | tf_op jit(solution)/shard_map/ppermute | solution.py:55
  25.5 1.7 %collective-permute-done.5.refs_1_ = bf16[128,1024]{1,0:T(8,128)(2,1)S(1)} collective-permute-done((bf16[128,1024]{1,0:T(8,128)(2,1)S(1)}, bf16[128,1024]{1,0:T(8,128)(2,1)S(1)}, u32[]{:S(2)}, u32[]{:S(2)}) %collective-permute-start.5) | collective-permute-done | bytes 262176 | tf_op jit(solution)/shard_map/ppermute | solution.py:55
  27.2 0.0 collective-permute-start.6
  27.2 0.0 collective-permute-done.4
  27.2 2.6 %collective-permute-start.7 = (bf16[128,896]{1,0:T(8,128)(2,1)S(1)}, bf16[128,896]{1,0:T(8,128)(2,1)S(1)}, u32[]{:S(2)}, u32[]{:S(2)}) collective-permute-start(bf16[128,896]{1,0:T(8,128)(2,1)S(1)} %constant_dynamic-update-slice_fusion.four), channel_id=1, source_target_pairs={{0,12},{4,8},{8,4},{12,0},{1,13},{5,9},{9,5},{13,1},{2,14},{6,10},... | collective-permute-start | bytes 688136 | tf_op jit(solution)/shard_map/ppermute | solution.py:59
  29.8 1.9 %collective-permute-start.9 = (bf16[128,1024]{1,0:T(8,128)(2,1)S(1)}, bf16[128,1024]{1,0:T(8,128)(2,1)S(1)}, u32[]{:S(2)}, u32[]{:S(2)}) collective-permute-start(bf16[128,1024]{1,0:T(8,128)(2,1)S(1)} %pad_maximum_fusion.refs_0_), channel_id=1, source_target_pairs={{0,1},{1,0},{2,3},{3,2},{4,5},{5,4},{6,7},{7,6},{8,9},{9,8},{10,11... | collective-permute-start | bytes 786440 | tf_op jit(solution)/shard_map/ppermute | solution.py:51
  31.6 0.0 collective-permute-start.10
  31.6 0.0 collective-permute-done.8.refs_2_
  31.6 0.5 collective-permute-start.11
  32.1 1.9 %collective-permute-done.7.rest = bf16[128,896]{1,0:T(8,128)(2,1)S(1)} collective-permute-done((bf16[128,896]{1,0:T(8,128)(2,1)S(1)}, bf16[128,896]{1,0:T(8,128)(2,1)S(1)}, u32[]{:S(2)}, u32[]{:S(2)}) %collective-permute-start.7) | collective-permute-done | bytes 229408 | tf_op jit(solution)/shard_map/ppermute | solution.py:59
  34.0 0.9 collective-permute-done.6.refs_3_
  34.9 2.2 %collective-permute-start.12 = (bf16[128,1024]{1,0:T(8,128)(2,1)S(1)}, bf16[128,1024]{1,0:T(8,128)(2,1)S(1)}, u32[]{:S(2)}, u32[]{:S(2)}) collective-permute-start(bf16[128,1024]{1,0:T(8,128)(2,1)S(1)} %collective-permute-done.6.refs_3_), channel_id=1, source_target_pairs={{0,1},{1,0},{2,3},{3,2},{4,5},{5,4},{6,7},{7,6},{8,9},{9,8},{10,11... | collective-permute-start | bytes 786440 | tf_op jit(solution)/shard_map/ppermute | solution.py:51
  37.1 0.0 copy-done.1
  37.1 0.8 student.1
  37.9 0.0 collective-permute-done.9.refs_4_
  37.9 0.0 collective-permute-done.11.refs_6_
  37.9 0.0 collective-permute-done.10.refs_5_
  37.9 0.4 collective-permute-done.12.refs_7_
  38.3 1.6 %scores.1 = (bf16[1024,1024]{1,0:T(8,128)(2,1)S(1)}, bf16[256,1024]{1,0:T(8,128)(2,1)S(1)}, bf16[256,2176]{1,0:T(8,128)(2,1)S(1)}, f32[8,128]{1,0:T(8,128)S(1)}, f32[1,128]{1,0:T(1,128)S(1)}) custom-call(bf16[256,1024]{1,0:T(8,128)(2,1)S(1)} %get-tuple-element.32.student, bf16[256,896]{1,0:T(8,128)(2,1)S(1)} %get-tuple-element.31.rows, ...), custom_call_target="tpu_custom_call" | custom-call | tf_op jit(solution)/shard_map/scores/pallas_call | solution.py:291
  39.9 0.5 collective-permute-start.13
  40.4 0.8 collective-permute-done.13.pair
  41.2 15.0 %all_to_all.20.col_in = f32[16,8,128]{2,1,0:T(8,128)S(1)} all-to-all(f32[16,8,128]{2,1,0:T(8,128)S(1)} %cols.1), channel_id=1, replica_groups=mesh['zh'=4,'y'=4,'x'=4,'zl'=2,'c'=2] {'zh','y'}, dimensions={0} | all-to-all | bytes 131072 | tf_op jit(solution)/shard_map/all_to_all | solution.py:42
  56.2 1.2 %scaled.1 = (bf16[256,2176]{1,0:T(8,128)(2,1)S(1)}, f32[1,128]{1,0:T(1,128)S(1)}) custom-call(bf16[256,896]{1,0:T(8,128)(2,1)S(1)} %get-tuple-element.31.rows, f32[16,8,128]{2,1,0:T(8,128)S(1)} %all_to_all.20.col_in, f32[1,128]{1,0:T(1,128)S(1)} %get-tuple-element.35.pos_part, ...), custom_call_target="tpu_custom_call", output_to_operand_aliasing={{0}: (5, {})} | custom-call | tf_op jit(solution)/shard_map/scaled/pallas_call | solution.py:300
  57.4 0.0 copy-start.5
  57.4 18.7 %all_to_all.21.terms = bf16[8,32,2176]{2,1,0:T(8,128)(2,1)S(1)} all-to-all(bf16[8,32,2176]{2,1,0:T(8,128)(2,1)S(1)} %bitcast.6), channel_id=1, replica_groups=mesh['zh'=4,'y'=4,'x'=4,'zl'=2,'c'=2] {'x','zl'}, dimensions={0} | all-to-all | bytes 2228224 | tf_op jit(solution)/shard_map/all_to_all | solution.py:42
  76.0 0.0 copy-done.5
  76.0 0.9 rows.1
  76.9 8.1 %all_to_all.22.back = bf16[8,48,128]{2,1,0:T(8,128)(2,1)S(1)} all-to-all(bf16[8,48,128]{2,1,0:T(8,128)(2,1)S(1)} %get-tuple-element.45), channel_id=1, replica_groups=mesh['zh'=4,'y'=4,'x'=4,'zl'=2,'c'=2] {'x','zl'}, dimensions={0} | all-to-all | bytes 196608 | tf_op jit(solution)/shard_map/all_to_all | solution.py:42
  85.0 0.3 head.5
  85.3 13.1 %all_to_all.23.back = bf16[16,64,128]{2,1,0:T(8,128)(2,1)S(1)} all-to-all(bf16[16,64,128]{2,1,0:T(8,128)(2,1)S(1)} %head.5), channel_id=1, replica_groups=mesh['zh'=4,'y'=4,'x'=4,'zl'=2,'c'=2] {'zh','y'}, dimensions={0} | all-to-all | bytes 524288 | tf_op jit(solution)/shard_map/all_to_all | solution.py:42
  98.4 0.1 broadcast_in_dim.10._
  98.5 0.0 copy-start
  98.6 5.3 %collective-permute-start.14 = (f32[56,128]{1,0:T(8,128)S(1)}, f32[56,128]{1,0:T(8,128)S(1)}, u32[]{:S(2)}, u32[]{:S(2)}) collective-permute-start(f32[56,128]{1,0:T(8,128)S(1)} %last.1.mine), channel_id=1, source_target_pairs={{0,1},{1,0},{2,3},{3,2},{4,5},{5,4},{6,7},{7,6},{8,9},{9,8},{10,11... | collective-permute-start | bytes 86024 | tf_op jit(solution)/shard_map/ppermute | solution.py:51
  103.9 0.9 collective-permute-done.14.pair
  104.7 0.7 out.1
  105.4 0.0 copy-done
  (7 shorter events, 0.1 us)
Async XLA Ops:
  0.6 0.8 copy-start.3
  1.5 35.6 %copy-start.1 = (bf16[768,1024]{1,0:T(8,128)(2,1)S(1)}, bf16[768,1024]{1,0:T(8,128)(2,1)}, u32[]{:S(2)}) copy-start(bf16[768,1024]{1,0:T(8,128)(2,1)} %head.4) | copy-start | bytes 4718596
  1.6 14.7 %collective-permute-start.2 = (bf16[32,1024]{1,0:T(8,128)(2,1)S(1)}, bf16[32,1024]{1,0:T(8,128)(2,1)S(1)}, u32[]{:S(2)}, u32[]{:S(2)}) collective-permute-start(bf16[32,1024]{1,0:T(8,128)(2,1)S(1)} %teacher.2), channel_id=1, source_target_pairs={{0,64},{64,128},{128,192},{192,0},{1,65},{65,129},{129,193},{193,1... | collective-permute-start | bytes 196616 | tf_op jit(solution)/shard_map/ppermute | solution.py:55
  5.5 10.8 %collective-permute-start.1 = (bf16[32,1024]{1,0:T(8,128)(2,1)S(1)}, bf16[32,1024]{1,0:T(8,128)(2,1)S(1)}, u32[]{:S(2)}, u32[]{:S(2)}) collective-permute-start(bf16[32,1024]{1,0:T(8,128)(2,1)S(1)} %teacher.2), channel_id=1, source_target_pairs={{0,128},{64,192},{128,0},{192,64},{1,129},{65,193},{129,1},{193,65... | collective-permute-start | bytes 196616 | tf_op jit(solution)/shard_map/ppermute | solution.py:55
  10.6 7.7 %collective-permute-start = (bf16[32,1024]{1,0:T(8,128)(2,1)S(1)}, bf16[32,1024]{1,0:T(8,128)(2,1)S(1)}, u32[]{:S(2)}, u32[]{:S(2)}) collective-permute-start(bf16[32,1024]{1,0:T(8,128)(2,1)S(1)} %teacher.2), channel_id=1, source_target_pairs={{0,192},{64,0},{128,64},{192,128},{1,193},{65,1},{129,65},{193,129... | collective-permute-start | bytes 196616 | tf_op jit(solution)/shard_map/ppermute | solution.py:55
  13.0 1.4 %copy-start.2 = (bf16[32,32,768]{2,1,0:T(8,128)(2,1)S(1)}, bf16[32,32,768]{2,1,0:T(8,128)(2,1)}, u32[]{:S(2)}) copy-start(bf16[32,32,768]{2,1,0:T(8,128)(2,1)} %features.1) | copy-start | bytes 4718596
  14.4 0.7 copy-start.4
  15.1 0.7 copy-start.6
  18.3 3.1 %collective-permute-start.3 = (bf16[32,896]{1,0:T(8,128)(2,1)S(1)}, bf16[32,896]{1,0:T(8,128)(2,1)S(1)}, u32[]{:S(2)}, u32[]{:S(2)}) collective-permute-start(bf16[32,896]{1,0:T(8,128)(2,1)S(1)} %get-tuple-element.28), channel_id=1, source_target_pairs={{0,2},{2,0},{1,3},{3,1},{4,6},{6,4},{5,7},{7,5},{8,10},{10,8},{9,1... | collective-permute-start | bytes 172040 | tf_op jit(solution)/shard_map/ppermute | solution.py:51
  18.4 8.8 %collective-permute-start.5 = (bf16[128,1024]{1,0:T(8,128)(2,1)S(1)}, bf16[128,1024]{1,0:T(8,128)(2,1)S(1)}, u32[]{:S(2)}, u32[]{:S(2)}) collective-permute-start(bf16[128,1024]{1,0:T(8,128)(2,1)S(1)} %pad_maximum_fusion.refs_0_), channel_id=1, source_target_pairs={{0,16},{16,32},{32,48},{48,0},{1,17},{17,33},{33,49},{49,1},{2,18}... | collective-permute-start | bytes 786440 | tf_op jit(solution)/shard_map/ppermute | solution.py:55
  21.4 5.8 %collective-permute-start.4 = (bf16[64,896]{1,0:T(8,128)(2,1)S(1)}, bf16[64,896]{1,0:T(8,128)(2,1)S(1)}, u32[]{:S(2)}, u32[]{:S(2)}) collective-permute-start(bf16[64,896]{1,0:T(8,128)(2,1)S(1)} %pad_maximum_fusion.1), channel_id=1, source_target_pairs={{0,4},{4,0},{8,12},{12,8},{1,5},{5,1},{9,13},{13,9},{2,6},{6,2},{1... | collective-permute-start | bytes 344072 | tf_op jit(solution)/shard_map/ppermute | solution.py:59
  22.7 8.9 %collective-permute-start.8 = (bf16[128,1024]{1,0:T(8,128)(2,1)S(1)}, bf16[128,1024]{1,0:T(8,128)(2,1)S(1)}, u32[]{:S(2)}, u32[]{:S(2)}) collective-permute-start(bf16[128,1024]{1,0:T(8,128)(2,1)S(1)} %pad_maximum_fusion.refs_0_), channel_id=1, source_target_pairs={{0,48},{16,0},{32,16},{48,32},{1,49},{17,1},{33,17},{49,33},{2,50}... | collective-permute-start | bytes 786440 | tf_op jit(solution)/shard_map/ppermute | solution.py:55
  27.2 7.7 %collective-permute-start.6 = (bf16[128,1024]{1,0:T(8,128)(2,1)S(1)}, bf16[128,1024]{1,0:T(8,128)(2,1)S(1)}, u32[]{:S(2)}, u32[]{:S(2)}) collective-permute-start(bf16[128,1024]{1,0:T(8,128)(2,1)S(1)} %collective-permute-done.5.refs_1_), channel_id=1, source_target_pairs={{0,16},{16,32},{32,48},{48,0},{1,17},{17,33},{33,49},{49,1},{2,18}... | collective-permute-start | bytes 786440 | tf_op jit(solution)/shard_map/ppermute | solution.py:55
  27.2 6.8 %collective-permute-start.7 = (bf16[128,896]{1,0:T(8,128)(2,1)S(1)}, bf16[128,896]{1,0:T(8,128)(2,1)S(1)}, u32[]{:S(2)}, u32[]{:S(2)}) collective-permute-start(bf16[128,896]{1,0:T(8,128)(2,1)S(1)} %constant_dynamic-update-slice_fusion.four), channel_id=1, source_target_pairs={{0,12},{4,8},{8,4},{12,0},{1,13},{5,9},{9,5},{13,1},{2,14},{6,10},... | collective-permute-start | bytes 688136 | tf_op jit(solution)/shard_map/ppermute | solution.py:59
  29.8 8.1 %collective-permute-start.9 = (bf16[128,1024]{1,0:T(8,128)(2,1)S(1)}, bf16[128,1024]{1,0:T(8,128)(2,1)S(1)}, u32[]{:S(2)}, u32[]{:S(2)}) collective-permute-start(bf16[128,1024]{1,0:T(8,128)(2,1)S(1)} %pad_maximum_fusion.refs_0_), channel_id=1, source_target_pairs={{0,1},{1,0},{2,3},{3,2},{4,5},{5,4},{6,7},{7,6},{8,9},{9,8},{10,11... | collective-permute-start | bytes 786440 | tf_op jit(solution)/shard_map/ppermute | solution.py:51
  31.6 6.3 %collective-permute-start.10 = (bf16[128,1024]{1,0:T(8,128)(2,1)S(1)}, bf16[128,1024]{1,0:T(8,128)(2,1)S(1)}, u32[]{:S(2)}, u32[]{:S(2)}) collective-permute-start(bf16[128,1024]{1,0:T(8,128)(2,1)S(1)} %collective-permute-done.5.refs_1_), channel_id=1, source_target_pairs={{0,1},{1,0},{2,3},{3,2},{4,5},{5,4},{6,7},{7,6},{8,9},{9,8},{10,11... | collective-permute-start | bytes 786440 | tf_op jit(solution)/shard_map/ppermute | solution.py:51
  31.6 6.3 %collective-permute-start.11 = (bf16[128,1024]{1,0:T(8,128)(2,1)S(1)}, bf16[128,1024]{1,0:T(8,128)(2,1)S(1)}, u32[]{:S(2)}, u32[]{:S(2)}) collective-permute-start(bf16[128,1024]{1,0:T(8,128)(2,1)S(1)} %collective-permute-done.8.refs_2_), channel_id=1, source_target_pairs={{0,1},{1,0},{2,3},{3,2},{4,5},{5,4},{6,7},{7,6},{8,9},{9,8},{10,11... | collective-permute-start | bytes 786440 | tf_op jit(solution)/shard_map/ppermute | solution.py:51
  34.9 3.4 %collective-permute-start.12 = (bf16[128,1024]{1,0:T(8,128)(2,1)S(1)}, bf16[128,1024]{1,0:T(8,128)(2,1)S(1)}, u32[]{:S(2)}, u32[]{:S(2)}) collective-permute-start(bf16[128,1024]{1,0:T(8,128)(2,1)S(1)} %collective-permute-done.6.refs_3_), channel_id=1, source_target_pairs={{0,1},{1,0},{2,3},{3,2},{4,5},{5,4},{6,7},{7,6},{8,9},{9,8},{10,11... | collective-permute-start | bytes 786440 | tf_op jit(solution)/shard_map/ppermute | solution.py:51
  39.9 1.3 %collective-permute-start.13 = (f32[8,128]{1,0:T(8,128)S(1)}, f32[8,128]{1,0:T(8,128)S(1)}, u32[]{:S(2)}, u32[]{:S(2)}) collective-permute-start(f32[8,128]{1,0:T(8,128)S(1)} %get-tuple-element.34.mine), channel_id=1, source_target_pairs={{0,1},{1,0},{2,3},{3,2},{4,5},{5,4},{6,7},{7,6},{8,9},{9,8},{10,11... | collective-permute-start | bytes 12296 | tf_op jit(solution)/shard_map/ppermute | solution.py:51
  57.4 18.7 %copy-start.5 = (f32[768]{0:T(1024)S(1)}, f32[768]{0:T(1024)}, u32[]{:S(2)}) copy-start(f32[768]{0:T(1024)} %param.7) | copy-start | bytes 9220
  98.5 6.9 %copy-start = (bf16[32,32,768]{2,1,0:T(8,128)(2,1)}, bf16[32,32,768]{2,1,0:T(8,128)(2,1)S(1)}, u32[]{:S(2)}) copy-start(bf16[32,32,768]{2,1,0:T(8,128)(2,1)S(1)} %broadcast_in_dim.10._) | copy-start | bytes 4718596
  98.6 6.1 %collective-permute-start.14 = (f32[56,128]{1,0:T(8,128)S(1)}, f32[56,128]{1,0:T(8,128)S(1)}, u32[]{:S(2)}, u32[]{:S(2)}) collective-permute-start(f32[56,128]{1,0:T(8,128)S(1)} %last.1.mine), channel_id=1, source_target_pairs={{0,1},{1,0},{2,3},{3,2},{4,5},{5,4},{6,7},{7,6},{8,9},{9,8},{10,11... | collective-permute-start | bytes 86024 | tf_op jit(solution)/shard_map/ppermute | solution.py:51

commit v7 on v6

--- a/solution.py
+++ b/solution.py
@@ -103,9 +103,10 @@
     def slot(x_, zl_):
         return pl.ds(pl.multiple_of((((x_ + 4) & 3) * 2 + zl_) * OWN, OWN), OWN)
 
-    for k, (ref, start) in enumerate(((four, 0), (four, 64), (rest, 64), (rest, 0))):
-        rows[slot(x ^ k, zl), :] = ref[start : start + OWN, :]
-        rows[slot(x ^ k, 1 - zl), :] = ref[start + OWN : start + 2 * OWN, :]
+    for k, x_ in enumerate((x, x ^ 1, x ^ 3, x ^ 2)):
+        at = slice(k * OWN, (k + 1) * OWN)
+        rows[slot(x_, zl), :] = four[at, :]
+        rows[slot(x_, 1 - zl), :] = rest[at, :]
     raw = jnp.dot(rows[:, :D], head[...], preferred_element_type=f32)
     full[...], sizes[...] = unit_rows(raw)
     student[...] = full[...].astype(b16)
@@ -272,9 +273,9 @@
     up, down = along(mine, "y", 1), along(mine, "y", 3)
     far = along(up, "y", 1)
 
-    four = jnp.concatenate([own, other(own, "zl")], axis=0)
-    four = jnp.concatenate([four, across(four, 1)], axis=0)
-    rest = across(four, 3)
+    four = jnp.concatenate([own, across(own, 1)], axis=0)
+    four = jnp.concatenate([four, across(four, 3)], axis=0)
+    rest = other(four, "zl")
     far, rest = lax.optimization_barrier((far, rest))
     rows, student, unit, length = call(
         student_kernel,

time: 106 us -> 104 us (0.981)
  starting transfers between devices: 29.8 us -> 32.7 us
  blocking collectives: 54.8 us -> 52.6 us
  waiting for transfers between devices: 10.1 us -> 8.08 us
    ppermute x7, starting transfers between devices: 10.4 us -> 13.4 us  [other(): return lax.ppermute(block, axis, [(0, 1), (1, 0)])]
    all_to_all x4, blocking collectives: 54.8 us -> 52.6 us  [swap(): return lax.all_to_all(blocks, axes, 0, 0, tiled=True)]
    ppermute x7, waiting for transfers between devices: 3.68 us -> 2.07 us  [other(): return lax.ppermute(block, axis, [(0, 1), (1, 0)])]
    ppermute x2, waiting for transfers between devices: 1.86 us -> 0.52 us  [across(): return lax.ppermute(block, 'x', [(i, i ^ flip) for i in range(4)])]
where the time goes in v7:
time: 104 us
  blocking collectives  52.6 us (51%)
  starting transfers between devices  32.7 us (31%)
  waiting for transfers between devices  8.08 us (8%)
  Pallas kernels  6.17 us (6%)
  local copies, waits for them, and re-layouts  3.74 us (4%)
    all_to_all x4, blocking collectives, swap(): return lax.all_to_all(blocks, axes, 0, 0, tiled=True)  52.6 us
    ppermute x6, starting transfers between devices, along(): return lax.ppermute(block, axis, [(i, (i + step) % 4) for i in range(4)])  15.4 us
    ppermute x7, starting transfers between devices, other(): return lax.ppermute(block, axis, [(0, 1), (1, 0)])  13.4 us
    ppermute x6, waiting for transfers between devices, along(): return lax.ppermute(block, axis, [(i, (i + step) % 4) for i in range(4)])  5.48 us
    ppermute x2, starting transfers between devices, across(): return lax.ppermute(block, 'x', [(i, i ^ flip) for i in range(4)])  3.86 us
    unnamed x16, local copies, waits for them, and re-layouts  3.61 us
  transfers between devices with their start and end apart: 15, of which 8 were waited for; matrix products, arithmetic and copies ran while one was open for 0% of the time, Pallas kernels for 1%

profile of v7, /device:TPU:1, one launch (start us, length us, event | category | flops | bytes accessed | tf_op | source)
XLA Modules:
  0.0 104.1 jit_solution(13069366043185171475)
XLA Ops:
  0.6 0.0 copy-start.3
  0.6 0.8 copy-done.3
  1.5 0.0 copy-start.1
  1.5 0.1 teacher.2
  1.6 3.9 %collective-permute-start.2 = (bf16[32,1024]{1,0:T(8,128)(2,1)S(1)}, bf16[32,1024]{1,0:T(8,128)(2,1)S(1)}, u32[]{:S(2)}, u32[]{:S(2)}) collective-permute-start(bf16[32,1024]{1,0:T(8,128)(2,1)S(1)} %teacher.2), channel_id=1, source_target_pairs={{0,64},{64,128},{128,192},{192,0},{1,65},{65,129},{129,193},{193,1... | collective-permute-start | bytes 196616 | tf_op jit(solution)/shard_map/ppermute | solution.py:55
  5.5 5.1 %collective-permute-start.1 = (bf16[32,1024]{1,0:T(8,128)(2,1)S(1)}, bf16[32,1024]{1,0:T(8,128)(2,1)S(1)}, u32[]{:S(2)}, u32[]{:S(2)}) collective-permute-start(bf16[32,1024]{1,0:T(8,128)(2,1)S(1)} %teacher.2), channel_id=1, source_target_pairs={{0,128},{64,192},{128,0},{192,64},{1,129},{65,193},{129,1},{193,65... | collective-permute-start | bytes 196616 | tf_op jit(solution)/shard_map/ppermute | solution.py:55
  10.6 2.4 %collective-permute-start = (bf16[32,1024]{1,0:T(8,128)(2,1)S(1)}, bf16[32,1024]{1,0:T(8,128)(2,1)S(1)}, u32[]{:S(2)}, u32[]{:S(2)}) collective-permute-start(bf16[32,1024]{1,0:T(8,128)(2,1)S(1)} %teacher.2), channel_id=1, source_target_pairs={{0,192},{64,0},{128,64},{192,128},{1,193},{65,1},{129,65},{193,129... | collective-permute-start | bytes 196616 | tf_op jit(solution)/shard_map/ppermute | solution.py:55
  13.0 0.0 copy-start.2
  13.0 1.4 %copy-done.2 = bf16[32,32,768]{2,1,0:T(8,128)(2,1)S(1)} copy-done((bf16[32,32,768]{2,1,0:T(8,128)(2,1)S(1)}, bf16[32,32,768]{2,1,0:T(8,128)(2,1)}, u32[]{:S(2)}) %copy-start.2) | copy-done | bytes 1572888
  14.4 0.0 copy-start.4
  14.4 0.7 copy-done.4
  15.1 0.0 copy-start.6
  15.1 0.7 copy-done.6
  15.7 0.5 norm.1
  16.3 0.0 collective-permute-done.2
  16.3 0.0 collective-permute-done.1
  16.3 2.0 %collective-permute-done = bf16[32,1024]{1,0:T(8,128)(2,1)S(1)} collective-permute-done((bf16[32,1024]{1,0:T(8,128)(2,1)S(1)}, bf16[32,1024]{1,0:T(8,128)(2,1)S(1)}, u32[]{:S(2)}, u32[]{:S(2)}) %collective-permute-start) | collective-permute-done | bytes 65568 | tf_op jit(solution)/shard_map/ppermute | solution.py:55
  18.3 1.3 %collective-permute-start.3 = (bf16[32,896]{1,0:T(8,128)(2,1)S(1)}, bf16[32,896]{1,0:T(8,128)(2,1)S(1)}, u32[]{:S(2)}, u32[]{:S(2)}) collective-permute-start(bf16[32,896]{1,0:T(8,128)(2,1)S(1)} %get-tuple-element.28), channel_id=1, source_target_pairs={{0,4},{4,0},{8,12},{12,8},{1,5},{5,1},{9,13},{13,9},{2,6},{6,2},{1... | collective-permute-start | bytes 172040 | tf_op jit(solution)/shard_map/ppermute | solution.py:59
  19.6 1.3 %collective-permute-start.5 = (bf16[128,1024]{1,0:T(8,128)(2,1)S(1)}, bf16[128,1024]{1,0:T(8,128)(2,1)S(1)}, u32[]{:S(2)}, u32[]{:S(2)}) collective-permute-start(bf16[128,1024]{1,0:T(8,128)(2,1)S(1)} %pad_maximum_fusion.refs_0_), channel_id=1, source_target_pairs={{0,16},{16,32},{32,48},{48,0},{1,17},{17,33},{33,49},{49,1},{2,18}... | collective-permute-start | bytes 786440 | tf_op jit(solution)/shard_map/ppermute | solution.py:55
  20.9 0.5 collective-permute-done.3
  21.4 2.6 %collective-permute-start.4 = (bf16[64,896]{1,0:T(8,128)(2,1)S(1)}, bf16[64,896]{1,0:T(8,128)(2,1)S(1)}, u32[]{:S(2)}, u32[]{:S(2)}) collective-permute-start(bf16[64,896]{1,0:T(8,128)(2,1)S(1)} %pad_maximum_fusion.1), channel_id=1, source_target_pairs={{0,12},{4,8},{8,4},{12,0},{1,13},{5,9},{9,5},{13,1},{2,14},{6,10},... | collective-permute-start | bytes 344072 | tf_op jit(solution)/shard_map/ppermute | solution.py:59
  24.0 2.7 %collective-permute-start.8 = (bf16[128,1024]{1,0:T(8,128)(2,1)S(1)}, bf16[128,1024]{1,0:T(8,128)(2,1)S(1)}, u32[]{:S(2)}, u32[]{:S(2)}) collective-permute-start(bf16[128,1024]{1,0:T(8,128)(2,1)S(1)} %pad_maximum_fusion.refs_0_), channel_id=1, source_target_pairs={{0,48},{16,0},{32,16},{48,32},{1,49},{17,1},{33,17},{49,33},{2,50}... | collective-permute-start | bytes 786440 | tf_op jit(solution)/shard_map/ppermute | solution.py:55
  26.7 1.2 %collective-permute-done.5.refs_1_ = bf16[128,1024]{1,0:T(8,128)(2,1)S(1)} collective-permute-done((bf16[128,1024]{1,0:T(8,128)(2,1)S(1)}, bf16[128,1024]{1,0:T(8,128)(2,1)S(1)}, u32[]{:S(2)}, u32[]{:S(2)}) %collective-permute-start.5) | collective-permute-done | bytes 262176 | tf_op jit(solution)/shard_map/ppermute | solution.py:55
  28.0 0.0 collective-permute-start.6
  28.0 0.0 collective-permute-done.4
  28.0 0.1 collective-permute-start.7
  28.1 2.0 %collective-permute-start.9 = (bf16[128,1024]{1,0:T(8,128)(2,1)S(1)}, bf16[128,1024]{1,0:T(8,128)(2,1)S(1)}, u32[]{:S(2)}, u32[]{:S(2)}) collective-permute-start(bf16[128,1024]{1,0:T(8,128)(2,1)S(1)} %pad_maximum_fusion.refs_0_), channel_id=1, source_target_pairs={{0,1},{1,0},{2,3},{3,2},{4,5},{5,4},{6,7},{7,6},{8,9},{9,8},{10,11... | collective-permute-start | bytes 786440 | tf_op jit(solution)/shard_map/ppermute | solution.py:51
  30.1 0.1 collective-permute-start.10
  30.2 0.2 collective-permute-done.8.refs_2_
  30.4 2.9 %collective-permute-start.11 = (bf16[128,1024]{1,0:T(8,128)(2,1)S(1)}, bf16[128,1024]{1,0:T(8,128)(2,1)S(1)}, u32[]{:S(2)}, u32[]{:S(2)}) collective-permute-start(bf16[128,1024]{1,0:T(8,128)(2,1)S(1)} %collective-permute-done.8.refs_2_), channel_id=1, source_target_pairs={{0,1},{1,0},{2,3},{3,2},{4,5},{5,4},{6,7},{7,6},{8,9},{9,8},{10,11... | collective-permute-start | bytes 786440 | tf_op jit(solution)/shard_map/ppermute | solution.py:51
  33.2 0.0 collective-permute-done.7.rest
  33.3 2.1 %collective-permute-done.6.refs_3_ = bf16[128,1024]{1,0:T(8,128)(2,1)S(1)} collective-permute-done((bf16[128,1024]{1,0:T(8,128)(2,1)S(1)}, bf16[128,1024]{1,0:T(8,128)(2,1)S(1)}, u32[]{:S(2)}, u32[]{:S(2)}) %collective-permute-start.6) | collective-permute-done | bytes 262176 | tf_op jit(solution)/shard_map/ppermute | solution.py:55
  35.4 2.5 %collective-permute-start.12 = (bf16[128,1024]{1,0:T(8,128)(2,1)S(1)}, bf16[128,1024]{1,0:T(8,128)(2,1)S(1)}, u32[]{:S(2)}, u32[]{:S(2)}) collective-permute-start(bf16[128,1024]{1,0:T(8,128)(2,1)S(1)} %collective-permute-done.6.refs_3_), channel_id=1, source_target_pairs={{0,1},{1,0},{2,3},{3,2},{4,5},{5,4},{6,7},{7,6},{8,9},{9,8},{10,11... | collective-permute-start | bytes 786440 | tf_op jit(solution)/shard_map/ppermute | solution.py:51
  37.9 0.0 copy-done.1
  37.9 0.8 student.1
  38.7 0.0 collective-permute-done.9.refs_4_
  38.7 0.0 collective-permute-done.11.refs_6_
  38.7 0.0 collective-permute-done.10.refs_5_
  38.7 0.4 collective-permute-done.12.refs_7_
  39.1 1.6 %scores.1 = (bf16[1024,1024]{1,0:T(8,128)(2,1)S(1)}, bf16[256,1024]{1,0:T(8,128)(2,1)S(1)}, bf16[256,2176]{1,0:T(8,128)(2,1)S(1)}, f32[8,128]{1,0:T(8,128)S(1)}, f32[1,128]{1,0:T(1,128)S(1)}) custom-call(bf16[256,1024]{1,0:T(8,128)(2,1)S(1)} %get-tuple-element.32.student, bf16[256,896]{1,0:T(8,128)(2,1)S(1)} %get-tuple-element.31.rows, ...), custom_call_target="tpu_custom_call" | custom-call | tf_op jit(solution)/shard_map/scores/pallas_call | solution.py:292
  40.7 0.5 collective-permute-start.13
  41.2 0.8 collective-permute-done.13.pair
  42.0 13.8 %all_to_all.20.col_in = f32[16,8,128]{2,1,0:T(8,128)S(1)} all-to-all(f32[16,8,128]{2,1,0:T(8,128)S(1)} %cols.1), channel_id=1, replica_groups=mesh['zh'=4,'y'=4,'x'=4,'zl'=2,'c'=2] {'zh','y'}, dimensions={0} | all-to-all | bytes 131072 | tf_op jit(solution)/shard_map/all_to_all | solution.py:42
  55.8 1.2 %scaled.1 = (bf16[256,2176]{1,0:T(8,128)(2,1)S(1)}, f32[1,128]{1,0:T(1,128)S(1)}) custom-call(bf16[256,896]{1,0:T(8,128)(2,1)S(1)} %get-tuple-element.31.rows, f32[16,8,128]{2,1,0:T(8,128)S(1)} %all_to_all.20.col_in, f32[1,128]{1,0:T(1,128)S(1)} %get-tuple-element.35.pos_part, ...), custom_call_target="tpu_custom_call", output_to_operand_aliasing={{0}: (5, {})} | custom-call | tf_op jit(solution)/shard_map/scaled/pallas_call | solution.py:301
  57.0 0.0 copy-start.5
  57.0 17.9 %all_to_all.21.terms = bf16[8,32,2176]{2,1,0:T(8,128)(2,1)S(1)} all-to-all(bf16[8,32,2176]{2,1,0:T(8,128)(2,1)S(1)} %bitcast.6), channel_id=1, replica_groups=mesh['zh'=4,'y'=4,'x'=4,'zl'=2,'c'=2] {'x','zl'}, dimensions={0} | all-to-all | bytes 2228224 | tf_op jit(solution)/shard_map/all_to_all | solution.py:42
  74.9 0.0 copy-done.5
  74.9 0.9 rows.1
  75.8 8.2 %all_to_all.22.back = bf16[8,48,128]{2,1,0:T(8,128)(2,1)S(1)} all-to-all(bf16[8,48,128]{2,1,0:T(8,128)(2,1)S(1)} %get-tuple-element.45), channel_id=1, replica_groups=mesh['zh'=4,'y'=4,'x'=4,'zl'=2,'c'=2] {'x','zl'}, dimensions={0} | all-to-all | bytes 196608 | tf_op jit(solution)/shard_map/all_to_all | solution.py:42
  84.0 0.3 head.5
  84.3 12.7 %all_to_all.23.back = bf16[16,64,128]{2,1,0:T(8,128)(2,1)S(1)} all-to-all(bf16[16,64,128]{2,1,0:T(8,128)(2,1)S(1)} %head.5), channel_id=1, replica_groups=mesh['zh'=4,'y'=4,'x'=4,'zl'=2,'c'=2] {'zh','y'}, dimensions={0} | all-to-all | bytes 524288 | tf_op jit(solution)/shard_map/all_to_all | solution.py:42
  97.0 0.1 broadcast_in_dim.10._
  97.1 0.0 copy-start
  97.2 5.3 %collective-permute-start.14 = (f32[56,128]{1,0:T(8,128)S(1)}, f32[56,128]{1,0:T(8,128)S(1)}, u32[]{:S(2)}, u32[]{:S(2)}) collective-permute-start(f32[56,128]{1,0:T(8,128)S(1)} %last.1.mine), channel_id=1, source_target_pairs={{0,1},{1,0},{2,3},{3,2},{4,5},{5,4},{6,7},{7,6},{8,9},{9,8},{10,11... | collective-permute-start | bytes 86024 | tf_op jit(solution)/shard_map/ppermute | solution.py:51
  102.5 0.9 collective-permute-done.14.pair
  103.4 0.7 out.1
  104.0 0.0 copy-done
  (7 shorter events, 0.1 us)
Async XLA Ops:
  0.6 0.8 copy-start.3
  1.5 36.4 %copy-start.1 = (bf16[768,1024]{1,0:T(8,128)(2,1)S(1)}, bf16[768,1024]{1,0:T(8,128)(2,1)}, u32[]{:S(2)}) copy-start(bf16[768,1024]{1,0:T(8,128)(2,1)} %head.4) | copy-start | bytes 4718596
  1.6 14.7 %collective-permute-start.2 = (bf16[32,1024]{1,0:T(8,128)(2,1)S(1)}, bf16[32,1024]{1,0:T(8,128)(2,1)S(1)}, u32[]{:S(2)}, u32[]{:S(2)}) collective-permute-start(bf16[32,1024]{1,0:T(8,128)(2,1)S(1)} %teacher.2), channel_id=1, source_target_pairs={{0,64},{64,128},{128,192},{192,0},{1,65},{65,129},{129,193},{193,1... | collective-permute-start | bytes 196616 | tf_op jit(solution)/shard_map/ppermute | solution.py:55
  5.5 10.8 %collective-permute-start.1 = (bf16[32,1024]{1,0:T(8,128)(2,1)S(1)}, bf16[32,1024]{1,0:T(8,128)(2,1)S(1)}, u32[]{:S(2)}, u32[]{:S(2)}) collective-permute-start(bf16[32,1024]{1,0:T(8,128)(2,1)S(1)} %teacher.2), channel_id=1, source_target_pairs={{0,128},{64,192},{128,0},{192,64},{1,129},{65,193},{129,1},{193,65... | collective-permute-start | bytes 196616 | tf_op jit(solution)/shard_map/ppermute | solution.py:55
  10.6 7.7 %collective-permute-start = (bf16[32,1024]{1,0:T(8,128)(2,1)S(1)}, bf16[32,1024]{1,0:T(8,128)(2,1)S(1)}, u32[]{:S(2)}, u32[]{:S(2)}) collective-permute-start(bf16[32,1024]{1,0:T(8,128)(2,1)S(1)} %teacher.2), channel_id=1, source_target_pairs={{0,192},{64,0},{128,64},{192,128},{1,193},{65,1},{129,65},{193,129... | collective-permute-start | bytes 196616 | tf_op jit(solution)/shard_map/ppermute | solution.py:55
  13.0 1.4 %copy-start.2 = (bf16[32,32,768]{2,1,0:T(8,128)(2,1)S(1)}, bf16[32,32,768]{2,1,0:T(8,128)(2,1)}, u32[]{:S(2)}) copy-start(bf16[32,32,768]{2,1,0:T(8,128)(2,1)} %features.1) | copy-start | bytes 4718596
  14.4 0.7 copy-start.4
  15.1 0.7 copy-start.6
  18.3 3.1 %collective-permute-start.3 = (bf16[32,896]{1,0:T(8,128)(2,1)S(1)}, bf16[32,896]{1,0:T(8,128)(2,1)S(1)}, u32[]{:S(2)}, u32[]{:S(2)}) collective-permute-start(bf16[32,896]{1,0:T(8,128)(2,1)S(1)} %get-tuple-element.28), channel_id=1, source_target_pairs={{0,4},{4,0},{8,12},{12,8},{1,5},{5,1},{9,13},{13,9},{2,6},{6,2},{1... | collective-permute-start | bytes 172040 | tf_op jit(solution)/shard_map/ppermute | solution.py:59
  19.6 8.4 %collective-permute-start.5 = (bf16[128,1024]{1,0:T(8,128)(2,1)S(1)}, bf16[128,1024]{1,0:T(8,128)(2,1)S(1)}, u32[]{:S(2)}, u32[]{:S(2)}) collective-permute-start(bf16[128,1024]{1,0:T(8,128)(2,1)S(1)} %pad_maximum_fusion.refs_0_), channel_id=1, source_target_pairs={{0,16},{16,32},{32,48},{48,0},{1,17},{17,33},{33,49},{49,1},{2,18}... | collective-permute-start | bytes 786440 | tf_op jit(solution)/shard_map/ppermute | solution.py:55
  21.4 6.6 %collective-permute-start.4 = (bf16[64,896]{1,0:T(8,128)(2,1)S(1)}, bf16[64,896]{1,0:T(8,128)(2,1)S(1)}, u32[]{:S(2)}, u32[]{:S(2)}) collective-permute-start(bf16[64,896]{1,0:T(8,128)(2,1)S(1)} %pad_maximum_fusion.1), channel_id=1, source_target_pairs={{0,12},{4,8},{8,4},{12,0},{1,13},{5,9},{9,5},{13,1},{2,14},{6,10},... | collective-permute-start | bytes 344072 | tf_op jit(solution)/shard_map/ppermute | solution.py:59
  24.0 6.4 %collective-permute-start.8 = (bf16[128,1024]{1,0:T(8,128)(2,1)S(1)}, bf16[128,1024]{1,0:T(8,128)(2,1)S(1)}, u32[]{:S(2)}, u32[]{:S(2)}) collective-permute-start(bf16[128,1024]{1,0:T(8,128)(2,1)S(1)} %pad_maximum_fusion.refs_0_), channel_id=1, source_target_pairs={{0,48},{16,0},{32,16},{48,32},{1,49},{17,1},{33,17},{49,33},{2,50}... | collective-permute-start | bytes 786440 | tf_op jit(solution)/shard_map/ppermute | solution.py:55
  28.0 7.4 %collective-permute-start.6 = (bf16[128,1024]{1,0:T(8,128)(2,1)S(1)}, bf16[128,1024]{1,0:T(8,128)(2,1)S(1)}, u32[]{:S(2)}, u32[]{:S(2)}) collective-permute-start(bf16[128,1024]{1,0:T(8,128)(2,1)S(1)} %collective-permute-done.5.refs_1_), channel_id=1, source_target_pairs={{0,16},{16,32},{32,48},{48,0},{1,17},{17,33},{33,49},{49,1},{2,18}... | collective-permute-start | bytes 786440 | tf_op jit(solution)/shard_map/ppermute | solution.py:55
  28.0 5.3 %collective-permute-start.7 = (bf16[128,896]{1,0:T(8,128)(2,1)S(1)}, bf16[128,896]{1,0:T(8,128)(2,1)S(1)}, u32[]{:S(2)}, u32[]{:S(2)}) collective-permute-start(bf16[128,896]{1,0:T(8,128)(2,1)S(1)} %constant_dynamic-update-slice_fusion.four), channel_id=1, source_target_pairs={{0,2},{2,0},{1,3},{3,1},{4,6},{6,4},{5,7},{7,5},{8,10},{10,8},{9,1... | collective-permute-start | bytes 688136 | tf_op jit(solution)/shard_map/ppermute | solution.py:51
  28.1 10.6 %collective-permute-start.9 = (bf16[128,1024]{1,0:T(8,128)(2,1)S(1)}, bf16[128,1024]{1,0:T(8,128)(2,1)S(1)}, u32[]{:S(2)}, u32[]{:S(2)}) collective-permute-start(bf16[128,1024]{1,0:T(8,128)(2,1)S(1)} %pad_maximum_fusion.refs_0_), channel_id=1, source_target_pairs={{0,1},{1,0},{2,3},{3,2},{4,5},{5,4},{6,7},{7,6},{8,9},{9,8},{10,11... | collective-permute-start | bytes 786440 | tf_op jit(solution)/shard_map/ppermute | solution.py:51
  30.1 8.6 %collective-permute-start.10 = (bf16[128,1024]{1,0:T(8,128)(2,1)S(1)}, bf16[128,1024]{1,0:T(8,128)(2,1)S(1)}, u32[]{:S(2)}, u32[]{:S(2)}) collective-permute-start(bf16[128,1024]{1,0:T(8,128)(2,1)S(1)} %collective-permute-done.5.refs_1_), channel_id=1, source_target_pairs={{0,1},{1,0},{2,3},{3,2},{4,5},{5,4},{6,7},{7,6},{8,9},{9,8},{10,11... | collective-permute-start | bytes 786440 | tf_op jit(solution)/shard_map/ppermute | solution.py:51
  30.4 8.3 %collective-permute-start.11 = (bf16[128,1024]{1,0:T(8,128)(2,1)S(1)}, bf16[128,1024]{1,0:T(8,128)(2,1)S(1)}, u32[]{:S(2)}, u32[]{:S(2)}) collective-permute-start(bf16[128,1024]{1,0:T(8,128)(2,1)S(1)} %collective-permute-done.8.refs_2_), channel_id=1, source_target_pairs={{0,1},{1,0},{2,3},{3,2},{4,5},{5,4},{6,7},{7,6},{8,9},{9,8},{10,11... | collective-permute-start | bytes 786440 | tf_op jit(solution)/shard_map/ppermute | solution.py:51
  35.4 3.7 %collective-permute-start.12 = (bf16[128,1024]{1,0:T(8,128)(2,1)S(1)}, bf16[128,1024]{1,0:T(8,128)(2,1)S(1)}, u32[]{:S(2)}, u32[]{:S(2)}) collective-permute-start(bf16[128,1024]{1,0:T(8,128)(2,1)S(1)} %collective-permute-done.6.refs_3_), channel_id=1, source_target_pairs={{0,1},{1,0},{2,3},{3,2},{4,5},{5,4},{6,7},{7,6},{8,9},{9,8},{10,11... | collective-permute-start | bytes 786440 | tf_op jit(solution)/shard_map/ppermute | solution.py:51
  40.7 1.3 %collective-permute-start.13 = (f32[8,128]{1,0:T(8,128)S(1)}, f32[8,128]{1,0:T(8,128)S(1)}, u32[]{:S(2)}, u32[]{:S(2)}) collective-permute-start(f32[8,128]{1,0:T(8,128)S(1)} %get-tuple-element.34.mine), channel_id=1, source_target_pairs={{0,1},{1,0},{2,3},{3,2},{4,5},{5,4},{6,7},{7,6},{8,9},{9,8},{10,11... | collective-permute-start | bytes 12296 | tf_op jit(solution)/shard_map/ppermute | solution.py:51
  57.0 17.9 %copy-start.5 = (f32[768]{0:T(1024)S(1)}, f32[768]{0:T(1024)}, u32[]{:S(2)}) copy-start(f32[768]{0:T(1024)} %param.7) | copy-start | bytes 9220
  97.1 6.9 %copy-start = (bf16[32,32,768]{2,1,0:T(8,128)(2,1)}, bf16[32,32,768]{2,1,0:T(8,128)(2,1)S(1)}, u32[]{:S(2)}) copy-start(bf16[32,32,768]{2,1,0:T(8,128)(2,1)S(1)} %broadcast_in_dim.10._) | copy-start | bytes 4718596
  97.2 6.2 %collective-permute-start.14 = (f32[56,128]{1,0:T(8,128)S(1)}, f32[56,128]{1,0:T(8,128)S(1)}, u32[]{:S(2)}, u32[]{:S(2)}) collective-permute-start(f32[56,128]{1,0:T(8,128)S(1)} %last.1.mine), channel_id=1, source_target_pairs={{0,1},{1,0},{2,3},{3,2},{4,5},{5,4},{6,7},{7,6},{8,9},{9,8},{10,11... | collective-permute-start | bytes 86024 | tf_op jit(solution)/shard_map/ppermute | solution.py:51

commit v8 on v7

--- a/solution.py
+++ b/solution.py
@@ -62,6 +62,10 @@
 def halves(value):
     high = value.astype(b16)
     return high, (value - high.astype(f32)).astype(b16)
+
+
+def joined(value):
+    return jnp.concatenate([half.astype(f32) for half in halves(value)], axis=0).astype(b16)
 
 
 def product(left, right, left_dim, right_dim):
@@ -204,7 +208,7 @@
     loss = loss + jnp.sum(tail[...], axis=1, keepdims=True)
     pieces = [gain_part[:, k * 128 : (k + 1) * 128] for k in range(D // 128)]
     pieces += [jnp.broadcast_to(loss, (1, 128)), jnp.zeros((1, 128), f32)]
-    extra = jnp.concatenate(halves(jnp.concatenate(pieces, axis=0)), axis=0)
+    extra = joined(jnp.concatenate(pieces, axis=0))
     for s in range(NROW):
         sent[s, :OWN, :] = grad_raw[:, s * 128 : (s + 1) * 128]
         sent[s, OWN:, :] = extra
@@ -217,9 +221,8 @@
 def head_kernel(back, rows, sent):
     grad_raw = back[:, :OWN, :].reshape(SIDE, 128)
     head = product(rows[:, :D], grad_raw, 0, 0).astype(b16)
-    extra = jnp.sum(back[:, OWN : OWN + 8, :].astype(f32), axis=0)
-    extra = extra + jnp.sum(back[:, OWN + 8 :, :].astype(f32), axis=0)
-    extra = jnp.concatenate(halves(extra), axis=0)
+    extra = jnp.sum(back[:, OWN:, :].astype(f32), axis=0)
+    extra = joined(extra[:8] + extra[8:])
     for g in range(NCHIP):
         sent[g, :48, :] = head[g * 48 : (g + 1) * 48, :]
         sent[g, 48:, :] = extra

time: 104 us -> 104 us (level)
  no operation moved by 1% of the time
where the time goes in v8:
time: 104 us
  blocking collectives  52.6 us (51%)
  starting transfers between devices  32.7 us (31%)
  waiting for transfers between devices  8.08 us (8%)
  Pallas kernels  6.17 us (6%)
  local copies, waits for them, and re-layouts  3.74 us (4%)
    all_to_all x4, blocking collectives, swap(): return lax.all_to_all(blocks, axes, 0, 0, tiled=True)  52.6 us
    ppermute x6, starting transfers between devices, along(): return lax.ppermute(block, axis, [(i, (i + step) % 4) for i in range(4)])  15.4 us
    ppermute x7, starting transfers between devices, other(): return lax.ppermute(block, axis, [(0, 1), (1, 0)])  13.4 us
    ppermute x6, waiting for transfers between devices, along(): return lax.ppermute(block, axis, [(i, (i + step) % 4) for i in range(4)])  5.48 us
    ppermute x2, starting transfers between devices, across(): return lax.ppermute(block, 'x', [(i, i ^ flip) for i in range(4)])  3.86 us
    unnamed x16, local copies, waits for them, and re-layouts  3.61 us
  transfers between devices with their start and end apart: 15, of which 8 were waited for; matrix products, arithmetic and copies ran while one was open for 0% of the time, Pallas kernels for 1%

profile of v8, /device:TPU:1, one launch (start us, length us, event | category | flops | bytes accessed | tf_op | source)
XLA Modules:
  0.0 104.0 jit_solution(11956004108956389194)
XLA Ops:
  0.6 0.0 copy-start.3
  0.6 0.8 copy-done.3
  1.5 0.0 copy-start.1
  1.5 0.1 teacher.2
  1.6 3.9 %collective-permute-start.2 = (bf16[32,1024]{1,0:T(8,128)(2,1)S(1)}, bf16[32,1024]{1,0:T(8,128)(2,1)S(1)}, u32[]{:S(2)}, u32[]{:S(2)}) collective-permute-start(bf16[32,1024]{1,0:T(8,128)(2,1)S(1)} %teacher.2), channel_id=1, source_target_pairs={{0,64},{64,128},{128,192},{192,0},{1,65},{65,129},{129,193},{193,1... | collective-permute-start | bytes 196616 | tf_op jit(solution)/shard_map/ppermute | solution.py:55
  5.5 5.1 %collective-permute-start.1 = (bf16[32,1024]{1,0:T(8,128)(2,1)S(1)}, bf16[32,1024]{1,0:T(8,128)(2,1)S(1)}, u32[]{:S(2)}, u32[]{:S(2)}) collective-permute-start(bf16[32,1024]{1,0:T(8,128)(2,1)S(1)} %teacher.2), channel_id=1, source_target_pairs={{0,128},{64,192},{128,0},{192,64},{1,129},{65,193},{129,1},{193,65... | collective-permute-start | bytes 196616 | tf_op jit(solution)/shard_map/ppermute | solution.py:55
  10.6 2.4 %collective-permute-start = (bf16[32,1024]{1,0:T(8,128)(2,1)S(1)}, bf16[32,1024]{1,0:T(8,128)(2,1)S(1)}, u32[]{:S(2)}, u32[]{:S(2)}) collective-permute-start(bf16[32,1024]{1,0:T(8,128)(2,1)S(1)} %teacher.2), channel_id=1, source_target_pairs={{0,192},{64,0},{128,64},{192,128},{1,193},{65,1},{129,65},{193,129... | collective-permute-start | bytes 196616 | tf_op jit(solution)/shard_map/ppermute | solution.py:55
  13.0 0.0 copy-start.2
  13.0 1.4 %copy-done.2 = bf16[32,32,768]{2,1,0:T(8,128)(2,1)S(1)} copy-done((bf16[32,32,768]{2,1,0:T(8,128)(2,1)S(1)}, bf16[32,32,768]{2,1,0:T(8,128)(2,1)}, u32[]{:S(2)}) %copy-start.2) | copy-done | bytes 1572888
  14.4 0.0 copy-start.4
  14.4 0.7 copy-done.4
  15.1 0.0 copy-start.6
  15.1 0.7 copy-done.6
  15.7 0.5 norm.1
  16.3 0.0 collective-permute-done.2
  16.3 0.0 collective-permute-done.1
  16.3 2.0 %collective-permute-done = bf16[32,1024]{1,0:T(8,128)(2,1)S(1)} collective-permute-done((bf16[32,1024]{1,0:T(8,128)(2,1)S(1)}, bf16[32,1024]{1,0:T(8,128)(2,1)S(1)}, u32[]{:S(2)}, u32[]{:S(2)}) %collective-permute-start) | collective-permute-done | bytes 65568 | tf_op jit(solution)/shard_map/ppermute | solution.py:55
  18.3 1.3 %collective-permute-start.3 = (bf16[32,896]{1,0:T(8,128)(2,1)S(1)}, bf16[32,896]{1,0:T(8,128)(2,1)S(1)}, u32[]{:S(2)}, u32[]{:S(2)}) collective-permute-start(bf16[32,896]{1,0:T(8,128)(2,1)S(1)} %get-tuple-element.28), channel_id=1, source_target_pairs={{0,4},{4,0},{8,12},{12,8},{1,5},{5,1},{9,13},{13,9},{2,6},{6,2},{1... | collective-permute-start | bytes 172040 | tf_op jit(solution)/shard_map/ppermute | solution.py:59
  19.6 1.3 %collective-permute-start.5 = (bf16[128,1024]{1,0:T(8,128)(2,1)S(1)}, bf16[128,1024]{1,0:T(8,128)(2,1)S(1)}, u32[]{:S(2)}, u32[]{:S(2)}) collective-permute-start(bf16[128,1024]{1,0:T(8,128)(2,1)S(1)} %pad_maximum_fusion.refs_0_), channel_id=1, source_target_pairs={{0,16},{16,32},{32,48},{48,0},{1,17},{17,33},{33,49},{49,1},{2,18}... | collective-permute-start | bytes 786440 | tf_op jit(solution)/shard_map/ppermute | solution.py:55
  20.9 0.5 collective-permute-done.3
  21.4 2.6 %collective-permute-start.4 = (bf16[64,896]{1,0:T(8,128)(2,1)S(1)}, bf16[64,896]{1,0:T(8,128)(2,1)S(1)}, u32[]{:S(2)}, u32[]{:S(2)}) collective-permute-start(bf16[64,896]{1,0:T(8,128)(2,1)S(1)} %pad_maximum_fusion.1), channel_id=1, source_target_pairs={{0,12},{4,8},{8,4},{12,0},{1,13},{5,9},{9,5},{13,1},{2,14},{6,10},... | collective-permute-start | bytes 344072 | tf_op jit(solution)/shard_map/ppermute | solution.py:59
  24.0 2.7 %collective-permute-start.8 = (bf16[128,1024]{1,0:T(8,128)(2,1)S(1)}, bf16[128,1024]{1,0:T(8,128)(2,1)S(1)}, u32[]{:S(2)}, u32[]{:S(2)}) collective-permute-start(bf16[128,1024]{1,0:T(8,128)(2,1)S(1)} %pad_maximum_fusion.refs_0_), channel_id=1, source_target_pairs={{0,48},{16,0},{32,16},{48,32},{1,49},{17,1},{33,17},{49,33},{2,50}... | collective-permute-start | bytes 786440 | tf_op jit(solution)/shard_map/ppermute | solution.py:55
  26.7 1.2 %collective-permute-done.5.refs_1_ = bf16[128,1024]{1,0:T(8,128)(2,1)S(1)} collective-permute-done((bf16[128,1024]{1,0:T(8,128)(2,1)S(1)}, bf16[128,1024]{1,0:T(8,128)(2,1)S(1)}, u32[]{:S(2)}, u32[]{:S(2)}) %collective-permute-start.5) | collective-permute-done | bytes 262176 | tf_op jit(solution)/shard_map/ppermute | solution.py:55
  28.0 0.0 collective-permute-start.6
  28.0 0.0 collective-permute-done.4
  28.0 0.1 collective-permute-start.7
  28.1 2.0 %collective-permute-start.9 = (bf16[128,1024]{1,0:T(8,128)(2,1)S(1)}, bf16[128,1024]{1,0:T(8,128)(2,1)S(1)}, u32[]{:S(2)}, u32[]{:S(2)}) collective-permute-start(bf16[128,1024]{1,0:T(8,128)(2,1)S(1)} %pad_maximum_fusion.refs_0_), channel_id=1, source_target_pairs={{0,1},{1,0},{2,3},{3,2},{4,5},{5,4},{6,7},{7,6},{8,9},{9,8},{10,11... | collective-permute-start | bytes 786440 | tf_op jit(solution)/shard_map/ppermute | solution.py:51
  30.1 0.1 collective-permute-start.10
  30.2 0.2 collective-permute-done.8.refs_2_
  30.4 2.9 %collective-permute-start.11 = (bf16[128,1024]{1,0:T(8,128)(2,1)S(1)}, bf16[128,1024]{1,0:T(8,128)(2,1)S(1)}, u32[]{:S(2)}, u32[]{:S(2)}) collective-permute-start(bf16[128,1024]{1,0:T(8,128)(2,1)S(1)} %collective-permute-done.8.refs_2_), channel_id=1, source_target_pairs={{0,1},{1,0},{2,3},{3,2},{4,5},{5,4},{6,7},{7,6},{8,9},{9,8},{10,11... | collective-permute-start | bytes 786440 | tf_op jit(solution)/shard_map/ppermute | solution.py:51
  33.2 0.0 collective-permute-done.7.rest
  33.3 2.1 %collective-permute-done.6.refs_3_ = bf16[128,1024]{1,0:T(8,128)(2,1)S(1)} collective-permute-done((bf16[128,1024]{1,0:T(8,128)(2,1)S(1)}, bf16[128,1024]{1,0:T(8,128)(2,1)S(1)}, u32[]{:S(2)}, u32[]{:S(2)}) %collective-permute-start.6) | collective-permute-done | bytes 262176 | tf_op jit(solution)/shard_map/ppermute | solution.py:55
  35.4 2.5 %collective-permute-start.12 = (bf16[128,1024]{1,0:T(8,128)(2,1)S(1)}, bf16[128,1024]{1,0:T(8,128)(2,1)S(1)}, u32[]{:S(2)}, u32[]{:S(2)}) collective-permute-start(bf16[128,1024]{1,0:T(8,128)(2,1)S(1)} %collective-permute-done.6.refs_3_), channel_id=1, source_target_pairs={{0,1},{1,0},{2,3},{3,2},{4,5},{5,4},{6,7},{7,6},{8,9},{9,8},{10,11... | collective-permute-start | bytes 786440 | tf_op jit(solution)/shard_map/ppermute | solution.py:51
  37.9 0.0 copy-done.1
  37.9 0.8 student.1
  38.7 0.0 collective-permute-done.9.refs_4_
  38.7 0.0 collective-permute-done.11.refs_6_
  38.7 0.0 collective-permute-done.10.refs_5_
  38.7 0.4 collective-permute-done.12.refs_7_
  39.1 1.6 %scores.1 = (bf16[1024,1024]{1,0:T(8,128)(2,1)S(1)}, bf16[256,1024]{1,0:T(8,128)(2,1)S(1)}, bf16[256,2176]{1,0:T(8,128)(2,1)S(1)}, f32[8,128]{1,0:T(8,128)S(1)}, f32[1,128]{1,0:T(1,128)S(1)}) custom-call(bf16[256,1024]{1,0:T(8,128)(2,1)S(1)} %get-tuple-element.32.student, bf16[256,896]{1,0:T(8,128)(2,1)S(1)} %get-tuple-element.31.rows, ...), custom_call_target="tpu_custom_call" | custom-call | tf_op jit(solution)/shard_map/scores/pallas_call | solution.py:295
  40.7 0.5 collective-permute-start.13
  41.2 0.8 collective-permute-done.13.pair
  42.0 13.8 %all_to_all.20.col_in = f32[16,8,128]{2,1,0:T(8,128)S(1)} all-to-all(f32[16,8,128]{2,1,0:T(8,128)S(1)} %cols.1), channel_id=1, replica_groups=mesh['zh'=4,'y'=4,'x'=4,'zl'=2,'c'=2] {'zh','y'}, dimensions={0} | all-to-all | bytes 131072 | tf_op jit(solution)/shard_map/all_to_all | solution.py:42
  55.8 1.2 %scaled.1 = (bf16[256,2176]{1,0:T(8,128)(2,1)S(1)}, f32[1,128]{1,0:T(1,128)S(1)}) custom-call(bf16[256,896]{1,0:T(8,128)(2,1)S(1)} %get-tuple-element.31.rows, f32[16,8,128]{2,1,0:T(8,128)S(1)} %all_to_all.20.col_in, f32[1,128]{1,0:T(1,128)S(1)} %get-tuple-element.35.pos_part, ...), custom_call_target="tpu_custom_call", output_to_operand_aliasing={{0}: (5, {})} | custom-call | tf_op jit(solution)/shard_map/scaled/pallas_call | solution.py:304
  57.0 0.0 copy-start.5
  57.0 17.9 %all_to_all.21.terms = bf16[8,32,2176]{2,1,0:T(8,128)(2,1)S(1)} all-to-all(bf16[8,32,2176]{2,1,0:T(8,128)(2,1)S(1)} %bitcast.6), channel_id=1, replica_groups=mesh['zh'=4,'y'=4,'x'=4,'zl'=2,'c'=2] {'x','zl'}, dimensions={0} | all-to-all | bytes 2228224 | tf_op jit(solution)/shard_map/all_to_all | solution.py:42
  74.9 0.0 copy-done.5
  74.9 0.9 rows.1
  75.8 8.2 %all_to_all.22.back = bf16[8,48,128]{2,1,0:T(8,128)(2,1)S(1)} all-to-all(bf16[8,48,128]{2,1,0:T(8,128)(2,1)S(1)} %get-tuple-element.45), channel_id=1, replica_groups=mesh['zh'=4,'y'=4,'x'=4,'zl'=2,'c'=2] {'x','zl'}, dimensions={0} | all-to-all | bytes 196608 | tf_op jit(solution)/shard_map/all_to_all | solution.py:42
  84.0 0.3 head.5
  84.3 12.7 %all_to_all.23.back = bf16[16,64,128]{2,1,0:T(8,128)(2,1)S(1)} all-to-all(bf16[16,64,128]{2,1,0:T(8,128)(2,1)S(1)} %head.5), channel_id=1, replica_groups=mesh['zh'=4,'y'=4,'x'=4,'zl'=2,'c'=2] {'zh','y'}, dimensions={0} | all-to-all | bytes 524288 | tf_op jit(solution)/shard_map/all_to_all | solution.py:42
  97.0 0.1 broadcast_in_dim.10._
  97.1 0.0 copy-start
  97.2 5.3 %collective-permute-start.14 = (f32[56,128]{1,0:T(8,128)S(1)}, f32[56,128]{1,0:T(8,128)S(1)}, u32[]{:S(2)}, u32[]{:S(2)}) collective-permute-start(f32[56,128]{1,0:T(8,128)S(1)} %last.1.mine), channel_id=1, source_target_pairs={{0,1},{1,0},{2,3},{3,2},{4,5},{5,4},{6,7},{7,6},{8,9},{9,8},{10,11... | collective-permute-start | bytes 86024 | tf_op jit(solution)/shard_map/ppermute | solution.py:51
  102.5 0.9 collective-permute-done.14.pair
  103.4 0.7 out.1
  104.0 0.0 copy-done
  (7 shorter events, 0.1 us)
Async XLA Ops:
  0.6 0.8 copy-start.3
  1.5 36.4 %copy-start.1 = (bf16[768,1024]{1,0:T(8,128)(2,1)S(1)}, bf16[768,1024]{1,0:T(8,128)(2,1)}, u32[]{:S(2)}) copy-start(bf16[768,1024]{1,0:T(8,128)(2,1)} %head.4) | copy-start | bytes 4718596
  1.6 14.7 %collective-permute-start.2 = (bf16[32,1024]{1,0:T(8,128)(2,1)S(1)}, bf16[32,1024]{1,0:T(8,128)(2,1)S(1)}, u32[]{:S(2)}, u32[]{:S(2)}) collective-permute-start(bf16[32,1024]{1,0:T(8,128)(2,1)S(1)} %teacher.2), channel_id=1, source_target_pairs={{0,64},{64,128},{128,192},{192,0},{1,65},{65,129},{129,193},{193,1... | collective-permute-start | bytes 196616 | tf_op jit(solution)/shard_map/ppermute | solution.py:55
  5.5 10.8 %collective-permute-start.1 = (bf16[32,1024]{1,0:T(8,128)(2,1)S(1)}, bf16[32,1024]{1,0:T(8,128)(2,1)S(1)}, u32[]{:S(2)}, u32[]{:S(2)}) collective-permute-start(bf16[32,1024]{1,0:T(8,128)(2,1)S(1)} %teacher.2), channel_id=1, source_target_pairs={{0,128},{64,192},{128,0},{192,64},{1,129},{65,193},{129,1},{193,65... | collective-permute-start | bytes 196616 | tf_op jit(solution)/shard_map/ppermute | solution.py:55
  10.6 7.7 %collective-permute-start = (bf16[32,1024]{1,0:T(8,128)(2,1)S(1)}, bf16[32,1024]{1,0:T(8,128)(2,1)S(1)}, u32[]{:S(2)}, u32[]{:S(2)}) collective-permute-start(bf16[32,1024]{1,0:T(8,128)(2,1)S(1)} %teacher.2), channel_id=1, source_target_pairs={{0,192},{64,0},{128,64},{192,128},{1,193},{65,1},{129,65},{193,129... | collective-permute-start | bytes 196616 | tf_op jit(solution)/shard_map/ppermute | solution.py:55
  13.0 1.4 %copy-start.2 = (bf16[32,32,768]{2,1,0:T(8,128)(2,1)S(1)}, bf16[32,32,768]{2,1,0:T(8,128)(2,1)}, u32[]{:S(2)}) copy-start(bf16[32,32,768]{2,1,0:T(8,128)(2,1)} %features.1) | copy-start | bytes 4718596
  14.4 0.7 copy-start.4
  15.1 0.7 copy-start.6
  18.3 3.1 %collective-permute-start.3 = (bf16[32,896]{1,0:T(8,128)(2,1)S(1)}, bf16[32,896]{1,0:T(8,128)(2,1)S(1)}, u32[]{:S(2)}, u32[]{:S(2)}) collective-permute-start(bf16[32,896]{1,0:T(8,128)(2,1)S(1)} %get-tuple-element.28), channel_id=1, source_target_pairs={{0,4},{4,0},{8,12},{12,8},{1,5},{5,1},{9,13},{13,9},{2,6},{6,2},{1... | collective-permute-start | bytes 172040 | tf_op jit(solution)/shard_map/ppermute | solution.py:59
  19.6 8.4 %collective-permute-start.5 = (bf16[128,1024]{1,0:T(8,128)(2,1)S(1)}, bf16[128,1024]{1,0:T(8,128)(2,1)S(1)}, u32[]{:S(2)}, u32[]{:S(2)}) collective-permute-start(bf16[128,1024]{1,0:T(8,128)(2,1)S(1)} %pad_maximum_fusion.refs_0_), channel_id=1, source_target_pairs={{0,16},{16,32},{32,48},{48,0},{1,17},{17,33},{33,49},{49,1},{2,18}... | collective-permute-start | bytes 786440 | tf_op jit(solution)/shard_map/ppermute | solution.py:55
  21.4 6.6 %collective-permute-start.4 = (bf16[64,896]{1,0:T(8,128)(2,1)S(1)}, bf16[64,896]{1,0:T(8,128)(2,1)S(1)}, u32[]{:S(2)}, u32[]{:S(2)}) collective-permute-start(bf16[64,896]{1,0:T(8,128)(2,1)S(1)} %pad_maximum_fusion.1), channel_id=1, source_target_pairs={{0,12},{4,8},{8,4},{12,0},{1,13},{5,9},{9,5},{13,1},{2,14},{6,10},... | collective-permute-start | bytes 344072 | tf_op jit(solution)/shard_map/ppermute | solution.py:59
  24.0 6.4 %collective-permute-start.8 = (bf16[128,1024]{1,0:T(8,128)(2,1)S(1)}, bf16[128,1024]{1,0:T(8,128)(2,1)S(1)}, u32[]{:S(2)}, u32[]{:S(2)}) collective-permute-start(bf16[128,1024]{1,0:T(8,128)(2,1)S(1)} %pad_maximum_fusion.refs_0_), channel_id=1, source_target_pairs={{0,48},{16,0},{32,16},{48,32},{1,49},{17,1},{33,17},{49,33},{2,50}... | collective-permute-start | bytes 786440 | tf_op jit(solution)/shard_map/ppermute | solution.py:55
  28.0 7.4 %collective-permute-start.6 = (bf16[128,1024]{1,0:T(8,128)(2,1)S(1)}, bf16[128,1024]{1,0:T(8,128)(2,1)S(1)}, u32[]{:S(2)}, u32[]{:S(2)}) collective-permute-start(bf16[128,1024]{1,0:T(8,128)(2,1)S(1)} %collective-permute-done.5.refs_1_), channel_id=1, source_target_pairs={{0,16},{16,32},{32,48},{48,0},{1,17},{17,33},{33,49},{49,1},{2,18}... | collective-permute-start | bytes 786440 | tf_op jit(solution)/shard_map/ppermute | solution.py:55
  28.0 5.3 %collective-permute-start.7 = (bf16[128,896]{1,0:T(8,128)(2,1)S(1)}, bf16[128,896]{1,0:T(8,128)(2,1)S(1)}, u32[]{:S(2)}, u32[]{:S(2)}) collective-permute-start(bf16[128,896]{1,0:T(8,128)(2,1)S(1)} %constant_dynamic-update-slice_fusion.four), channel_id=1, source_target_pairs={{0,2},{2,0},{1,3},{3,1},{4,6},{6,4},{5,7},{7,5},{8,10},{10,8},{9,1... | collective-permute-start | bytes 688136 | tf_op jit(solution)/shard_map/ppermute | solution.py:51
  28.1 10.6 %collective-permute-start.9 = (bf16[128,1024]{1,0:T(8,128)(2,1)S(1)}, bf16[128,1024]{1,0:T(8,128)(2,1)S(1)}, u32[]{:S(2)}, u32[]{:S(2)}) collective-permute-start(bf16[128,1024]{1,0:T(8,128)(2,1)S(1)} %pad_maximum_fusion.refs_0_), channel_id=1, source_target_pairs={{0,1},{1,0},{2,3},{3,2},{4,5},{5,4},{6,7},{7,6},{8,9},{9,8},{10,11... | collective-permute-start | bytes 786440 | tf_op jit(solution)/shard_map/ppermute | solution.py:51
  30.1 8.6 %collective-permute-start.10 = (bf16[128,1024]{1,0:T(8,128)(2,1)S(1)}, bf16[128,1024]{1,0:T(8,128)(2,1)S(1)}, u32[]{:S(2)}, u32[]{:S(2)}) collective-permute-start(bf16[128,1024]{1,0:T(8,128)(2,1)S(1)} %collective-permute-done.5.refs_1_), channel_id=1, source_target_pairs={{0,1},{1,0},{2,3},{3,2},{4,5},{5,4},{6,7},{7,6},{8,9},{9,8},{10,11... | collective-permute-start | bytes 786440 | tf_op jit(solution)/shard_map/ppermute | solution.py:51
  30.4 8.3 %collective-permute-start.11 = (bf16[128,1024]{1,0:T(8,128)(2,1)S(1)}, bf16[128,1024]{1,0:T(8,128)(2,1)S(1)}, u32[]{:S(2)}, u32[]{:S(2)}) collective-permute-start(bf16[128,1024]{1,0:T(8,128)(2,1)S(1)} %collective-permute-done.8.refs_2_), channel_id=1, source_target_pairs={{0,1},{1,0},{2,3},{3,2},{4,5},{5,4},{6,7},{7,6},{8,9},{9,8},{10,11... | collective-permute-start | bytes 786440 | tf_op jit(solution)/shard_map/ppermute | solution.py:51
  35.4 3.7 %collective-permute-start.12 = (bf16[128,1024]{1,0:T(8,128)(2,1)S(1)}, bf16[128,1024]{1,0:T(8,128)(2,1)S(1)}, u32[]{:S(2)}, u32[]{:S(2)}) collective-permute-start(bf16[128,1024]{1,0:T(8,128)(2,1)S(1)} %collective-permute-done.6.refs_3_), channel_id=1, source_target_pairs={{0,1},{1,0},{2,3},{3,2},{4,5},{5,4},{6,7},{7,6},{8,9},{9,8},{10,11... | collective-permute-start | bytes 786440 | tf_op jit(solution)/shard_map/ppermute | solution.py:51
  40.7 1.3 %collective-permute-start.13 = (f32[8,128]{1,0:T(8,128)S(1)}, f32[8,128]{1,0:T(8,128)S(1)}, u32[]{:S(2)}, u32[]{:S(2)}) collective-permute-start(f32[8,128]{1,0:T(8,128)S(1)} %get-tuple-element.34.mine), channel_id=1, source_target_pairs={{0,1},{1,0},{2,3},{3,2},{4,5},{5,4},{6,7},{7,6},{8,9},{9,8},{10,11... | collective-permute-start | bytes 12296 | tf_op jit(solution)/shard_map/ppermute | solution.py:51
  57.0 17.9 %copy-start.5 = (f32[768]{0:T(1024)S(1)}, f32[768]{0:T(1024)}, u32[]{:S(2)}) copy-start(f32[768]{0:T(1024)} %param.7) | copy-start | bytes 9220
  97.1 6.9 %copy-start = (bf16[32,32,768]{2,1,0:T(8,128)(2,1)}, bf16[32,32,768]{2,1,0:T(8,128)(2,1)S(1)}, u32[]{:S(2)}) copy-start(bf16[32,32,768]{2,1,0:T(8,128)(2,1)S(1)} %broadcast_in_dim.10._) | copy-start | bytes 4718596
  97.2 6.2 %collective-permute-start.14 = (f32[56,128]{1,0:T(8,128)S(1)}, f32[56,128]{1,0:T(8,128)S(1)}, u32[]{:S(2)}, u32[]{:S(2)}) collective-permute-start(f32[56,128]{1,0:T(8,128)S(1)} %last.1.mine), channel_id=1, source_target_pairs={{0,1},{1,0},{2,3},{3,2},{4,5},{5,4},{6,7},{7,6},{8,9},{9,8},{10,11... | collective-permute-start | bytes 86024 | tf_op jit(solution)/shard_map/ppermute | solution.py:51

commit v9 on v8

--- a/solution.py
+++ b/solution.py
@@ -257,7 +257,7 @@
 def body(features, teacher, gain, w_head, positives):
     wide = 2 * HALF
 
-    mine = call(teacher_kernel, shaped(OWN, E, dtype=b16), "V", "teacher")(teacher)
+    mine = call(teacher_kernel, shaped(OWN, E, dtype=b16), "V", "teacher", limit=56 << 20)(teacher)
     mine = jnp.concatenate([mine] + [along(mine, "zh", k) for k in (3, 2, 1)], axis=0)
 
     gain = gain.reshape(D // 128, 128)

time: 104 us -> 105 us (level)
  Pallas kernels: 6.17 us -> 7.7 us
    pallas_call x1, Pallas kernels: 0.11 us -> 1.7 us  [body(): call(teacher_kernel, shaped(OWN, E, dtype=b16), 'V', 'teacher', limit=56...]
  transfers between devices with their start and end apart: 15 -> 15, of which waited for: 8 -> 9; matrix products, arithmetic and copies ran while one was open for 0% -> 0% of each run, Pallas kernels for 1% -> 1%
where the time goes in v9:
time: 105 us
  blocking collectives  52.6 us (50%)
  starting transfers between devices  32.5 us (31%)
  waiting for transfers between devices  8.36 us (8%)
  Pallas kernels  7.7 us (7%)
  local copies, waits for them, and re-layouts  2.91 us (3%)
    all_to_all x4, blocking collectives, swap(): return lax.all_to_all(blocks, axes, 0, 0, tiled=True)  52.6 us
    ppermute x6, starting transfers between devices, along(): return lax.ppermute(block, axis, [(i, (i + step) % 4) for i in range(4)])  15.3 us
    ppermute x7, starting transfers between devices, other(): return lax.ppermute(block, axis, [(0, 1), (1, 0)])  13.3 us
    ppermute x6, waiting for transfers between devices, along(): return lax.ppermute(block, axis, [(i, (i + step) % 4) for i in range(4)])  5.72 us
    ppermute x2, starting transfers between devices, across(): return lax.ppermute(block, 'x', [(i, i ^ flip) for i in range(4)])  3.86 us
    unnamed x16, local copies, waits for them, and re-layouts  2.79 us
    ppermute x7, waiting for transfers between devices, other(): return lax.ppermute(block, axis, [(0, 1), (1, 0)])  2.12 us
  transfers between devices with their start and end apart: 15, of which 9 were waited for; matrix products, arithmetic and copies ran while one was open for 0% of the time, Pallas kernels for 1%

profile of v9, /device:TPU:1, one launch (start us, length us, event | category | flops | bytes accessed | tf_op | source)
XLA Modules:
  0.0 104.9 jit_solution(7100780537202351478)
XLA Ops:
  0.6 0.0 copy-start.1
  0.6 1.7 %teacher.2 = bf16[32,1024]{1,0:T(8,128)(2,1)} custom-call(bf16[32,1024]{1,0:T(8,128)(2,1)} %teacher.3), custom_call_target="tpu_custom_call" | custom-call | tf_op jit(solution)/shard_map/teacher/pallas_call | solution.py:260
  2.3 3.8 %collective-permute-start.2 = (bf16[32,1024]{1,0:T(8,128)(2,1)}, bf16[32,1024]{1,0:T(8,128)(2,1)S(1)}, u32[]{:S(2)}, u32[]{:S(2)}) collective-permute-start(bf16[32,1024]{1,0:T(8,128)(2,1)} %teacher.2), channel_id=1, source_target_pairs={{0,64},{64,128},{128,192},{192,0},{1,65},{65,129},{129,193},{193,1... | collective-permute-start | bytes 196616 | tf_op jit(solution)/shard_map/ppermute | solution.py:55
  6.2 5.1 %collective-permute-start.1 = (bf16[32,1024]{1,0:T(8,128)(2,1)}, bf16[32,1024]{1,0:T(8,128)(2,1)S(1)}, u32[]{:S(2)}, u32[]{:S(2)}) collective-permute-start(bf16[32,1024]{1,0:T(8,128)(2,1)} %teacher.2), channel_id=1, source_target_pairs={{0,128},{64,192},{128,0},{192,64},{1,129},{65,193},{129,1},{193,65... | collective-permute-start | bytes 196616 | tf_op jit(solution)/shard_map/ppermute | solution.py:55
  11.3 2.4 %collective-permute-start = (bf16[32,1024]{1,0:T(8,128)(2,1)}, bf16[32,1024]{1,0:T(8,128)(2,1)S(1)}, u32[]{:S(2)}, u32[]{:S(2)}) collective-permute-start(bf16[32,1024]{1,0:T(8,128)(2,1)} %teacher.2), channel_id=1, source_target_pairs={{0,192},{64,0},{128,64},{192,128},{1,193},{65,1},{129,65},{193,129... | collective-permute-start | bytes 196616 | tf_op jit(solution)/shard_map/ppermute | solution.py:55
  13.7 0.0 copy-start.2
  13.7 1.4 %copy-done.2 = bf16[32,32,768]{2,1,0:T(8,128)(2,1)S(1)} copy-done((bf16[32,32,768]{2,1,0:T(8,128)(2,1)S(1)}, bf16[32,32,768]{2,1,0:T(8,128)(2,1)}, u32[]{:S(2)}) %copy-start.2) | copy-done | bytes 1572888
  15.1 0.0 copy-start.3
  15.1 0.7 copy-done.3
  15.7 0.0 copy-start.5
  15.8 0.7 copy-done.5
  16.4 0.0 copy-start.6
  16.4 0.5 norm.1
  17.0 0.0 collective-permute-done.2
  17.0 0.0 collective-permute-done.1
  17.0 2.2 %collective-permute-done = bf16[32,1024]{1,0:T(8,128)(2,1)S(1)} collective-permute-done((bf16[32,1024]{1,0:T(8,128)(2,1)}, bf16[32,1024]{1,0:T(8,128)(2,1)S(1)}, u32[]{:S(2)}, u32[]{:S(2)}) %collective-permute-start) | collective-permute-done | bytes 65568 | tf_op jit(solution)/shard_map/ppermute | solution.py:55
  19.1 0.0 copy-done.6
  19.2 1.3 %collective-permute-start.3 = (bf16[32,896]{1,0:T(8,128)(2,1)S(1)}, bf16[32,896]{1,0:T(8,128)(2,1)S(1)}, u32[]{:S(2)}, u32[]{:S(2)}) collective-permute-start(bf16[32,896]{1,0:T(8,128)(2,1)S(1)} %get-tuple-element.28), channel_id=1, source_target_pairs={{0,4},{4,0},{8,12},{12,8},{1,5},{5,1},{9,13},{13,9},{2,6},{6,2},{1... | collective-permute-start | bytes 172040 | tf_op jit(solution)/shard_map/ppermute | solution.py:59
  20.5 1.3 %collective-permute-start.5 = (bf16[128,1024]{1,0:T(8,128)(2,1)S(1)}, bf16[128,1024]{1,0:T(8,128)(2,1)S(1)}, u32[]{:S(2)}, u32[]{:S(2)}) collective-permute-start(bf16[128,1024]{1,0:T(8,128)(2,1)S(1)} %pad_maximum_fusion.refs_0_), channel_id=1, source_target_pairs={{0,16},{16,32},{32,48},{48,0},{1,17},{17,33},{33,49},{49,1},{2,18}... | collective-permute-start | bytes 786440 | tf_op jit(solution)/shard_map/ppermute | solution.py:55
  21.8 0.5 collective-permute-done.3
  22.3 2.6 %collective-permute-start.4 = (bf16[64,896]{1,0:T(8,128)(2,1)S(1)}, bf16[64,896]{1,0:T(8,128)(2,1)S(1)}, u32[]{:S(2)}, u32[]{:S(2)}) collective-permute-start(bf16[64,896]{1,0:T(8,128)(2,1)S(1)} %pad_maximum_fusion.1), channel_id=1, source_target_pairs={{0,12},{4,8},{8,4},{12,0},{1,13},{5,9},{9,5},{13,1},{2,14},{6,10},... | collective-permute-start | bytes 344072 | tf_op jit(solution)/shard_map/ppermute | solution.py:59
  24.9 2.7 %collective-permute-start.8 = (bf16[128,1024]{1,0:T(8,128)(2,1)S(1)}, bf16[128,1024]{1,0:T(8,128)(2,1)S(1)}, u32[]{:S(2)}, u32[]{:S(2)}) collective-permute-start(bf16[128,1024]{1,0:T(8,128)(2,1)S(1)} %pad_maximum_fusion.refs_0_), channel_id=1, source_target_pairs={{0,48},{16,0},{32,16},{48,32},{1,49},{17,1},{33,17},{49,33},{2,50}... | collective-permute-start | bytes 786440 | tf_op jit(solution)/shard_map/ppermute | solution.py:55
  27.6 1.3 %collective-permute-done.5.refs_1_ = bf16[128,1024]{1,0:T(8,128)(2,1)S(1)} collective-permute-done((bf16[128,1024]{1,0:T(8,128)(2,1)S(1)}, bf16[128,1024]{1,0:T(8,128)(2,1)S(1)}, u32[]{:S(2)}, u32[]{:S(2)}) %collective-permute-start.5) | collective-permute-done | bytes 262176 | tf_op jit(solution)/shard_map/ppermute | solution.py:55
  28.9 0.0 collective-permute-start.6
  28.9 0.0 collective-permute-done.4
  28.9 0.1 collective-permute-start.7
  29.0 2.0 %collective-permute-start.9 = (bf16[128,1024]{1,0:T(8,128)(2,1)S(1)}, bf16[128,1024]{1,0:T(8,128)(2,1)S(1)}, u32[]{:S(2)}, u32[]{:S(2)}) collective-permute-start(bf16[128,1024]{1,0:T(8,128)(2,1)S(1)} %pad_maximum_fusion.refs_0_), channel_id=1, source_target_pairs={{0,1},{1,0},{2,3},{3,2},{4,5},{5,4},{6,7},{7,6},{8,9},{9,8},{10,11... | collective-permute-start | bytes 786440 | tf_op jit(solution)/shard_map/ppermute | solution.py:51
  31.0 0.1 collective-permute-start.10
  31.1 0.2 collective-permute-done.8.refs_2_
  31.3 2.8 %collective-permute-start.11 = (bf16[128,1024]{1,0:T(8,128)(2,1)S(1)}, bf16[128,1024]{1,0:T(8,128)(2,1)S(1)}, u32[]{:S(2)}, u32[]{:S(2)}) collective-permute-start(bf16[128,1024]{1,0:T(8,128)(2,1)S(1)} %collective-permute-done.8.refs_2_), channel_id=1, source_target_pairs={{0,1},{1,0},{2,3},{3,2},{4,5},{5,4},{6,7},{7,6},{8,9},{9,8},{10,11... | collective-permute-start | bytes 786440 | tf_op jit(solution)/shard_map/ppermute | solution.py:51
  34.1 0.1 collective-permute-done.7.rest
  34.2 2.1 %collective-permute-done.6.refs_3_ = bf16[128,1024]{1,0:T(8,128)(2,1)S(1)} collective-permute-done((bf16[128,1024]{1,0:T(8,128)(2,1)S(1)}, bf16[128,1024]{1,0:T(8,128)(2,1)S(1)}, u32[]{:S(2)}, u32[]{:S(2)}) %collective-permute-start.6) | collective-permute-done | bytes 262176 | tf_op jit(solution)/shard_map/ppermute | solution.py:55
  36.3 2.5 %collective-permute-start.12 = (bf16[128,1024]{1,0:T(8,128)(2,1)S(1)}, bf16[128,1024]{1,0:T(8,128)(2,1)S(1)}, u32[]{:S(2)}, u32[]{:S(2)}) collective-permute-start(bf16[128,1024]{1,0:T(8,128)(2,1)S(1)} %collective-permute-done.6.refs_3_), channel_id=1, source_target_pairs={{0,1},{1,0},{2,3},{3,2},{4,5},{5,4},{6,7},{7,6},{8,9},{9,8},{10,11... | collective-permute-start | bytes 786440 | tf_op jit(solution)/shard_map/ppermute | solution.py:51
  38.8 0.0 copy-done.1
  38.8 0.7 student.1
  39.6 0.0 collective-permute-done.9.refs_4_
  39.6 0.0 collective-permute-done.11.refs_6_
  39.6 0.0 collective-permute-done.10.refs_5_
  39.6 0.4 collective-permute-done.12.refs_7_
  40.0 1.6 %scores.1 = (bf16[1024,1024]{1,0:T(8,128)(2,1)S(1)}, bf16[256,1024]{1,0:T(8,128)(2,1)S(1)}, bf16[256,2176]{1,0:T(8,128)(2,1)S(1)}, f32[8,128]{1,0:T(8,128)S(1)}, f32[1,128]{1,0:T(1,128)S(1)}) custom-call(bf16[256,1024]{1,0:T(8,128)(2,1)S(1)} %get-tuple-element.32.student, bf16[256,896]{1,0:T(8,128)(2,1)S(1)} %get-tuple-element.31.rows, ...), custom_call_target="tpu_custom_call" | custom-call | tf_op jit(solution)/shard_map/scores/pallas_call | solution.py:295
  41.6 0.5 collective-permute-start.13
  42.0 0.8 collective-permute-done.13.pair
  42.9 13.8 %all_to_all.20.col_in = f32[16,8,128]{2,1,0:T(8,128)S(1)} all-to-all(f32[16,8,128]{2,1,0:T(8,128)S(1)} %cols.1), channel_id=1, replica_groups=mesh['zh'=4,'y'=4,'x'=4,'zl'=2,'c'=2] {'zh','y'}, dimensions={0} | all-to-all | bytes 131072 | tf_op jit(solution)/shard_map/all_to_all | solution.py:42
  56.6 1.2 %scaled.1 = (bf16[256,2176]{1,0:T(8,128)(2,1)S(1)}, f32[1,128]{1,0:T(1,128)S(1)}) custom-call(bf16[256,896]{1,0:T(8,128)(2,1)S(1)} %get-tuple-element.31.rows, f32[16,8,128]{2,1,0:T(8,128)S(1)} %all_to_all.20.col_in, f32[1,128]{1,0:T(1,128)S(1)} %get-tuple-element.35.pos_part, ...), custom_call_target="tpu_custom_call", output_to_operand_aliasing={{0}: (5, {})} | custom-call | tf_op jit(solution)/shard_map/scaled/pallas_call | solution.py:304
  57.8 0.0 copy-start.4
  57.8 18.0 %all_to_all.21.terms = bf16[8,32,2176]{2,1,0:T(8,128)(2,1)S(1)} all-to-all(bf16[8,32,2176]{2,1,0:T(8,128)(2,1)S(1)} %bitcast.6), channel_id=1, replica_groups=mesh['zh'=4,'y'=4,'x'=4,'zl'=2,'c'=2] {'x','zl'}, dimensions={0} | all-to-all | bytes 2228224 | tf_op jit(solution)/shard_map/all_to_all | solution.py:42
  75.8 0.0 copy-done.4
  75.8 0.9 rows.1
  76.7 8.1 %all_to_all.22.back = bf16[8,48,128]{2,1,0:T(8,128)(2,1)S(1)} all-to-all(bf16[8,48,128]{2,1,0:T(8,128)(2,1)S(1)} %get-tuple-element.45), channel_id=1, replica_groups=mesh['zh'=4,'y'=4,'x'=4,'zl'=2,'c'=2] {'x','zl'}, dimensions={0} | all-to-all | bytes 196608 | tf_op jit(solution)/shard_map/all_to_all | solution.py:42
  84.8 0.3 head.5
  85.1 12.7 %all_to_all.23.back = bf16[16,64,128]{2,1,0:T(8,128)(2,1)S(1)} all-to-all(bf16[16,64,128]{2,1,0:T(8,128)(2,1)S(1)} %head.5), channel_id=1, replica_groups=mesh['zh'=4,'y'=4,'x'=4,'zl'=2,'c'=2] {'zh','y'}, dimensions={0} | all-to-all | bytes 524288 | tf_op jit(solution)/shard_map/all_to_all | solution.py:42
  97.9 0.1 broadcast_in_dim.10._
  98.0 0.0 copy-start
  98.0 5.3 %collective-permute-start.14 = (f32[56,128]{1,0:T(8,128)S(1)}, f32[56,128]{1,0:T(8,128)S(1)}, u32[]{:S(2)}, u32[]{:S(2)}) collective-permute-start(f32[56,128]{1,0:T(8,128)S(1)} %last.1.mine), channel_id=1, source_target_pairs={{0,1},{1,0},{2,3},{3,2},{4,5},{5,4},{6,7},{7,6},{8,9},{9,8},{10,11... | collective-permute-start | bytes 86024 | tf_op jit(solution)/shard_map/ppermute | solution.py:51
  103.4 0.9 collective-permute-done.14.pair
  104.2 0.7 out.1
  104.9 0.0 copy-done
  (7 shorter events, 0.1 us)
Async XLA Ops:
  0.6 38.2 %copy-start.1 = (bf16[768,1024]{1,0:T(8,128)(2,1)S(1)}, bf16[768,1024]{1,0:T(8,128)(2,1)}, u32[]{:S(2)}) copy-start(bf16[768,1024]{1,0:T(8,128)(2,1)} %head.4) | copy-start | bytes 4718596
  2.3 14.6 %collective-permute-start.2 = (bf16[32,1024]{1,0:T(8,128)(2,1)}, bf16[32,1024]{1,0:T(8,128)(2,1)S(1)}, u32[]{:S(2)}, u32[]{:S(2)}) collective-permute-start(bf16[32,1024]{1,0:T(8,128)(2,1)} %teacher.2), channel_id=1, source_target_pairs={{0,64},{64,128},{128,192},{192,0},{1,65},{65,129},{129,193},{193,1... | collective-permute-start | bytes 196616 | tf_op jit(solution)/shard_map/ppermute | solution.py:55
  6.2 10.8 %collective-permute-start.1 = (bf16[32,1024]{1,0:T(8,128)(2,1)}, bf16[32,1024]{1,0:T(8,128)(2,1)S(1)}, u32[]{:S(2)}, u32[]{:S(2)}) collective-permute-start(bf16[32,1024]{1,0:T(8,128)(2,1)} %teacher.2), channel_id=1, source_target_pairs={{0,128},{64,192},{128,0},{192,64},{1,129},{65,193},{129,1},{193,65... | collective-permute-start | bytes 196616 | tf_op jit(solution)/shard_map/ppermute | solution.py:55
  11.3 7.9 %collective-permute-start = (bf16[32,1024]{1,0:T(8,128)(2,1)}, bf16[32,1024]{1,0:T(8,128)(2,1)S(1)}, u32[]{:S(2)}, u32[]{:S(2)}) collective-permute-start(bf16[32,1024]{1,0:T(8,128)(2,1)} %teacher.2), channel_id=1, source_target_pairs={{0,192},{64,0},{128,64},{192,128},{1,193},{65,1},{129,65},{193,129... | collective-permute-start | bytes 196616 | tf_op jit(solution)/shard_map/ppermute | solution.py:55
  13.7 1.4 %copy-start.2 = (bf16[32,32,768]{2,1,0:T(8,128)(2,1)S(1)}, bf16[32,32,768]{2,1,0:T(8,128)(2,1)}, u32[]{:S(2)}) copy-start(bf16[32,32,768]{2,1,0:T(8,128)(2,1)} %features.1) | copy-start | bytes 4718596
  15.1 0.7 copy-start.3
  15.7 0.7 copy-start.5
  16.4 2.7 %copy-start.6 = (bf16[32,1024]{1,0:T(8,128)(2,1)S(1)}, bf16[32,1024]{1,0:T(8,128)(2,1)}, u32[]{:S(2)}) copy-start(bf16[32,1024]{1,0:T(8,128)(2,1)} %teacher.2) | copy-start | bytes 196612
  19.2 3.1 %collective-permute-start.3 = (bf16[32,896]{1,0:T(8,128)(2,1)S(1)}, bf16[32,896]{1,0:T(8,128)(2,1)S(1)}, u32[]{:S(2)}, u32[]{:S(2)}) collective-permute-start(bf16[32,896]{1,0:T(8,128)(2,1)S(1)} %get-tuple-element.28), channel_id=1, source_target_pairs={{0,4},{4,0},{8,12},{12,8},{1,5},{5,1},{9,13},{13,9},{2,6},{6,2},{1... | collective-permute-start | bytes 172040 | tf_op jit(solution)/shard_map/ppermute | solution.py:59
  20.5 8.4 %collective-permute-start.5 = (bf16[128,1024]{1,0:T(8,128)(2,1)S(1)}, bf16[128,1024]{1,0:T(8,128)(2,1)S(1)}, u32[]{:S(2)}, u32[]{:S(2)}) collective-permute-start(bf16[128,1024]{1,0:T(8,128)(2,1)S(1)} %pad_maximum_fusion.refs_0_), channel_id=1, source_target_pairs={{0,16},{16,32},{32,48},{48,0},{1,17},{17,33},{33,49},{49,1},{2,18}... | collective-permute-start | bytes 786440 | tf_op jit(solution)/shard_map/ppermute | solution.py:55
  22.3 6.6 %collective-permute-start.4 = (bf16[64,896]{1,0:T(8,128)(2,1)S(1)}, bf16[64,896]{1,0:T(8,128)(2,1)S(1)}, u32[]{:S(2)}, u32[]{:S(2)}) collective-permute-start(bf16[64,896]{1,0:T(8,128)(2,1)S(1)} %pad_maximum_fusion.1), channel_id=1, source_target_pairs={{0,12},{4,8},{8,4},{12,0},{1,13},{5,9},{9,5},{13,1},{2,14},{6,10},... | collective-permute-start | bytes 344072 | tf_op jit(solution)/shard_map/ppermute | solution.py:59
  24.9 6.4 %collective-permute-start.8 = (bf16[128,1024]{1,0:T(8,128)(2,1)S(1)}, bf16[128,1024]{1,0:T(8,128)(2,1)S(1)}, u32[]{:S(2)}, u32[]{:S(2)}) collective-permute-start(bf16[128,1024]{1,0:T(8,128)(2,1)S(1)} %pad_maximum_fusion.refs_0_), channel_id=1, source_target_pairs={{0,48},{16,0},{32,16},{48,32},{1,49},{17,1},{33,17},{49,33},{2,50}... | collective-permute-start | bytes 786440 | tf_op jit(solution)/shard_map/ppermute | solution.py:55
  28.9 7.4 %collective-permute-start.6 = (bf16[128,1024]{1,0:T(8,128)(2,1)S(1)}, bf16[128,1024]{1,0:T(8,128)(2,1)S(1)}, u32[]{:S(2)}, u32[]{:S(2)}) collective-permute-start(bf16[128,1024]{1,0:T(8,128)(2,1)S(1)} %collective-permute-done.5.refs_1_), channel_id=1, source_target_pairs={{0,16},{16,32},{32,48},{48,0},{1,17},{17,33},{33,49},{49,1},{2,18}... | collective-permute-start | bytes 786440 | tf_op jit(solution)/shard_map/ppermute | solution.py:55
  28.9 5.3 %collective-permute-start.7 = (bf16[128,896]{1,0:T(8,128)(2,1)S(1)}, bf16[128,896]{1,0:T(8,128)(2,1)S(1)}, u32[]{:S(2)}, u32[]{:S(2)}) collective-permute-start(bf16[128,896]{1,0:T(8,128)(2,1)S(1)} %constant_dynamic-update-slice_fusion.four), channel_id=1, source_target_pairs={{0,2},{2,0},{1,3},{3,1},{4,6},{6,4},{5,7},{7,5},{8,10},{10,8},{9,1... | collective-permute-start | bytes 688136 | tf_op jit(solution)/shard_map/ppermute | solution.py:51
  29.0 10.6 %collective-permute-start.9 = (bf16[128,1024]{1,0:T(8,128)(2,1)S(1)}, bf16[128,1024]{1,0:T(8,128)(2,1)S(1)}, u32[]{:S(2)}, u32[]{:S(2)}) collective-permute-start(bf16[128,1024]{1,0:T(8,128)(2,1)S(1)} %pad_maximum_fusion.refs_0_), channel_id=1, source_target_pairs={{0,1},{1,0},{2,3},{3,2},{4,5},{5,4},{6,7},{7,6},{8,9},{9,8},{10,11... | collective-permute-start | bytes 786440 | tf_op jit(solution)/shard_map/ppermute | solution.py:51
  31.0 8.6 %collective-permute-start.10 = (bf16[128,1024]{1,0:T(8,128)(2,1)S(1)}, bf16[128,1024]{1,0:T(8,128)(2,1)S(1)}, u32[]{:S(2)}, u32[]{:S(2)}) collective-permute-start(bf16[128,1024]{1,0:T(8,128)(2,1)S(1)} %collective-permute-done.5.refs_1_), channel_id=1, source_target_pairs={{0,1},{1,0},{2,3},{3,2},{4,5},{5,4},{6,7},{7,6},{8,9},{9,8},{10,11... | collective-permute-start | bytes 786440 | tf_op jit(solution)/shard_map/ppermute | solution.py:51
  31.3 8.3 %collective-permute-start.11 = (bf16[128,1024]{1,0:T(8,128)(2,1)S(1)}, bf16[128,1024]{1,0:T(8,128)(2,1)S(1)}, u32[]{:S(2)}, u32[]{:S(2)}) collective-permute-start(bf16[128,1024]{1,0:T(8,128)(2,1)S(1)} %collective-permute-done.8.refs_2_), channel_id=1, source_target_pairs={{0,1},{1,0},{2,3},{3,2},{4,5},{5,4},{6,7},{7,6},{8,9},{9,8},{10,11... | collective-permute-start | bytes 786440 | tf_op jit(solution)/shard_map/ppermute | solution.py:51
  36.3 3.7 %collective-permute-start.12 = (bf16[128,1024]{1,0:T(8,128)(2,1)S(1)}, bf16[128,1024]{1,0:T(8,128)(2,1)S(1)}, u32[]{:S(2)}, u32[]{:S(2)}) collective-permute-start(bf16[128,1024]{1,0:T(8,128)(2,1)S(1)} %collective-permute-done.6.refs_3_), channel_id=1, source_target_pairs={{0,1},{1,0},{2,3},{3,2},{4,5},{5,4},{6,7},{7,6},{8,9},{9,8},{10,11... | collective-permute-start | bytes 786440 | tf_op jit(solution)/shard_map/ppermute | solution.py:51
  41.6 1.3 %collective-permute-start.13 = (f32[8,128]{1,0:T(8,128)S(1)}, f32[8,128]{1,0:T(8,128)S(1)}, u32[]{:S(2)}, u32[]{:S(2)}) collective-permute-start(f32[8,128]{1,0:T(8,128)S(1)} %get-tuple-element.34.mine), channel_id=1, source_target_pairs={{0,1},{1,0},{2,3},{3,2},{4,5},{5,4},{6,7},{7,6},{8,9},{9,8},{10,11... | collective-permute-start | bytes 12296 | tf_op jit(solution)/shard_map/ppermute | solution.py:51
  57.8 18.0 %copy-start.4 = (f32[768]{0:T(1024)S(1)}, f32[768]{0:T(1024)}, u32[]{:S(2)}) copy-start(f32[768]{0:T(1024)} %param.7) | copy-start | bytes 9220
  98.0 6.9 %copy-start = (bf16[32,32,768]{2,1,0:T(8,128)(2,1)}, bf16[32,32,768]{2,1,0:T(8,128)(2,1)S(1)}, u32[]{:S(2)}) copy-start(bf16[32,32,768]{2,1,0:T(8,128)(2,1)S(1)} %broadcast_in_dim.10._) | copy-start | bytes 4718596
  98.0 6.2 %collective-permute-start.14 = (f32[56,128]{1,0:T(8,128)S(1)}, f32[56,128]{1,0:T(8,128)S(1)}, u32[]{:S(2)}, u32[]{:S(2)}) collective-permute-start(f32[56,128]{1,0:T(8,128)S(1)} %last.1.mine), channel_id=1, source_target_pairs={{0,1},{1,0},{2,3},{3,2},{4,5},{5,4},{6,7},{7,6},{8,9},{9,8},{10,11... | collective-permute-start | bytes 86024 | tf_op jit(solution)/shard_map/ppermute | solution.py:51

commit v10 on v8

--- a/solution.py
+++ b/solution.py
@@ -17,7 +17,7 @@
 SIDE = NROW * OWN
 HALF = NCHIP * OWN
 MARK = 128
-CHUNK = 128
+CHUNK = 256
 BLOCK = 4 * OWN
 f32, b16 = jnp.float32, jnp.bfloat16
 SPACES = {

time: 104 us -> 104 us (level)
  no operation moved by 1% of the time
where the time goes in v10:
time: 104 us
  blocking collectives  52.6 us (51%)
  starting transfers between devices  32.7 us (31%)
  waiting for transfers between devices  8.08 us (8%)
  Pallas kernels  6.1 us (6%)
  local copies, waits for them, and re-layouts  3.74 us (4%)
    all_to_all x4, blocking collectives, swap(): return lax.all_to_all(blocks, axes, 0, 0, tiled=True)  52.6 us
    ppermute x6, starting transfers between devices, along(): return lax.ppermute(block, axis, [(i, (i + step) % 4) for i in range(4)])  15.4 us
    ppermute x7, starting transfers between devices, other(): return lax.ppermute(block, axis, [(0, 1), (1, 0)])  13.4 us
    ppermute x6, waiting for transfers between devices, along(): return lax.ppermute(block, axis, [(i, (i + step) % 4) for i in range(4)])  5.48 us
    ppermute x2, starting transfers between devices, across(): return lax.ppermute(block, 'x', [(i, i ^ flip) for i in range(4)])  3.86 us
    unnamed x16, local copies, waits for them, and re-layouts  3.61 us
  transfers between devices with their start and end apart: 15, of which 8 were waited for; matrix products, arithmetic and copies ran while one was open for 0% of the time, Pallas kernels for 1%

profile of v10, /device:TPU:1, one launch (start us, length us, event | category | flops | bytes accessed | tf_op | source)
XLA Modules:
  0.0 104.0 jit_solution(17366205197701958654)
XLA Ops:
  0.6 0.0 copy-start.3
  0.6 0.8 copy-done.3
  1.5 0.0 copy-start.1
  1.5 0.1 teacher.2
  1.6 3.9 %collective-permute-start.2 = (bf16[32,1024]{1,0:T(8,128)(2,1)S(1)}, bf16[32,1024]{1,0:T(8,128)(2,1)S(1)}, u32[]{:S(2)}, u32[]{:S(2)}) collective-permute-start(bf16[32,1024]{1,0:T(8,128)(2,1)S(1)} %teacher.2), channel_id=1, source_target_pairs={{0,64},{64,128},{128,192},{192,0},{1,65},{65,129},{129,193},{193,1... | collective-permute-start | bytes 196616 | tf_op jit(solution)/shard_map/ppermute | solution.py:55
  5.5 5.1 %collective-permute-start.1 = (bf16[32,1024]{1,0:T(8,128)(2,1)S(1)}, bf16[32,1024]{1,0:T(8,128)(2,1)S(1)}, u32[]{:S(2)}, u32[]{:S(2)}) collective-permute-start(bf16[32,1024]{1,0:T(8,128)(2,1)S(1)} %teacher.2), channel_id=1, source_target_pairs={{0,128},{64,192},{128,0},{192,64},{1,129},{65,193},{129,1},{193,65... | collective-permute-start | bytes 196616 | tf_op jit(solution)/shard_map/ppermute | solution.py:55
  10.6 2.4 %collective-permute-start = (bf16[32,1024]{1,0:T(8,128)(2,1)S(1)}, bf16[32,1024]{1,0:T(8,128)(2,1)S(1)}, u32[]{:S(2)}, u32[]{:S(2)}) collective-permute-start(bf16[32,1024]{1,0:T(8,128)(2,1)S(1)} %teacher.2), channel_id=1, source_target_pairs={{0,192},{64,0},{128,64},{192,128},{1,193},{65,1},{129,65},{193,129... | collective-permute-start | bytes 196616 | tf_op jit(solution)/shard_map/ppermute | solution.py:55
  13.0 0.0 copy-start.2
  13.0 1.4 %copy-done.2 = bf16[32,32,768]{2,1,0:T(8,128)(2,1)S(1)} copy-done((bf16[32,32,768]{2,1,0:T(8,128)(2,1)S(1)}, bf16[32,32,768]{2,1,0:T(8,128)(2,1)}, u32[]{:S(2)}) %copy-start.2) | copy-done | bytes 1572888
  14.4 0.0 copy-start.4
  14.4 0.7 copy-done.4
  15.1 0.0 copy-start.6
  15.1 0.7 copy-done.6
  15.7 0.5 norm.1
  16.3 0.0 collective-permute-done.2
  16.3 0.0 collective-permute-done.1
  16.3 2.0 %collective-permute-done = bf16[32,1024]{1,0:T(8,128)(2,1)S(1)} collective-permute-done((bf16[32,1024]{1,0:T(8,128)(2,1)S(1)}, bf16[32,1024]{1,0:T(8,128)(2,1)S(1)}, u32[]{:S(2)}, u32[]{:S(2)}) %collective-permute-start) | collective-permute-done | bytes 65568 | tf_op jit(solution)/shard_map/ppermute | solution.py:55
  18.3 1.3 %collective-permute-start.3 = (bf16[32,896]{1,0:T(8,128)(2,1)S(1)}, bf16[32,896]{1,0:T(8,128)(2,1)S(1)}, u32[]{:S(2)}, u32[]{:S(2)}) collective-permute-start(bf16[32,896]{1,0:T(8,128)(2,1)S(1)} %get-tuple-element.28), channel_id=1, source_target_pairs={{0,4},{4,0},{8,12},{12,8},{1,5},{5,1},{9,13},{13,9},{2,6},{6,2},{1... | collective-permute-start | bytes 172040 | tf_op jit(solution)/shard_map/ppermute | solution.py:59
  19.6 1.3 %collective-permute-start.5 = (bf16[128,1024]{1,0:T(8,128)(2,1)S(1)}, bf16[128,1024]{1,0:T(8,128)(2,1)S(1)}, u32[]{:S(2)}, u32[]{:S(2)}) collective-permute-start(bf16[128,1024]{1,0:T(8,128)(2,1)S(1)} %pad_maximum_fusion.refs_0_), channel_id=1, source_target_pairs={{0,16},{16,32},{32,48},{48,0},{1,17},{17,33},{33,49},{49,1},{2,18}... | collective-permute-start | bytes 786440 | tf_op jit(solution)/shard_map/ppermute | solution.py:55
  20.9 0.5 collective-permute-done.3
  21.4 2.6 %collective-permute-start.4 = (bf16[64,896]{1,0:T(8,128)(2,1)S(1)}, bf16[64,896]{1,0:T(8,128)(2,1)S(1)}, u32[]{:S(2)}, u32[]{:S(2)}) collective-permute-start(bf16[64,896]{1,0:T(8,128)(2,1)S(1)} %pad_maximum_fusion.1), channel_id=1, source_target_pairs={{0,12},{4,8},{8,4},{12,0},{1,13},{5,9},{9,5},{13,1},{2,14},{6,10},... | collective-permute-start | bytes 344072 | tf_op jit(solution)/shard_map/ppermute | solution.py:59
  24.0 2.7 %collective-permute-start.8 = (bf16[128,1024]{1,0:T(8,128)(2,1)S(1)}, bf16[128,1024]{1,0:T(8,128)(2,1)S(1)}, u32[]{:S(2)}, u32[]{:S(2)}) collective-permute-start(bf16[128,1024]{1,0:T(8,128)(2,1)S(1)} %pad_maximum_fusion.refs_0_), channel_id=1, source_target_pairs={{0,48},{16,0},{32,16},{48,32},{1,49},{17,1},{33,17},{49,33},{2,50}... | collective-permute-start | bytes 786440 | tf_op jit(solution)/shard_map/ppermute | solution.py:55
  26.7 1.2 %collective-permute-done.5.refs_1_ = bf16[128,1024]{1,0:T(8,128)(2,1)S(1)} collective-permute-done((bf16[128,1024]{1,0:T(8,128)(2,1)S(1)}, bf16[128,1024]{1,0:T(8,128)(2,1)S(1)}, u32[]{:S(2)}, u32[]{:S(2)}) %collective-permute-start.5) | collective-permute-done | bytes 262176 | tf_op jit(solution)/shard_map/ppermute | solution.py:55
  28.0 0.0 collective-permute-start.6
  28.0 0.0 collective-permute-done.4
  28.0 0.1 collective-permute-start.7
  28.1 2.0 %collective-permute-start.9 = (bf16[128,1024]{1,0:T(8,128)(2,1)S(1)}, bf16[128,1024]{1,0:T(8,128)(2,1)S(1)}, u32[]{:S(2)}, u32[]{:S(2)}) collective-permute-start(bf16[128,1024]{1,0:T(8,128)(2,1)S(1)} %pad_maximum_fusion.refs_0_), channel_id=1, source_target_pairs={{0,1},{1,0},{2,3},{3,2},{4,5},{5,4},{6,7},{7,6},{8,9},{9,8},{10,11... | collective-permute-start | bytes 786440 | tf_op jit(solution)/shard_map/ppermute | solution.py:51
  30.1 0.1 collective-permute-start.10
  30.2 0.2 collective-permute-done.8.refs_2_
  30.4 2.9 %collective-permute-start.11 = (bf16[128,1024]{1,0:T(8,128)(2,1)S(1)}, bf16[128,1024]{1,0:T(8,128)(2,1)S(1)}, u32[]{:S(2)}, u32[]{:S(2)}) collective-permute-start(bf16[128,1024]{1,0:T(8,128)(2,1)S(1)} %collective-permute-done.8.refs_2_), channel_id=1, source_target_pairs={{0,1},{1,0},{2,3},{3,2},{4,5},{5,4},{6,7},{7,6},{8,9},{9,8},{10,11... | collective-permute-start | bytes 786440 | tf_op jit(solution)/shard_map/ppermute | solution.py:51
  33.2 0.0 collective-permute-done.7.rest
  33.3 2.1 %collective-permute-done.6.refs_3_ = bf16[128,1024]{1,0:T(8,128)(2,1)S(1)} collective-permute-done((bf16[128,1024]{1,0:T(8,128)(2,1)S(1)}, bf16[128,1024]{1,0:T(8,128)(2,1)S(1)}, u32[]{:S(2)}, u32[]{:S(2)}) %collective-permute-start.6) | collective-permute-done | bytes 262176 | tf_op jit(solution)/shard_map/ppermute | solution.py:55
  35.4 2.5 %collective-permute-start.12 = (bf16[128,1024]{1,0:T(8,128)(2,1)S(1)}, bf16[128,1024]{1,0:T(8,128)(2,1)S(1)}, u32[]{:S(2)}, u32[]{:S(2)}) collective-permute-start(bf16[128,1024]{1,0:T(8,128)(2,1)S(1)} %collective-permute-done.6.refs_3_), channel_id=1, source_target_pairs={{0,1},{1,0},{2,3},{3,2},{4,5},{5,4},{6,7},{7,6},{8,9},{9,8},{10,11... | collective-permute-start | bytes 786440 | tf_op jit(solution)/shard_map/ppermute | solution.py:51
  37.9 0.0 copy-done.1
  37.9 0.8 student.1
  38.7 0.0 collective-permute-done.9.refs_4_
  38.7 0.0 collective-permute-done.11.refs_6_
  38.7 0.0 collective-permute-done.10.refs_5_
  38.7 0.4 collective-permute-done.12.refs_7_
  39.1 1.6 %scores.1 = (bf16[1024,1024]{1,0:T(8,128)(2,1)S(1)}, bf16[256,1024]{1,0:T(8,128)(2,1)S(1)}, bf16[256,2176]{1,0:T(8,128)(2,1)S(1)}, f32[8,128]{1,0:T(8,128)S(1)}, f32[1,128]{1,0:T(1,128)S(1)}) custom-call(bf16[256,1024]{1,0:T(8,128)(2,1)S(1)} %get-tuple-element.32.student, bf16[256,896]{1,0:T(8,128)(2,1)S(1)} %get-tuple-element.31.rows, ...), custom_call_target="tpu_custom_call" | custom-call | tf_op jit(solution)/shard_map/scores/pallas_call | solution.py:295
  40.6 0.5 collective-permute-start.13
  41.1 0.8 collective-permute-done.13.pair
  41.9 13.8 %all_to_all.20.col_in = f32[16,8,128]{2,1,0:T(8,128)S(1)} all-to-all(f32[16,8,128]{2,1,0:T(8,128)S(1)} %cols.1), channel_id=1, replica_groups=mesh['zh'=4,'y'=4,'x'=4,'zl'=2,'c'=2] {'zh','y'}, dimensions={0} | all-to-all | bytes 131072 | tf_op jit(solution)/shard_map/all_to_all | solution.py:42
  55.7 1.2 %scaled.1 = (bf16[256,2176]{1,0:T(8,128)(2,1)S(1)}, f32[1,128]{1,0:T(1,128)S(1)}) custom-call(bf16[256,896]{1,0:T(8,128)(2,1)S(1)} %get-tuple-element.31.rows, f32[16,8,128]{2,1,0:T(8,128)S(1)} %all_to_all.20.col_in, f32[1,128]{1,0:T(1,128)S(1)} %get-tuple-element.35.pos_part, ...), custom_call_target="tpu_custom_call", output_to_operand_aliasing={{0}: (5, {})} | custom-call | tf_op jit(solution)/shard_map/scaled/pallas_call | solution.py:304
  56.9 0.0 copy-start.5
  56.9 17.9 %all_to_all.21.terms = bf16[8,32,2176]{2,1,0:T(8,128)(2,1)S(1)} all-to-all(bf16[8,32,2176]{2,1,0:T(8,128)(2,1)S(1)} %bitcast.6), channel_id=1, replica_groups=mesh['zh'=4,'y'=4,'x'=4,'zl'=2,'c'=2] {'x','zl'}, dimensions={0} | all-to-all | bytes 2228224 | tf_op jit(solution)/shard_map/all_to_all | solution.py:42
  74.9 0.0 copy-done.5
  74.9 0.9 rows.1
  75.8 8.2 %all_to_all.22.back = bf16[8,48,128]{2,1,0:T(8,128)(2,1)S(1)} all-to-all(bf16[8,48,128]{2,1,0:T(8,128)(2,1)S(1)} %get-tuple-element.45), channel_id=1, replica_groups=mesh['zh'=4,'y'=4,'x'=4,'zl'=2,'c'=2] {'x','zl'}, dimensions={0} | all-to-all | bytes 196608 | tf_op jit(solution)/shard_map/all_to_all | solution.py:42
  83.9 0.3 head.5
  84.2 12.7 %all_to_all.23.back = bf16[16,64,128]{2,1,0:T(8,128)(2,1)S(1)} all-to-all(bf16[16,64,128]{2,1,0:T(8,128)(2,1)S(1)} %head.5), channel_id=1, replica_groups=mesh['zh'=4,'y'=4,'x'=4,'zl'=2,'c'=2] {'zh','y'}, dimensions={0} | all-to-all | bytes 524288 | tf_op jit(solution)/shard_map/all_to_all | solution.py:42
  96.9 0.1 broadcast_in_dim.10._
  97.1 0.0 copy-start
  97.1 5.3 %collective-permute-start.14 = (f32[56,128]{1,0:T(8,128)S(1)}, f32[56,128]{1,0:T(8,128)S(1)}, u32[]{:S(2)}, u32[]{:S(2)}) collective-permute-start(f32[56,128]{1,0:T(8,128)S(1)} %last.1.mine), channel_id=1, source_target_pairs={{0,1},{1,0},{2,3},{3,2},{4,5},{5,4},{6,7},{7,6},{8,9},{9,8},{10,11... | collective-permute-start | bytes 86024 | tf_op jit(solution)/shard_map/ppermute | solution.py:51
  102.5 0.9 collective-permute-done.14.pair
  103.3 0.7 out.1
  104.0 0.0 copy-done
  (7 shorter events, 0.1 us)
Async XLA Ops:
  0.6 0.8 copy-start.3
  1.5 36.4 %copy-start.1 = (bf16[768,1024]{1,0:T(8,128)(2,1)S(1)}, bf16[768,1024]{1,0:T(8,128)(2,1)}, u32[]{:S(2)}) copy-start(bf16[768,1024]{1,0:T(8,128)(2,1)} %head.4) | copy-start | bytes 4718596
  1.6 14.7 %collective-permute-start.2 = (bf16[32,1024]{1,0:T(8,128)(2,1)S(1)}, bf16[32,1024]{1,0:T(8,128)(2,1)S(1)}, u32[]{:S(2)}, u32[]{:S(2)}) collective-permute-start(bf16[32,1024]{1,0:T(8,128)(2,1)S(1)} %teacher.2), channel_id=1, source_target_pairs={{0,64},{64,128},{128,192},{192,0},{1,65},{65,129},{129,193},{193,1... | collective-permute-start | bytes 196616 | tf_op jit(solution)/shard_map/ppermute | solution.py:55
  5.5 10.8 %collective-permute-start.1 = (bf16[32,1024]{1,0:T(8,128)(2,1)S(1)}, bf16[32,1024]{1,0:T(8,128)(2,1)S(1)}, u32[]{:S(2)}, u32[]{:S(2)}) collective-permute-start(bf16[32,1024]{1,0:T(8,128)(2,1)S(1)} %teacher.2), channel_id=1, source_target_pairs={{0,128},{64,192},{128,0},{192,64},{1,129},{65,193},{129,1},{193,65... | collective-permute-start | bytes 196616 | tf_op jit(solution)/shard_map/ppermute | solution.py:55
  10.6 7.7 %collective-permute-start = (bf16[32,1024]{1,0:T(8,128)(2,1)S(1)}, bf16[32,1024]{1,0:T(8,128)(2,1)S(1)}, u32[]{:S(2)}, u32[]{:S(2)}) collective-permute-start(bf16[32,1024]{1,0:T(8,128)(2,1)S(1)} %teacher.2), channel_id=1, source_target_pairs={{0,192},{64,0},{128,64},{192,128},{1,193},{65,1},{129,65},{193,129... | collective-permute-start | bytes 196616 | tf_op jit(solution)/shard_map/ppermute | solution.py:55
  13.0 1.4 %copy-start.2 = (bf16[32,32,768]{2,1,0:T(8,128)(2,1)S(1)}, bf16[32,32,768]{2,1,0:T(8,128)(2,1)}, u32[]{:S(2)}) copy-start(bf16[32,32,768]{2,1,0:T(8,128)(2,1)} %features.1) | copy-start | bytes 4718596
  14.4 0.7 copy-start.4
  15.1 0.7 copy-start.6
  18.3 3.1 %collective-permute-start.3 = (bf16[32,896]{1,0:T(8,128)(2,1)S(1)}, bf16[32,896]{1,0:T(8,128)(2,1)S(1)}, u32[]{:S(2)}, u32[]{:S(2)}) collective-permute-start(bf16[32,896]{1,0:T(8,128)(2,1)S(1)} %get-tuple-element.28), channel_id=1, source_target_pairs={{0,4},{4,0},{8,12},{12,8},{1,5},{5,1},{9,13},{13,9},{2,6},{6,2},{1... | collective-permute-start | bytes 172040 | tf_op jit(solution)/shard_map/ppermute | solution.py:59
  19.6 8.4 %collective-permute-start.5 = (bf16[128,1024]{1,0:T(8,128)(2,1)S(1)}, bf16[128,1024]{1,0:T(8,128)(2,1)S(1)}, u32[]{:S(2)}, u32[]{:S(2)}) collective-permute-start(bf16[128,1024]{1,0:T(8,128)(2,1)S(1)} %pad_maximum_fusion.refs_0_), channel_id=1, source_target_pairs={{0,16},{16,32},{32,48},{48,0},{1,17},{17,33},{33,49},{49,1},{2,18}... | collective-permute-start | bytes 786440 | tf_op jit(solution)/shard_map/ppermute | solution.py:55
  21.4 6.6 %collective-permute-start.4 = (bf16[64,896]{1,0:T(8,128)(2,1)S(1)}, bf16[64,896]{1,0:T(8,128)(2,1)S(1)}, u32[]{:S(2)}, u32[]{:S(2)}) collective-permute-start(bf16[64,896]{1,0:T(8,128)(2,1)S(1)} %pad_maximum_fusion.1), channel_id=1, source_target_pairs={{0,12},{4,8},{8,4},{12,0},{1,13},{5,9},{9,5},{13,1},{2,14},{6,10},... | collective-permute-start | bytes 344072 | tf_op jit(solution)/shard_map/ppermute | solution.py:59
  24.0 6.4 %collective-permute-start.8 = (bf16[128,1024]{1,0:T(8,128)(2,1)S(1)}, bf16[128,1024]{1,0:T(8,128)(2,1)S(1)}, u32[]{:S(2)}, u32[]{:S(2)}) collective-permute-start(bf16[128,1024]{1,0:T(8,128)(2,1)S(1)} %pad_maximum_fusion.refs_0_), channel_id=1, source_target_pairs={{0,48},{16,0},{32,16},{48,32},{1,49},{17,1},{33,17},{49,33},{2,50}... | collective-permute-start | bytes 786440 | tf_op jit(solution)/shard_map/ppermute | solution.py:55
  28.0 7.4 %collective-permute-start.6 = (bf16[128,1024]{1,0:T(8,128)(2,1)S(1)}, bf16[128,1024]{1,0:T(8,128)(2,1)S(1)}, u32[]{:S(2)}, u32[]{:S(2)}) collective-permute-start(bf16[128,1024]{1,0:T(8,128)(2,1)S(1)} %collective-permute-done.5.refs_1_), channel_id=1, source_target_pairs={{0,16},{16,32},{32,48},{48,0},{1,17},{17,33},{33,49},{49,1},{2,18}... | collective-permute-start | bytes 786440 | tf_op jit(solution)/shard_map/ppermute | solution.py:55
  28.0 5.3 %collective-permute-start.7 = (bf16[128,896]{1,0:T(8,128)(2,1)S(1)}, bf16[128,896]{1,0:T(8,128)(2,1)S(1)}, u32[]{:S(2)}, u32[]{:S(2)}) collective-permute-start(bf16[128,896]{1,0:T(8,128)(2,1)S(1)} %constant_dynamic-update-slice_fusion.four), channel_id=1, source_target_pairs={{0,2},{2,0},{1,3},{3,1},{4,6},{6,4},{5,7},{7,5},{8,10},{10,8},{9,1... | collective-permute-start | bytes 688136 | tf_op jit(solution)/shard_map/ppermute | solution.py:51
  28.1 10.6 %collective-permute-start.9 = (bf16[128,1024]{1,0:T(8,128)(2,1)S(1)}, bf16[128,1024]{1,0:T(8,128)(2,1)S(1)}, u32[]{:S(2)}, u32[]{:S(2)}) collective-permute-start(bf16[128,1024]{1,0:T(8,128)(2,1)S(1)} %pad_maximum_fusion.refs_0_), channel_id=1, source_target_pairs={{0,1},{1,0},{2,3},{3,2},{4,5},{5,4},{6,7},{7,6},{8,9},{9,8},{10,11... | collective-permute-start | bytes 786440 | tf_op jit(solution)/shard_map/ppermute | solution.py:51
  30.1 8.6 %collective-permute-start.10 = (bf16[128,1024]{1,0:T(8,128)(2,1)S(1)}, bf16[128,1024]{1,0:T(8,128)(2,1)S(1)}, u32[]{:S(2)}, u32[]{:S(2)}) collective-permute-start(bf16[128,1024]{1,0:T(8,128)(2,1)S(1)} %collective-permute-done.5.refs_1_), channel_id=1, source_target_pairs={{0,1},{1,0},{2,3},{3,2},{4,5},{5,4},{6,7},{7,6},{8,9},{9,8},{10,11... | collective-permute-start | bytes 786440 | tf_op jit(solution)/shard_map/ppermute | solution.py:51
  30.4 8.3 %collective-permute-start.11 = (bf16[128,1024]{1,0:T(8,128)(2,1)S(1)}, bf16[128,1024]{1,0:T(8,128)(2,1)S(1)}, u32[]{:S(2)}, u32[]{:S(2)}) collective-permute-start(bf16[128,1024]{1,0:T(8,128)(2,1)S(1)} %collective-permute-done.8.refs_2_), channel_id=1, source_target_pairs={{0,1},{1,0},{2,3},{3,2},{4,5},{5,4},{6,7},{7,6},{8,9},{9,8},{10,11... | collective-permute-start | bytes 786440 | tf_op jit(solution)/shard_map/ppermute | solution.py:51
  35.4 3.7 %collective-permute-start.12 = (bf16[128,1024]{1,0:T(8,128)(2,1)S(1)}, bf16[128,1024]{1,0:T(8,128)(2,1)S(1)}, u32[]{:S(2)}, u32[]{:S(2)}) collective-permute-start(bf16[128,1024]{1,0:T(8,128)(2,1)S(1)} %collective-permute-done.6.refs_3_), channel_id=1, source_target_pairs={{0,1},{1,0},{2,3},{3,2},{4,5},{5,4},{6,7},{7,6},{8,9},{9,8},{10,11... | collective-permute-start | bytes 786440 | tf_op jit(solution)/shard_map/ppermute | solution.py:51
  40.6 1.3 %collective-permute-start.13 = (f32[8,128]{1,0:T(8,128)S(1)}, f32[8,128]{1,0:T(8,128)S(1)}, u32[]{:S(2)}, u32[]{:S(2)}) collective-permute-start(f32[8,128]{1,0:T(8,128)S(1)} %get-tuple-element.34.mine), channel_id=1, source_target_pairs={{0,1},{1,0},{2,3},{3,2},{4,5},{5,4},{6,7},{7,6},{8,9},{9,8},{10,11... | collective-permute-start | bytes 12296 | tf_op jit(solution)/shard_map/ppermute | solution.py:51
  56.9 18.0 %copy-start.5 = (f32[768]{0:T(1024)S(1)}, f32[768]{0:T(1024)}, u32[]{:S(2)}) copy-start(f32[768]{0:T(1024)} %param.7) | copy-start | bytes 9220
  97.1 6.9 %copy-start = (bf16[32,32,768]{2,1,0:T(8,128)(2,1)}, bf16[32,32,768]{2,1,0:T(8,128)(2,1)S(1)}, u32[]{:S(2)}) copy-start(bf16[32,32,768]{2,1,0:T(8,128)(2,1)S(1)} %broadcast_in_dim.10._) | copy-start | bytes 4718596
  97.1 6.2 %collective-permute-start.14 = (f32[56,128]{1,0:T(8,128)S(1)}, f32[56,128]{1,0:T(8,128)S(1)}, u32[]{:S(2)}, u32[]{:S(2)}) collective-permute-start(f32[56,128]{1,0:T(8,128)S(1)} %last.1.mine), channel_id=1, source_target_pairs={{0,1},{1,0},{2,3},{3,2},{4,5},{5,4},{6,7},{7,6},{8,9},{9,8},{10,11... | collective-permute-start | bytes 86024 | tf_op jit(solution)/shard_map/ppermute | solution.py:51
